TPU v7x, 128 devices: a whole 4x4x4 slice. The times are simulated.
128 devices in a mesh: dp: 4 (over x_lo, core), space: 32 (over z, x_hi, y).
Axes of the slice: x: 4 (x_hi: 2, x_lo: 2; x = x_hi * 2 + x_lo), y: 4, z: 4, core: 2. Of those that a mesh axis runs over, the one named last changes fastest.
Arguments:
- volumes: bfloat16 [64, 8, 64, 512], P('space', 'dp'), may hold values from -6 to 6
- cotangent: bfloat16 [32, 8, 256, 128], P('space', 'dp'), may hold values from -0.119628906 to 0.119628906
- conv4_weight: bfloat16 [27, 128, 64], replicated, may hold values from -0.15625 to 0.15625
- conv5_weight: bfloat16 [27, 256, 128], replicated, may hold values from -0.109375 to 0.109375
Outputs:
- output5: bfloat16 [32, 8, 256, 128], P('space', 'dp')
- weight4: float32 [27, 128, 64], replicated
- weight5: float32 [27, 256, 128], P(None, None, 'space')
All inputs are finite; a program needn't handle non-finite values.
Results may differ from a plain program's by a relative error of at most 0.0064.
Values may be sent and summed in bfloat16 or wider, within the bound.
No kernel may reach another device: no remote copies, remote signals or barrier semaphores. Data moves between devices by JAX's collectives and lax.ppermute only.
A program may use at most 128 MiB of HBM per device.

v0:
```python
import jax
import jax.numpy as jnp
from jax import lax
from jax.sharding import PartitionSpec as P

HEIGHT = 32
WIDTH = 16


def padded_2(cells, sides, width):
    for axis, dim in sides:
        count = lax.axis_size(axis)
        ends = count - 1
        head = lax.slice_in_dim(cells, 0, width, axis=dim)
        tail = lax.slice_in_dim(cells, cells.shape[dim] - width, cells.shape[dim], axis=dim)
        cells = jnp.concatenate(
            [
                lax.ppermute(tail, axis, [(i, (i + 1) % count) for i in range(ends)]),
                cells,
                lax.ppermute(head, axis, [((i + 1) % count, i) for i in range(ends)]),
            ],
            axis=dim,
        )
    return cells


def plane_shift(values, b, e, row_len):
    length = values.shape[-1]
    margins = [(0, 0)] * (values.ndim - 1) + [(row_len + 1, row_len + 1)]
    padded = jnp.pad(values, margins)
    offset = row_len + 1 + b * row_len + e
    shifted = lax.slice_in_dim(padded, offset, offset + length, axis=values.ndim - 1)
    column = jnp.arange(length) % row_len
    keep_mask = ((column + e >= 0) & (column + e < row_len)).astype(values.dtype)
    return shifted * keep_mask


def plane_stack(values, row_len):
    return jnp.concatenate(
        [plane_shift(values, b, e, row_len) for b in (-1, 0, 1) for e in (-1, 0, 1)], axis=2
    )


def arrange(weight):
    outer, inner = (weight.shape[1], weight.shape[2])
    return weight.reshape(3, 9, outer, inner).transpose(0, 2, 1, 3).reshape(3, outer, 9 * inner)


def unarrange(grad, inner):
    outer = grad.shape[1]
    return grad.reshape(3, outer, 9, inner).transpose(0, 2, 1, 3).reshape(27, outer, inner)


def flipped(weight):
    return weight[::-1].transpose(0, 2, 1)


def convolve(stacked, arranged):
    planes = stacked.shape[0] - 2
    summed = jnp.einsum(
        "fk,dvkp->dvfp", arranged[0], stacked[0:planes], preferred_element_type=jnp.float32
    )
    for a in range(1, 3):
        summed = summed + jnp.einsum(
            "fk,dvkp->dvfp",
            arranged[a],
            stacked[a : a + planes],
            preferred_element_type=jnp.float32,
        )
    return summed


def weight_grad(grad, stacked, inner):
    planes = grad.shape[0]
    pieces = [
        jnp.einsum(
            "dvfp,dvkp->fk", grad, stacked[a : a + planes], preferred_element_type=jnp.float32
        )
        for a in range(3)
    ]
    return unarrange(jnp.stack(pieces), inner)


def silu_slope(values):
    sig = jax.nn.sigmoid(values)
    return sig * (1.0 + values * (1.0 - sig))


def pool_blocks(values):
    planes, vols, chans = (values.shape[0], values.shape[1], values.shape[2])
    blocks = values.reshape(planes // 2, 2, vols, chans, HEIGHT // 2, 2, WIDTH // 2, 2)
    return (blocks.sum(axis=(1, 5, 7)) * 0.125).reshape(planes // 2, vols, chans, -1)


def unpool_blocks(values):
    planes, vols, chans = (values.shape[0], values.shape[1], values.shape[2])
    fine = values.astype(jnp.float32).reshape(planes, 1, vols, chans, HEIGHT // 2, 1, WIDTH // 2, 1)
    fine = jnp.broadcast_to(fine, (planes, 2, vols, chans, HEIGHT // 2, 2, WIDTH // 2, 2))
    return fine.reshape(2 * planes, vols, chans, -1) / 8.0


def per_device(volumes, cotangent, conv4_weight, conv5_weight):
    row_len5 = WIDTH // 2
    padded4 = padded_2(volumes, (("space", 0),), 1)
    stacked4 = plane_stack(padded4, WIDTH)
    preact4 = convolve(stacked4, arrange(conv4_weight))
    inputs5 = pool_blocks(jax.nn.silu(preact4)).astype(jnp.bfloat16)
    owned = conv5_weight.shape[2] // lax.axis_size("space")
    narrow = lax.all_to_all(inputs5, "space", split_axis=2, concat_axis=0, tiled=True)
    own_weight = lax.dynamic_slice_in_dim(conv5_weight, lax.axis_index("space") * owned, owned, 2)
    stacked5 = jnp.pad(plane_stack(narrow, row_len5), ((1, 1), (0, 0), (0, 0), (0, 0)))
    arranged5 = arrange(own_weight)
    window = stacked5
    preact5 = lax.psum_scatter(
        convolve(window, arranged5), "space", scatter_dimension=0, tiled=True
    )
    output5 = jax.nn.silu(preact5).astype(jnp.bfloat16)
    grad_pre5 = (cotangent.astype(jnp.float32) * silu_slope(preact5)).astype(jnp.bfloat16)
    back_weight = arrange(flipped(own_weight))
    planes5 = narrow.shape[0]
    block_rows = lax.all_gather(grad_pre5, "space", axis=0, tiled=True)
    first_row = jnp.int32(0)
    inward = jnp.zeros((planes5 + 2,) + narrow.shape[1:], jnp.float32)
    row_count = block_rows.shape[0]
    spread = plane_stack(block_rows, row_len5)
    for a in range(3):
        target = first_row + 2 - a
        contribution = jnp.einsum(
            "ck,jvkp->jvcp", back_weight[a], spread, preferred_element_type=jnp.float32
        )
        current = lax.dynamic_slice_in_dim(inward, target, row_count, 0)
        inward = lax.dynamic_update_slice_in_dim(inward, current + contribution, target, 0)
    window = stacked5
    pieces = [
        jnp.einsum(
            "jvfp,jvkp->fk",
            block_rows,
            window[a : a + row_count],
            preferred_element_type=jnp.float32,
        )
        for a in range(3)
    ]
    inward, weight_acc = (inward, jnp.stack(pieces))
    local_grad = inward[1 : planes5 + 1].astype(jnp.bfloat16)
    grad_in5 = lax.all_to_all(local_grad, "space", split_axis=0, concat_axis=2, tiled=True)
    weight5 = unarrange(weight_acc, owned)
    weight5 = lax.psum(weight5, "dp")
    grad_pre4 = (unpool_blocks(grad_in5) * silu_slope(preact4)).astype(jnp.bfloat16)
    weight4 = lax.psum(weight_grad(grad_pre4, stacked4, conv4_weight.shape[2]), ("dp", "space"))
    return (output5, weight4, weight5)


def solution(mesh):
    placed = (P("space", "dp", None, None), P("space", "dp", None, None), P(), P())
    return jax.shard_map(
        per_device,
        mesh=mesh,
        in_specs=placed,
        out_specs=(P("space", "dp", None, None), P(), P(None, None, "space")),
        check_vma=False,
    )
```

profile of v0, /device:TPU:1, one launch (start us, length us, event | category | flops | bytes accessed | tf_op | source)
XLA Modules:
  0.0 648.4 jit_solution(4506861109478360730)
XLA Ops:
  10.3 5.3 collective-permute-start
  30.0 14.2 %all-to-all-start = ((bf16[1,2,128,128]{3,1,0,2:T(2,128)(2,1)}), bf16[1,2,128,128]{3,1,0,2:T(2,128)(2,1)S(1)}, u32[]{:S(2)}, u32[]{:S(2)}) async-start(bf16[1,2,128,128]{3,1,0,2:T(2,128)(2,1)} %copy.36), calls=%async_computation | async-start | bytes 131072 | tf_op jit(solution)/shard_map/all_to_all | solution.py:109
  44.5 8.6 %all-to-all-done = bf16[1,2,128,128]{3,1,0,2:T(2,128)(2,1)S(1)} async-done(((bf16[1,2,128,128]{3,1,0,2:T(2,128)(2,1)}), bf16[1,2,128,128]{3,1,0,2:T(2,128)(2,1)S(1)}, u32[]{:S(2)}, u32[]{:S(2)}) %all-to-all-start) | async-done | bytes 65568 | tf_op jit(solution)/shard_map/all_to_all | solution.py:109
  54.3 4.8 concatenate.16
  62.5 4.6 add_bitcast_fusion
  68.9 175.0 %reduce-scatter.2.cloned.1.call-done = f32[1,2,256,128]{2,3,1,0:T(8,128)} async-done(((f32[32,2,256,128]{2,3,1,0:T(8,128)}), f32[1,2,256,128]{2,3,1,0:T(8,128)}) %reduce-scatter.2.cloned.1.call-update) | async-done | bytes 262160 | tf_op jit(solution)/shard_map/reduce_scatter | solution.py:114
  251.3 94.8 %all-gather.2.cloned.1.call-done = bf16[32,2,256,128]{3,2,1,0:T(8,128)(2,1)} async-done(((bf16[1,2,256,128]{3,2,1,0:T(8,128)(2,1)}), bf16[32,2,256,128]{3,2,1,0:T(8,128)(2,1)}) %all-gather.2.cloned.1.call-update) | async-done | bytes 4194320 | tf_op jit(solution)/shard_map/all_gather | solution.py:121
  346.1 3.5 convolution_bitcast_fusion.3
  349.6 3.5 convolution_bitcast_fusion.5
  356.7 6.0 fusion.1
  362.7 3.6 fusion.3
  366.3 3.7 fusion.5
  370.0 3.7 fusion.7
  376.9 3.8 fusion.9
  380.7 3.9 fusion.11
  384.6 3.6 fusion.13
  388.2 3.6 fusion.15
  391.9 14.3 %convolution_bitcast_fusion.2 = f32[32,2,4,128]{3,2,1,0:T(4,128)S(1)} fusion(bf16[32,2,2304,128]{3,2,1,0:T(8,128)(2,1)} %fusion.15, bf16[4,2304,1,1]{1,0,2,3:T(4,128)(2,1)S(1)} %reshape.168), kind=kOutput, calls=%fused_computation.31 | convolution fusion | flops 150994944 | bytes 37898240 | tf_op jit(solution)/shard_map/ck,jvkp->jvcp/dot_general | solution.py:128
  406.2 14.3 %fusion.18 = f32[34,2,4,128]{3,2,1,0:T(4,128)S(1)} fusion(f32[34,2,4,128]{3,2,1,0:T(4,128)S(1)} %dynamic_update_slice.9, bf16[32,2,2304,128]{3,2,1,0:T(8,128)(2,1)} %fusion.15, bf16[4,2304,1,1]{1,0,2,3:T(4,128)(2,1)S(1)} %reshape.169), kind=kOutput, calls=%fused_computation.33 | convolution fusion | flops 151027712 | bytes 38029312 | tf_op jit(solution)/shard_map/ck,jvkp->jvcp/dot_general | solution.py:128
  420.6 14.3 %fusion.20 = f32[34,2,4,128]{3,2,1,0:T(4,128)S(1)} fusion(f32[34,2,4,128]{3,2,1,0:T(4,128)S(1)} %fusion.18, bf16[32,2,2304,128]{3,2,1,0:T(8,128)(2,1)} %fusion.15, bf16[4,2304,1,1]{1,0,2,3:T(4,128)(2,1)S(1)} %reshape.170), kind=kOutput, calls=%fused_computation.35 | convolution fusion | flops 151027712 | bytes 38029312 | tf_op jit(solution)/shard_map/ck,jvkp->jvcp/dot_general | solution.py:128
  435.6 5.4 all-to-all-start.1
  442.1 7.8 %all-to-all-done.1 = bf16[32,2,4,128]{3,2,1,0:T(4,128)(2,1)S(1)} async-done(((bf16[32,2,4,128]{3,2,1,0:T(4,128)(2,1)}), bf16[32,2,4,128]{3,2,1,0:T(4,128)(2,1)S(1)}, u32[]{:S(2)}, u32[]{:S(2)}) %all-to-all-start.1) | async-done | bytes 65568 | tf_op jit(solution)/shard_map/all_to_all | solution.py:145
  463.1 21.6 %all-reduce.10.cloned.1.call-done = f32[27,256,4]{1,2,0:T(4,128)} async-done(((f32[27,256,4]{1,2,0:T(4,128)}), f32[27,256,4]{1,2,0:T(4,128)}) %all-reduce.10.cloned.1.call-update) | async-done | bytes 110608 | tf_op jit(solution)/shard_map/psum | solution.py:147
  484.7 153.0 %all-reduce.8.cloned.1.call-done = f32[27,128,64]{1,2,0:T(8,128)} async-done(((f32[27,128,64]{1,2,0:T(8,128)}), f32[27,128,64]{1,2,0:T(8,128)}) %all-reduce.8.cloned.1.call-update) | async-done | bytes 884752 | tf_op jit(solution)/shard_map/psum | solution.py:149
  (101 shorter events, 56.7 us)
Async XLA Ops:
  7.2 10.3 %copy-start = (bf16[27,256,128]{2,1,0:T(8,128)(2,1)S(1)}, bf16[27,256,128]{2,1,0:T(8,128)(2,1)}, u32[]{:S(2)}) copy-start(bf16[27,256,128]{2,1,0:T(8,128)(2,1)} %param.7) | copy-start | bytes 5308420
  9.0 13.7 %collective-permute-start.1 = (bf16[1,2,64,512]{3,2,1,0:T(8,128)(2,1)}, bf16[1,2,64,512]{3,2,1,0:T(8,128)(2,1)}, u32[]{:S(2)}, u32[]{:S(2)}) collective-permute-start(bf16[1,2,64,512]{3,2,1,0:T(8,128)(2,1)} %get-tuple-element.17), channel_id=1, source_target_pairs={{1,0},{2,1},{3,2},{4,3},{5,4},{6,5},{7,6},{8,7},{9,8},{10,9},{11,1... | collective-permute-start | bytes 393224 | tf_op jit(solution)/shard_map/ppermute | solution.py:20
  10.3 10.5 %collective-permute-start = (bf16[1,2,64,512]{3,2,1,0:T(8,128)(2,1)}, bf16[1,2,64,512]{3,2,1,0:T(8,128)(2,1)}, u32[]{:S(2)}, u32[]{:S(2)}) collective-permute-start(bf16[1,2,64,512]{3,2,1,0:T(8,128)(2,1)} %get-tuple-element.18), channel_id=1, source_target_pairs={{0,1},{1,2},{2,3},{3,4},{4,5},{5,6},{6,7},{7,8},{8,9},{9,10},{10,1... | collective-permute-start | bytes 393224 | tf_op jit(solution)/shard_map/ppermute | solution.py:18
  23.6 2.4 copy-start.4
  24.5 2.5 copy-start.5
  25.7 2.1 copy-start.7
  26.0 2.9 copy-start.3
  30.0 23.1 %all-to-all-start = ((bf16[1,2,128,128]{3,1,0,2:T(2,128)(2,1)}), bf16[1,2,128,128]{3,1,0,2:T(2,128)(2,1)S(1)}, u32[]{:S(2)}, u32[]{:S(2)}) async-start(bf16[1,2,128,128]{3,1,0,2:T(2,128)(2,1)} %copy.36), calls=%async_computation | async-start | bytes 131072 | tf_op jit(solution)/shard_map/all_to_all | solution.py:109
  44.2 199.6 %reduce-scatter.2.cloned.1.call-start = ((), (), s32[]{:S(2)}) async-start(), calls=%async_computation.3 | async-start | bytes 8650752 | tf_op jit(solution)/shard_map/reduce_scatter | solution.py:114
  59.0 2.1 copy-start.9
  61.2 1.3 copy-start.8
  67.2 278.9 %all-gather.2.cloned.1.call-start = ((), (), s32[]{:S(2)}) async-start(), calls=%async_computation.4 | async-start | bytes 4325376 | tf_op jit(solution)/shard_map/all_gather | solution.py:121
  356.7 6.0 copy-start.2
  435.6 14.3 %all-to-all-start.1 = ((bf16[32,2,4,128]{3,2,1,0:T(4,128)(2,1)}), bf16[32,2,4,128]{3,2,1,0:T(4,128)(2,1)S(1)}, u32[]{:S(2)}, u32[]{:S(2)}) async-start(bf16[32,2,4,128]{3,2,1,0:T(4,128)(2,1)} %slice.303), calls=%async_computation.2 | async-start | bytes 131072 | tf_op jit(solution)/shard_map/all_to_all | solution.py:145
  441.0 43.7 %all-reduce.10.cloned.1.call-start = ((), (), s32[]{:S(2)}) async-start(), calls=%async_computation.6 | async-start | bytes 221184 | tf_op jit(solution)/shard_map/psum | solution.py:147
  441.8 195.9 %all-reduce.8.cloned.1.call-start = ((), (), s32[]{:S(2)}) async-start(), calls=%async_computation.5 | async-start | bytes 1769472 | tf_op jit(solution)/shard_map/psum | solution.py:149
  454.9 5.6 slice-start
  455.3 5.2 slice-start.1
  457.9 183.5 %copy-start.1 = (bf16[27,256,128]{2,1,0:T(8,128)(2,1)S(1)}, bf16[27,256,128]{2,1,0:T(8,128)(2,1)}, u32[]{:S(2)}) copy-start(bf16[27,256,128]{2,1,0:T(8,128)(2,1)} %param.7) | copy-start | bytes 5308420
  460.5 1.8 copy-start.6
Sparse Core Ops, SparseCore 0:
  67.3 176.5 reduce-scatter.1
  247.5 98.5 all-gather.1
  444.9 39.7 all-reduce.9
  490.6 146.9 all-reduce.7
where the time goes:
time: 655 us; the launch traced here: 648 us
  waiting for transfers between devices  461 us (70%)
  matrix products  70.3 us (11%)
  other arithmetic  42.9 us (7%)
  local copies, waits for them, and re-layouts  32.8 us (5%)
  starting transfers between devices  26.9 us (4%)
  between operations  14.8 us (2%)
    reduce_scatter x1, waiting for transfers between devices, per_device(): lax.psum_scatter(convolve(window, arranged5), 'space', scatter_dimension=...  175 us
    psum x1, waiting for transfers between devices, per_device(): lax.psum(weight_grad(grad_pre4, stacked4, conv4_weight.shape[2]), ('dp',...  153 us
    all_gather x1, waiting for transfers between devices, per_device(): block_rows = lax.all_gather(grad_pre5, 'space', axis=0, tiled=True)  94.8 us
    dot_general x3, matrix products, per_device(): jnp.einsum('ck,jvkp->jvcp', back_weight[a], spread, preferred_element_typ...  43 us
    unnamed x17, other arithmetic  33.5 us
    psum x1, waiting for transfers between devices, per_device(): weight5 = lax.psum(weight5, 'dp')  21.6 us
    all_to_all x1, starting transfers between devices, per_device(): lax.all_to_all(inputs5, 'space', split_axis=2, concat_axis=0, tiled=True)  14.2 us
  transfers between devices with their start and end apart: 8, of which 6 were waited for; matrix products, arithmetic and copies ran while one was open for 4% of the time, Pallas kernels for 0%

commit v1 on v0

v1 whole, which is shorter than its diff:
```python
import jax
import jax.numpy as jnp
from jax import lax
from jax.experimental import pallas as pl
from jax.experimental.pallas import tpu as pltpu
from jax.sharding import PartitionSpec as P

HEIGHT = 32
WIDTH = 16
TAPS = tuple((b, e) for b in (-1, 0, 1) for e in (-1, 0, 1))
BF16 = jnp.bfloat16
F32 = jnp.float32
VMEM = pl.BlockSpec(memory_space=pltpu.VMEM)


def swap_pairs(count, phase):
    pairs = []
    for low in range(phase, count, 2):
        high = (low + 1) % count
        pairs += [(low, high), (high, low)]
    return pairs


def swapped(values, phase):
    return lax.ppermute(values, "space", swap_pairs(lax.axis_size("space"), phase))


def other_core(values):
    count = lax.axis_size("dp")
    return lax.ppermute(values, "dp", [(i, i ^ 1) for i in range(count)])


def neighbours(first, second):
    here = lax.axis_index("space")
    odd = here % 2 == 1
    below = jnp.where(odd, first, second)
    above = jnp.where(odd, second, first)
    below = jnp.where(here == 0, jnp.zeros_like(below), below)
    above = jnp.where(here == lax.axis_size("space") - 1, jnp.zeros_like(above), above)
    return below, above


def keep_mask(b, e, row_len, length):
    lane = lax.broadcasted_iota(jnp.int32, (1, length), 1)
    column = lane % row_len + e
    row = lane // row_len + b
    inside = (column >= 0) & (column < row_len) & (row >= 0) & (row < length // row_len)
    return inside.astype(F32)


def tap(values, b, e, row_len):
    length = values.shape[1]
    offset = b * row_len + e
    if offset == 0:
        return values
    return pltpu.roll(values, -offset % length, 1) * keep_mask(b, e, row_len, length)


def dot(left, right):
    return jnp.dot(left, right, preferred_element_type=F32)


def dot_rows(left, right):
    return lax.dot_general(left, right, (((1,), (1,)), ((), ())), preferred_element_type=F32)


def pool_matrix(fine_axis, shape):
    fine = lax.broadcasted_iota(jnp.int32, shape, fine_axis)
    coarse = lax.broadcasted_iota(jnp.int32, shape, 1 - fine_axis)
    owner = (fine // (2 * WIDTH)) * (WIDTH // 2) + (fine % WIDTH) // 2
    return (owner == coarse).astype(BF16)


def layer4_kernel(vol_ref, first_ref, second_ref, weight_ref, pooled_ref, slope_ref, stack_ref):
    chans, cells = vol_ref.shape[2], vol_ref.shape[3]
    rows = len(TAPS) * chans
    for n in range(2):
        below, above = neighbours(first_ref[n], second_ref[n])
        for j, plane in enumerate((below, vol_ref[0, n], vol_ref[1, n], above)):
            wide = plane.astype(F32)
            for t, (b, e) in enumerate(TAPS):
                stack_ref[pl.ds(j * rows + t * chans, chans), pl.ds(n * cells, cells)] = tap(
                    wide, b, e, WIDTH
                ).astype(BF16)
    pool = pool_matrix(0, (cells, cells // 4))
    for n in range(2):
        lanes = pl.ds(n * cells, cells)
        total = None
        for d in range(2):
            preact = dot(weight_ref[...], stack_ref[pl.ds(d * rows, 3 * rows), lanes])
            sig = jax.nn.sigmoid(preact)
            slope_ref[d, :, lanes] = sig * (1.0 + preact * (1.0 - sig)) * 0.125
            active = preact * sig
            total = active if total is None else total + active
        high = total.astype(BF16)
        low = (total - high.astype(F32)).astype(BF16)
        pooled = (dot(high, pool) + dot(low, pool)) * 0.125
        pooled_ref[:, pl.ds(n * cells // 4, cells // 4)] = pooled.astype(BF16)


def layer4(volumes, first, second, weight):
    vols, chans, cells = volumes.shape[1:]
    outer = weight.shape[0]
    return pl.pallas_call(
        layer4_kernel,
        out_shape=(
            jax.ShapeDtypeStruct((outer, vols * cells // 4), BF16),
            jax.ShapeDtypeStruct((2, outer, vols * cells), F32),
            jax.ShapeDtypeStruct((4 * len(TAPS) * chans, vols * cells), BF16),
        ),
        in_specs=[VMEM] * 4,
        out_specs=(VMEM, VMEM, VMEM),
        name="layer4",
    )(volumes, first, second, weight)


def spread_taps(planes, out_ref, row_len, cells, sign):
    chans = planes[0].shape[0]
    for j, plane in enumerate(planes):
        for n in range(plane.shape[1] // cells):
            wide = plane[:, n * cells : (n + 1) * cells].astype(F32)
            for t, (b, e) in enumerate(TAPS):
                out_ref[pl.ds((j * len(TAPS) + t) * chans, chans), pl.ds(n * cells, cells)] = tap(
                    wide, sign * b, sign * e, row_len
                ).astype(BF16)


def layer5_kernel(
    pooled_ref, first_ref, second_ref, weight_ref, cot_ref, out_ref, grad_ref, stack_ref
):
    below, above = neighbours(first_ref[...], second_ref[...])
    cells = cot_ref.shape[2]
    spread_taps((below, pooled_ref[...], above), stack_ref, WIDTH // 2, cells, 1)
    chans = pooled_ref.shape[0]
    preact = None
    for o in range(0, 27, 2):
        if o < 26:
            weight = jnp.concatenate([weight_ref[o], weight_ref[o + 1]], axis=1)
        else:
            weight = weight_ref[o]
        part = dot(weight, stack_ref[pl.ds(o * chans, weight.shape[1]), :])
        preact = part if preact is None else preact + part
    sig = jax.nn.sigmoid(preact)
    active = preact * sig
    slope = sig * (1.0 + preact * (1.0 - sig))
    for n in range(cot_ref.shape[0]):
        lanes = slice(n * cells, (n + 1) * cells)
        out_ref[n] = active[:, lanes].astype(BF16)
        grad_ref[:, lanes] = (cot_ref[n].astype(F32) * slope[:, lanes]).astype(BF16)


def layer5(pooled, first, second, weight, cot):
    vols, outer, cells = cot.shape
    return pl.pallas_call(
        layer5_kernel,
        out_shape=(
            jax.ShapeDtypeStruct((vols, outer, cells), BF16),
            jax.ShapeDtypeStruct((outer, vols * cells), BF16),
            jax.ShapeDtypeStruct((27 * pooled.shape[0], vols * cells), BF16),
        ),
        in_specs=[VMEM] * 5,
        out_specs=(VMEM, VMEM, VMEM),
        name="layer5",
    )(pooled, first, second, weight, cot)


def backward_kernel(
    grad_ref, first_ref, second_ref, back_ref, stack5_ref, stack4_ref, slope_ref,
    keep_ref, send_ref, spread_ref, acc_ref,
):
    core = lax.axis_index("dp") % 2
    grad = grad_ref[...]
    outer = grad.shape[0]
    half = outer // 2
    chans = back_ref.shape[1]
    cells = grad.shape[1] // 2
    top, bottom = grad[:half], grad[half:]
    ordered = jnp.concatenate(
        [jnp.where(core == 0, top, bottom), jnp.where(core == 0, bottom, top)], axis=0
    )
    for o in range(0, 27, 2):
        count = min(2, 27 - o)
        part = dot_rows(ordered, stack5_ref[pl.ds(o * chans, count * chans), :]).astype(BF16)
        for i in range(count):
            block = part[:, i * chans : (i + 1) * chans]
            for k in range(2):
                slot = 2 * (o + i) + k
                keep_ref[slot, pl.ds(0, 64), :] = block[k * 64 : (k + 1) * 64]
                send_ref[slot, pl.ds(0, 64), :] = block[half + k * 64 : half + (k + 1) * 64]
    below, above = neighbours(first_ref[...], second_ref[...])
    spread_taps((above, grad, below), spread_ref, WIDTH // 2, cells, -1)
    inward = None
    for o in range(27):
        part = dot(back_ref[o], spread_ref[pl.ds(o * outer, outer), :])
        inward = part if inward is None else inward + part
    inward = inward.astype(BF16)
    unpool = pool_matrix(1, (cells, 4 * cells))
    fine = jnp.concatenate(
        [dot(inward[:, n * cells : (n + 1) * cells], unpool) for n in range(2)], axis=1
    )
    grads = jnp.concatenate(
        [(fine * slope_ref[0]).astype(BF16), (fine * slope_ref[1]).astype(BF16)], axis=0
    )
    rows = stack4_ref.shape[0] // 4
    for j in range(4):
        plane = stack4_ref[pl.ds(j * rows, rows), :]
        if j == 0:
            acc_ref[pl.ds(0, rows), :] = dot_rows(plane, grads[:chans])
        elif j == 3:
            acc_ref[pl.ds(2 * rows, rows), :] += dot_rows(plane, grads[chans:])
        else:
            both = dot_rows(plane, grads)
            acc_ref[pl.ds(j * rows, rows), :] = both[:, :chans]
            acc_ref[pl.ds((j - 1) * rows, rows), :] += both[:, chans:]
    inner = rows // len(TAPS)
    quarter = inner // 4
    for o in range(27):
        for k in range(2):
            mine = pl.multiple_of(o * inner + core * (inner // 2) + k * quarter, quarter)
            theirs = pl.multiple_of(o * inner + (1 - core) * (inner // 2) + k * quarter, quarter)
            keep_ref[2 * o + k, pl.ds(64, quarter), :] = acc_ref[pl.ds(mine, quarter), :].astype(BF16)
            send_ref[2 * o + k, pl.ds(64, quarter), :] = acc_ref[pl.ds(theirs, quarter), :].astype(BF16)
    for slot in range(54, 64):
        keep_ref[slot] = jnp.zeros(keep_ref.shape[1:], BF16)
        send_ref[slot] = jnp.zeros(send_ref.shape[1:], BF16)


def backward(grad, first, second, back, stack5, stack4, slope):
    outer, lanes = grad.shape
    return pl.pallas_call(
        backward_kernel,
        out_shape=(
            jax.ShapeDtypeStruct((64, 80, 128), BF16),
            jax.ShapeDtypeStruct((64, 80, 128), BF16),
        ),
        in_specs=[VMEM] * 7,
        out_specs=(VMEM, VMEM),
        scratch_shapes=[
            pltpu.VMEM((27 * outer, lanes), BF16),
            pltpu.VMEM((3 * stack4.shape[0] // 4, back.shape[1]), F32),
        ],
        name="backward",
    )(grad, first, second, back, stack5, stack4, slope)


def per_device(volumes, cotangent, conv4_weight, conv5_weight):
    space = lax.axis_index("space")
    odd = space % 2
    first4 = swapped(lax.dynamic_index_in_dim(volumes, 1 - odd, 0, keepdims=False), 0)
    second4 = swapped(lax.dynamic_index_in_dim(volumes, odd, 0, keepdims=False), 1)
    arranged4 = conv4_weight.transpose(1, 0, 2).reshape(conv4_weight.shape[1], -1)
    back5 = conv5_weight.transpose(0, 2, 1)
    pooled, slope, stack4 = layer4(volumes, first4, second4, arranged4)
    output5, grad, stack5 = layer5(
        pooled, swapped(pooled, 0), swapped(pooled, 1), conv5_weight, cotangent[0]
    )
    keep, send = backward(grad, swapped(grad, 0), swapped(grad, 1), back5, stack5, stack4, slope)
    axes = ("dp", "space")
    spaces, groups = lax.axis_size("space"), lax.axis_size("dp")
    per_core = [
        [dp * spaces + s for dp in range(core, groups, 2) for s in range(spaces)]
        for core in range(2)
    ]

    def exchange(parts):
        return lax.all_to_all(
            parts, axes, split_axis=0, concat_axis=0, tiled=True, axis_index_groups=per_core
        )

    part = (keep.astype(F32) + other_core(send).astype(F32)).astype(BF16)
    owned = exchange(part).astype(F32).sum(axis=0).astype(BF16)
    rows5, rows4 = owned[:64], owned[64:]
    columns = jnp.pad(rows5.T.reshape(spaces, -1, 64), ((0, 0), (0, 4), (0, 64)))
    outgoing = jnp.concatenate(
        [
            jnp.broadcast_to(rows4, (64, 16, 128)),
            jnp.broadcast_to(columns, (2, spaces, 8, 128)).reshape(64, 8, 128),
        ],
        axis=1,
    )
    mine = exchange(outgoing)
    theirs = other_core(mine)
    core = lax.axis_index("dp") % 2
    zero = jnp.where(core == 0, mine, theirs)[:54]
    one = jnp.where(core == 0, theirs, mine)[:54]
    both = jnp.stack([zero, one]).reshape(2, 27, 2, 24, 128)
    weight4 = both[:, :, :, :16].transpose(1, 4, 0, 2, 3).reshape(27, 128, 64).astype(F32)
    weight5 = both[:, :, :, 16:20, :64].transpose(1, 0, 2, 4, 3).reshape(27, 256, 4).astype(F32)
    return (output5[None], weight4, weight5)


def solution(mesh):
    placed = (P("space", "dp", None, None), P("space", "dp", None, None), P(), P())
    return jax.shard_map(
        per_device,
        mesh=mesh,
        in_specs=placed,
        out_specs=(P("space", "dp", None, None), P(), P(None, None, "space")),
        check_vma=False,
    )
```

time: 655 us -> 115 us (0.18)
  waiting for transfers between devices: 461 us -> 11.9 us
  matrix products: 70.3 us -> 0 us
  blocking collectives: 0 us -> 43.2 us
  other arithmetic: 42.9 us -> 2.04 us
  local copies, waits for them, and re-layouts: 32.8 us -> 9.36 us
  Pallas kernels: 0 us -> 18.9 us
  between operations: 14.8 us -> 0.74 us
    reduce_scatter x1 -> x0, waiting for transfers between devices: 175 us -> none  [per_device(): lax.psum_scatter(convolve(window, arranged5), 'space', scatter_dimension=...]
    psum x2 -> x0, waiting for transfers between devices: 175 us -> none  [the longest x1 153 us: per_device(): lax.psum(weight_grad(grad_pre4, stacked4, conv4_weight.shape[2]), ('dp',...]
    all_gather x1 -> x0, waiting for transfers between devices: 94.8 us -> none  [per_device(): block_rows = lax.all_gather(grad_pre5, 'space', axis=0, tiled=True)]
    dot_general x15 -> x0, matrix products: 70.3 us -> none  [the longest x3 43 us: per_device(): jnp.einsum('ck,jvkp->jvcp', back_weight[a], spread, preferred_element_typ...]
    all_to_all x0 -> x2, blocking collectives: none -> 43.2 us  [exchange(): lax.all_to_all(parts, axes, split_axis=0, concat_axis=0, tiled=True, axis...]
    unnamed x17 -> x0, other arithmetic: 33.5 us -> none
    ppermute x2 -> x8, starting transfers between devices: 6.6 us -> 28.2 us  [the longest x6 21.7 us: swapped(): lax.ppermute(values, 'space', swap_pairs(lax.axis_size('space'), phase))]
    all_to_all x2 -> x0, starting transfers between devices: 19.7 us -> none  [the longest x1 14.2 us: per_device(): lax.all_to_all(inputs5, 'space', split_axis=2, concat_axis=0, tiled=True)]
  transfers between devices with their start and end apart: 8 -> 8, of which waited for: 6 -> 7; matrix products, arithmetic and copies ran while one was open for 4% -> 4% of each run, Pallas kernels for 0% -> 0%
where the time goes in v1:
time: 115 us; the launch traced here: 114 us
  blocking collectives  43.2 us (38%)
  starting transfers between devices  28.2 us (25%)
  Pallas kernels  18.9 us (16%)
  waiting for transfers between devices  11.9 us (10%)
  local copies, waits for them, and re-layouts  9.36 us (8%)
  other arithmetic  2.04 us (2%)
    all_to_all x2, blocking collectives, exchange(): lax.all_to_all(parts, axes, split_axis=0, concat_axis=0, tiled=True, axis...  43.2 us
    ppermute x6, starting transfers between devices, swapped(): lax.ppermute(values, 'space', swap_pairs(lax.axis_size('space'), phase))  21.7 us
    pallas_call x1, Pallas kernels, backward(): pl.pallas_call(backward_kernel, out_shape=(jax.ShapeDtypeStruct((64, 80,...  9.02 us
    ppermute x6, waiting for transfers between devices, swapped(): lax.ppermute(values, 'space', swap_pairs(lax.axis_size('space'), phase))  7.68 us
    ppermute x2, starting transfers between devices, other_core(): return lax.ppermute(values, 'dp', [(i, i ^ 1) for i in range(count)])  6.5 us
    pallas_call x1, Pallas kernels, layer4(): pl.pallas_call(layer4_kernel, out_shape=(jax.ShapeDtypeStruct((outer, vol...  6.1 us
    unnamed x15, local copies, waits for them, and re-layouts  4.25 us
    ppermute x2, waiting for transfers between devices, other_core(): return lax.ppermute(values, 'dp', [(i, i ^ 1) for i in range(count)])  4.22 us
  transfers between devices with their start and end apart: 8, of which 7 were waited for; matrix products, arithmetic and copies ran while one was open for 4% of the time, Pallas kernels for 0%

profile of v1, /device:TPU:1, one launch (start us, length us, event | category | flops | bytes accessed | tf_op | source)
XLA Modules:
  0.0 114.3 jit_solution(10261793645255061698)
XLA Ops:
  0.6 1.0 dynamic-slice_bitcast_fusion
  1.6 9.6 %collective-permute-start.1 = (bf16[2,64,512]{2,1,0:T(8,128)(2,1)S(1)}, bf16[2,64,512]{2,1,0:T(8,128)(2,1)S(1)}, u32[]{:S(2)}, u32[]{:S(2)}) collective-permute-start(bf16[2,64,512]{2,1,0:T(8,128)(2,1)S(1)} %get-tuple-element.21), channel_id=1, source_target_pairs={{1,2},{2,1},{3,4},{4,3},{5,6},{6,5},{7,8},{8,7},{9,10},{10,9},{11,... | collective-permute-start | bytes 393224 | tf_op jit(solution)/shard_map/ppermute | solution.py:25
  11.2 2.0 %copy.19.weight_ref = bf16[128,1728]{1,0:T(8,128)(2,1)} copy(bf16[128,1728]{0,1:T(8,128)(2,1)} %bitcast.30) | data formatting | bytes 884736 | tf_op jit(solution)/shard_map/reshape | solution.py:251
  13.2 1.2 %collective-permute-done.1.second_ref = bf16[2,64,512]{2,1,0:T(8,128)(2,1)S(1)} collective-permute-done((bf16[2,64,512]{2,1,0:T(8,128)(2,1)S(1)}, bf16[2,64,512]{2,1,0:T(8,128)(2,1)S(1)}, u32[]{:S(2)}, u32[]{:S(2)}) %collective-permute-start.1) | collective-permute-done | bytes 131104 | tf_op jit(solution)/shard_map/ppermute | solution.py:25
  14.4 0.8 collective-permute-done.first_ref
  15.3 0.7 copy-done.4
  15.9 6.1 %layer4.1 = (bf16[128,256]{1,0:T(8,128)(2,1)}, f32[2,128,1024]{2,1,0:T(8,128)}, bf16[2304,1024]{1,0:T(8,128)(2,1)}) custom-call(bf16[2,2,64,512]{3,2,1,0:T(8,128)(2,1)} %vol_ref.1, bf16[2,64,512]{2,1,0:T(8,128)(2,1)} %copy-done.4, bf16[2,64,512]{2,1,0:T(8,128)(2,1)} %copy-done.3, bf16[128,1728]{1,0:T(8,128)(2,1)} %copy.19.weight_ref), custom_call_target="tpu_custom_call" | custom-call | tf_op jit(solution)/shard_map/layer4/pallas_call | solution.py:104
  22.0 6.7 %collective-permute-start.3 = (bf16[128,256]{1,0:T(8,128)(2,1)}, bf16[128,256]{1,0:T(8,128)(2,1)S(1)}, u32[]{:S(2)}, u32[]{:S(2)}) collective-permute-start(bf16[128,256]{1,0:T(8,128)(2,1)} %get-tuple-element.11.pooled_ref), channel_id=1, source_target_pairs={{1,2},{2,1},{3,4},{4,3},{5,6},{6,5},{7,8},{8,7},{9,10},{10,9},{11,... | collective-permute-start | bytes 196616 | tf_op jit(solution)/shard_map/ppermute | solution.py:25
  28.7 2.4 %collective-permute-done.3.second_ref = bf16[128,256]{1,0:T(8,128)(2,1)S(1)} collective-permute-done((bf16[128,256]{1,0:T(8,128)(2,1)}, bf16[128,256]{1,0:T(8,128)(2,1)S(1)}, u32[]{:S(2)}, u32[]{:S(2)}) %collective-permute-start.3) | collective-permute-done | bytes 65568 | tf_op jit(solution)/shard_map/ppermute | solution.py:25
  31.1 1.3 %collective-permute-done.2.first_ref = bf16[128,256]{1,0:T(8,128)(2,1)S(1)} collective-permute-done((bf16[128,256]{1,0:T(8,128)(2,1)}, bf16[128,256]{1,0:T(8,128)(2,1)S(1)}, u32[]{:S(2)}, u32[]{:S(2)}) %collective-permute-start.2) | collective-permute-done | bytes 65568 | tf_op jit(solution)/shard_map/ppermute | solution.py:25
  33.0 3.8 %layer5.1 = (bf16[2,256,128]{2,1,0:T(8,128)(2,1)}, bf16[256,256]{1,0:T(8,128)(2,1)}, bf16[3456,256]{1,0:T(8,128)(2,1)}) custom-call(bf16[128,256]{1,0:T(8,128)(2,1)} %get-tuple-element.11.pooled_ref, bf16[128,256]{1,0:T(8,128)(2,1)} %copy-done.6, bf16[128,256]{1,0:T(8,128)(2,1)} %copy-done.5, bf16[27,256,128]{2,1,0:T(8,128)(2,1)} %weight_ref.1, ...), custom_call_target="tpu_custom_call" | custom-call | tf_op jit(solution)/shard_map/layer5/pallas_call | solution.py:154
  36.7 5.5 %collective-permute-start.5 = (bf16[256,256]{1,0:T(8,128)(2,1)}, bf16[256,256]{1,0:T(8,128)(2,1)S(1)}, u32[]{:S(2)}, u32[]{:S(2)}) collective-permute-start(bf16[256,256]{1,0:T(8,128)(2,1)} %get-tuple-element.13.grad_ref), channel_id=1, source_target_pairs={{1,2},{2,1},{3,4},{4,3},{5,6},{6,5},{7,8},{8,7},{9,10},{10,9},{11,... | collective-permute-start | bytes 393224 | tf_op jit(solution)/shard_map/ppermute | solution.py:25
  42.2 2.3 %copy.20 = bf16[27,256,128]{1,2,0:T(8,128)(2,1)} copy(bf16[27,256,128]{2,1,0:T(8,128)(2,1)S(1)} %copy-done) | data formatting | bytes 3538944 | tf_op args[3]
  44.5 2.0 %collective-permute-done.5.second_ref = bf16[256,256]{1,0:T(8,128)(2,1)S(1)} collective-permute-done((bf16[256,256]{1,0:T(8,128)(2,1)}, bf16[256,256]{1,0:T(8,128)(2,1)S(1)}, u32[]{:S(2)}, u32[]{:S(2)}) %collective-permute-start.5) | collective-permute-done | bytes 131104 | tf_op jit(solution)/shard_map/ppermute | solution.py:25
  47.2 9.0 %backward.1 = (bf16[64,80,128]{2,1,0:T(8,128)(2,1)}, bf16[64,80,128]{2,1,0:T(8,128)(2,1)}) custom-call(bf16[256,256]{1,0:T(8,128)(2,1)} %get-tuple-element.13.grad_ref, bf16[256,256]{1,0:T(8,128)(2,1)} %copy-done.2, bf16[256,256]{1,0:T(8,128)(2,1)} %copy-done.1, bf16[27,128,256]{2,1,0:T(8,128)(2,1)} %bitcast.23, ...), custom_call_target="tpu_custom_call" | custom-call | tf_op jit(solution)/shard_map/backward/pallas_call | solution.py:230
  56.2 3.8 %collective-permute-start.6 = (bf16[64,80,128]{2,1,0:T(8,128)(2,1)}, bf16[64,80,128]{2,1,0:T(8,128)(2,1)S(1)}, u32[]{:S(2)}, u32[]{:S(2)}) collective-permute-start(bf16[64,80,128]{2,1,0:T(8,128)(2,1)} %get-tuple-element.18), channel_id=1, source_target_pairs={{0,32},{32,0},{64,96},{96,64},{1,33},{33,1},{65,97},{97,65},{2,34}... | collective-permute-start | bytes 3932168 | tf_op jit(solution)/shard_map/ppermute | solution.py:30
  60.0 2.9 %collective-permute-done.6 = bf16[64,80,128]{2,1,0:T(8,128)(2,1)S(1)} collective-permute-done((bf16[64,80,128]{2,1,0:T(8,128)(2,1)}, bf16[64,80,128]{2,1,0:T(8,128)(2,1)S(1)}, u32[]{:S(2)}, u32[]{:S(2)}) %collective-permute-start.6) | collective-permute-done | bytes 1310752 | tf_op jit(solution)/shard_map/ppermute | solution.py:30
  62.9 1.7 %add_convert_fusion = bf16[64,80,128]{2,1,0:T(8,128)(2,1)S(1)} fusion(bf16[64,80,128]{2,1,0:T(8,128)(2,1)S(1)} %collective-permute-done.6, bf16[64,80,128]{2,1,0:T(8,128)(2,1)} %get-tuple-element.17), kind=kLoop, calls=%fused_computation | loop fusion | flops 2621440 | bytes 3932160 | tf_op jit(solution)/shard_map/convert_element_type | solution.py:270
  64.5 27.0 %all_to_all.10 = bf16[64,80,128]{2,1,0:T(8,128)(2,1)S(1)} all-to-all(bf16[64,80,128]{2,1,0:T(8,128)(2,1)S(1)} %add_convert_fusion), channel_id=1, replica_groups={{0,1,2,3,4,5,6,7,8,9,10,11,12,13,14,15,16,17,18,19,20,21,22,23,24,25,26..., dimensions={0} | all-to-all | bytes 2621440 | tf_op jit(solution)/shard_map/all_to_all | solution.py:266
  92.0 16.2 %all_to_all.11 = bf16[64,24,128]{2,1,0:T(8,128)(2,1)S(1)} all-to-all(bf16[64,24,128]{2,1,0:T(8,128)(2,1)S(1)} %pad_maximum_fusion), channel_id=1, replica_groups={{0,1,2,3,4,5,6,7,8,9,10,11,12,13,14,15,16,17,18,19,20,21,22,23,24,25,26..., dimensions={0} | all-to-all | bytes 786432 | tf_op jit(solution)/shard_map/all_to_all | solution.py:266
  108.2 2.7 %collective-permute-start.7 = (bf16[64,24,128]{2,1,0:T(8,128)(2,1)S(1)}, bf16[64,24,128]{2,1,0:T(8,128)(2,1)S(1)}, u32[]{:S(2)}, u32[]{:S(2)}) collective-permute-start(bf16[64,24,128]{2,1,0:T(8,128)(2,1)S(1)} %all_to_all.11), channel_id=1, source_target_pairs={{0,32},{32,0},{64,96},{96,64},{1,33},{33,1},{65,97},{97,65},{2,34}... | collective-permute-start | bytes 1179656 | tf_op jit(solution)/shard_map/ppermute | solution.py:30
  110.9 1.3 %collective-permute-done.7 = bf16[64,24,128]{2,1,0:T(8,128)(2,1)S(1)} collective-permute-done((bf16[64,24,128]{2,1,0:T(8,128)(2,1)S(1)}, bf16[64,24,128]{2,1,0:T(8,128)(2,1)S(1)}, u32[]{:S(2)}, u32[]{:S(2)}) %collective-permute-start.7) | collective-permute-done | bytes 393248 | tf_op jit(solution)/shard_map/ppermute | solution.py:30
  112.5 0.8 reshape.30
  113.3 1.0 copy.22
  (29 shorter events, 2.0 us)
Async XLA Ops:
  1.6 12.8 %collective-permute-start.1 = (bf16[2,64,512]{2,1,0:T(8,128)(2,1)S(1)}, bf16[2,64,512]{2,1,0:T(8,128)(2,1)S(1)}, u32[]{:S(2)}, u32[]{:S(2)}) collective-permute-start(bf16[2,64,512]{2,1,0:T(8,128)(2,1)S(1)} %get-tuple-element.21), channel_id=1, source_target_pairs={{1,2},{2,1},{3,4},{4,3},{5,6},{6,5},{7,8},{8,7},{9,10},{10,9},{11,... | collective-permute-start | bytes 393224 | tf_op jit(solution)/shard_map/ppermute | solution.py:25
  11.2 4.1 %collective-permute-start = (bf16[2,64,512]{2,1,0:T(8,128)(2,1)S(1)}, bf16[2,64,512]{2,1,0:T(8,128)(2,1)S(1)}, u32[]{:S(2)}, u32[]{:S(2)}) collective-permute-start(bf16[2,64,512]{2,1,0:T(8,128)(2,1)S(1)} %get-tuple-element.22), channel_id=1, source_target_pairs={{0,1},{1,0},{2,3},{3,2},{4,5},{5,4},{6,7},{7,6},{8,9},{9,8},{10,11... | collective-permute-start | bytes 393224 | tf_op jit(solution)/shard_map/ppermute | solution.py:25
  13.2 29.0 %copy-start = (bf16[27,256,128]{2,1,0:T(8,128)(2,1)S(1)}, bf16[27,256,128]{2,1,0:T(8,128)(2,1)}, u32[]{:S(2)}) copy-start(bf16[27,256,128]{2,1,0:T(8,128)(2,1)} %weight_ref.1) | copy-start | bytes 5308420
  14.4 0.8 copy-start.3
  15.3 0.7 copy-start.4
  22.0 9.1 %collective-permute-start.3 = (bf16[128,256]{1,0:T(8,128)(2,1)}, bf16[128,256]{1,0:T(8,128)(2,1)S(1)}, u32[]{:S(2)}, u32[]{:S(2)}) collective-permute-start(bf16[128,256]{1,0:T(8,128)(2,1)} %get-tuple-element.11.pooled_ref), channel_id=1, source_target_pairs={{1,2},{2,1},{3,4},{4,3},{5,6},{6,5},{7,8},{8,7},{9,10},{10,9},{11,... | collective-permute-start | bytes 196616 | tf_op jit(solution)/shard_map/ppermute | solution.py:25
  28.7 3.6 %collective-permute-start.2 = (bf16[128,256]{1,0:T(8,128)(2,1)}, bf16[128,256]{1,0:T(8,128)(2,1)S(1)}, u32[]{:S(2)}, u32[]{:S(2)}) collective-permute-start(bf16[128,256]{1,0:T(8,128)(2,1)} %get-tuple-element.11.pooled_ref), channel_id=1, source_target_pairs={{0,1},{1,0},{2,3},{3,2},{4,5},{5,4},{6,7},{7,6},{8,9},{9,8},{10,11... | collective-permute-start | bytes 196616 | tf_op jit(solution)/shard_map/ppermute | solution.py:25
  31.1 1.3 %copy-start.5 = (bf16[128,256]{1,0:T(8,128)(2,1)}, bf16[128,256]{1,0:T(8,128)(2,1)S(1)}, u32[]{:S(2)}) copy-start(bf16[128,256]{1,0:T(8,128)(2,1)S(1)} %collective-permute-done.3.second_ref) | copy-start | bytes 196612
  32.3 0.6 copy-start.6
  36.7 9.8 %collective-permute-start.5 = (bf16[256,256]{1,0:T(8,128)(2,1)}, bf16[256,256]{1,0:T(8,128)(2,1)S(1)}, u32[]{:S(2)}, u32[]{:S(2)}) collective-permute-start(bf16[256,256]{1,0:T(8,128)(2,1)} %get-tuple-element.13.grad_ref), channel_id=1, source_target_pairs={{1,2},{2,1},{3,4},{4,3},{5,6},{6,5},{7,8},{8,7},{9,10},{10,9},{11,... | collective-permute-start | bytes 393224 | tf_op jit(solution)/shard_map/ppermute | solution.py:25
  42.2 4.3 %collective-permute-start.4 = (bf16[256,256]{1,0:T(8,128)(2,1)}, bf16[256,256]{1,0:T(8,128)(2,1)S(1)}, u32[]{:S(2)}, u32[]{:S(2)}) collective-permute-start(bf16[256,256]{1,0:T(8,128)(2,1)} %get-tuple-element.13.grad_ref), channel_id=1, source_target_pairs={{0,1},{1,0},{2,3},{3,2},{4,5},{5,4},{6,7},{7,6},{8,9},{9,8},{10,11... | collective-permute-start | bytes 393224 | tf_op jit(solution)/shard_map/ppermute | solution.py:25
  46.5 0.6 copy-start.1
  46.5 0.7 copy-start.2
  56.2 6.7 %collective-permute-start.6 = (bf16[64,80,128]{2,1,0:T(8,128)(2,1)}, bf16[64,80,128]{2,1,0:T(8,128)(2,1)S(1)}, u32[]{:S(2)}, u32[]{:S(2)}) collective-permute-start(bf16[64,80,128]{2,1,0:T(8,128)(2,1)} %get-tuple-element.18), channel_id=1, source_target_pairs={{0,32},{32,0},{64,96},{96,64},{1,33},{33,1},{65,97},{97,65},{2,34}... | collective-permute-start | bytes 3932168 | tf_op jit(solution)/shard_map/ppermute | solution.py:30
  108.2 4.0 %collective-permute-start.7 = (bf16[64,24,128]{2,1,0:T(8,128)(2,1)S(1)}, bf16[64,24,128]{2,1,0:T(8,128)(2,1)S(1)}, u32[]{:S(2)}, u32[]{:S(2)}) collective-permute-start(bf16[64,24,128]{2,1,0:T(8,128)(2,1)S(1)} %all_to_all.11), channel_id=1, source_target_pairs={{0,32},{32,0},{64,96},{96,64},{1,33},{33,1},{65,97},{97,65},{2,34}... | collective-permute-start | bytes 1179656 | tf_op jit(solution)/shard_map/ppermute | solution.py:30

commit v2 on v1

--- a/solution.py
+++ b/solution.py
@@ -11,6 +11,20 @@
 BF16 = jnp.bfloat16
 F32 = jnp.float32
 VMEM = pl.BlockSpec(memory_space=pltpu.VMEM)
+
+
+def call(kernel, name, outputs, operands, scratch=(), room=12, flops=0):
+    moved = sum(x.size * x.dtype.itemsize for x in operands)
+    return pl.pallas_call(
+        kernel,
+        out_shape=tuple(pltpu.VMEM(shape, dtype) for shape, dtype in outputs),
+        in_specs=[VMEM] * len(operands),
+        out_specs=tuple(VMEM for _ in outputs),
+        scratch_shapes=list(scratch),
+        compiler_params=pltpu.CompilerParams(vmem_limit_bytes=room * 2**20),
+        cost_estimate=pl.CostEstimate(flops=flops, bytes_accessed=moved, transcendentals=0),
+        name=name,
+    )(*[pltpu.with_memory_space_constraint(x, pltpu.VMEM) for x in operands])
 
 
 def swap_pairs(count, phase):
@@ -101,17 +115,17 @@
 def layer4(volumes, first, second, weight):
     vols, chans, cells = volumes.shape[1:]
     outer = weight.shape[0]
-    return pl.pallas_call(
+    return call(
         layer4_kernel,
-        out_shape=(
-            jax.ShapeDtypeStruct((outer, vols * cells // 4), BF16),
-            jax.ShapeDtypeStruct((2, outer, vols * cells), F32),
-            jax.ShapeDtypeStruct((4 * len(TAPS) * chans, vols * cells), BF16),
+        "layer4",
+        (
+            ((outer, vols * cells // 4), BF16),
+            ((2, outer, vols * cells), F32),
+            ((4 * len(TAPS) * chans, vols * cells), BF16),
         ),
-        in_specs=[VMEM] * 4,
-        out_specs=(VMEM, VMEM, VMEM),
-        name="layer4",
-    )(volumes, first, second, weight)
+        (volumes, first, second, weight),
+        flops=2 * weight.size * 2 * vols * cells,
+    )
 
 
 def spread_taps(planes, out_ref, row_len, cells, sign):
@@ -125,8 +139,23 @@
                 ).astype(BF16)
 
 
+def inward_part(weight_ref, spread_ref, a):
+    outer = weight_ref.shape[1]
+    total = None
+    for t in range(len(TAPS)):
+        part = lax.dot_general(
+            weight_ref[(a + 1) * len(TAPS) + t],
+            spread_ref[pl.ds(t * outer, outer), :],
+            (((0,), (0,)), ((), ())),
+            preferred_element_type=F32,
+        )
+        total = part if total is None else total + part
+    return total
+
+
 def layer5_kernel(
-    pooled_ref, first_ref, second_ref, weight_ref, cot_ref, out_ref, grad_ref, stack_ref
+    pooled_ref, first_ref, second_ref, weight_ref, cot_ref,
+    out_ref, grad_ref, stack_ref, spread_ref, to_first_ref, to_second_ref,
 ):
     below, above = neighbours(first_ref[...], second_ref[...])
     cells = cot_ref.shape[2]
@@ -147,53 +176,76 @@
         lanes = slice(n * cells, (n + 1) * cells)
         out_ref[n] = active[:, lanes].astype(BF16)
         grad_ref[:, lanes] = (cot_ref[n].astype(F32) * slope[:, lanes]).astype(BF16)
+    spread_taps((grad_ref[...],), spread_ref, WIDTH // 2, cells, -1)
+    down = inward_part(weight_ref, spread_ref, -1).astype(BF16)
+    up = inward_part(weight_ref, spread_ref, 1).astype(BF16)
+    odd = lax.axis_index("space") % 2 == 1
+    to_first_ref[...] = jnp.where(odd, down, up)
+    to_second_ref[...] = jnp.where(odd, up, down)
 
 
 def layer5(pooled, first, second, weight, cot):
     vols, outer, cells = cot.shape
-    return pl.pallas_call(
+    chans, lanes = pooled.shape
+    return call(
         layer5_kernel,
-        out_shape=(
-            jax.ShapeDtypeStruct((vols, outer, cells), BF16),
-            jax.ShapeDtypeStruct((outer, vols * cells), BF16),
-            jax.ShapeDtypeStruct((27 * pooled.shape[0], vols * cells), BF16),
+        "layer5",
+        (
+            ((vols, outer, cells), BF16),
+            ((outer, lanes), BF16),
+            ((27 * chans, lanes), BF16),
+            ((len(TAPS) * outer, lanes), BF16),
+            ((chans, lanes), BF16),
+            ((chans, lanes), BF16),
         ),
-        in_specs=[VMEM] * 5,
-        out_specs=(VMEM, VMEM, VMEM),
-        name="layer5",
-    )(pooled, first, second, weight, cot)
-
-
-def backward_kernel(
-    grad_ref, first_ref, second_ref, back_ref, stack5_ref, stack4_ref, slope_ref,
-    keep_ref, send_ref, spread_ref, acc_ref,
-):
+        (pooled, first, second, weight, cot),
+        flops=4 * weight.size * lanes,
+    )
+
+
+def own_kernel(grad_ref, stack_ref, weight_ref, spread_ref, inward_ref, keep_ref, send_ref):
+    inward_ref[...] = inward_part(weight_ref, spread_ref, 0)
     core = lax.axis_index("dp") % 2
-    grad = grad_ref[...]
-    outer = grad.shape[0]
-    half = outer // 2
-    chans = back_ref.shape[1]
-    cells = grad.shape[1] // 2
-    top, bottom = grad[:half], grad[half:]
+    half = grad_ref.shape[0] // 2
+    chans = stack_ref.shape[0] // 27
+    top, bottom = grad_ref[pl.ds(0, half), :], grad_ref[pl.ds(half, half), :]
     ordered = jnp.concatenate(
         [jnp.where(core == 0, top, bottom), jnp.where(core == 0, bottom, top)], axis=0
     )
     for o in range(0, 27, 2):
         count = min(2, 27 - o)
-        part = dot_rows(ordered, stack5_ref[pl.ds(o * chans, count * chans), :]).astype(BF16)
+        part = dot_rows(ordered, stack_ref[pl.ds(o * chans, count * chans), :]).astype(BF16)
         for i in range(count):
             block = part[:, i * chans : (i + 1) * chans]
             for k in range(2):
                 slot = 2 * (o + i) + k
-                keep_ref[slot, pl.ds(0, 64), :] = block[k * 64 : (k + 1) * 64]
-                send_ref[slot, pl.ds(0, 64), :] = block[half + k * 64 : half + (k + 1) * 64]
+                keep_ref[slot] = block[k * 64 : (k + 1) * 64]
+                send_ref[slot] = block[half + k * 64 : half + (k + 1) * 64]
+
+
+def own_parts(grad, stack, weight, spread):
+    outputs = (
+        ((weight.shape[2], grad.shape[1]), F32),
+        ((54, 64, 128), BF16),
+        ((54, 64, 128), BF16),
+    )
+    return call(
+        own_kernel,
+        "own_parts",
+        outputs,
+        (grad, stack, weight, spread),
+        flops=2 * grad.size * stack.shape[0] + 2 * weight.size * grad.shape[1] // 3,
+    )
+
+
+def weight4_kernel(
+    inward_ref, first_ref, second_ref, stack_ref, slope_ref, keep_ref, send_ref, acc_ref
+):
+    core = lax.axis_index("dp") % 2
     below, above = neighbours(first_ref[...], second_ref[...])
-    spread_taps((above, grad, below), spread_ref, WIDTH // 2, cells, -1)
-    inward = None
-    for o in range(27):
-        part = dot(back_ref[o], spread_ref[pl.ds(o * outer, outer), :])
-        inward = part if inward is None else inward + part
-    inward = inward.astype(BF16)
+    inward = (inward_ref[...] + below.astype(F32) + above.astype(F32)).astype(BF16)
+    chans = inward.shape[0]
+    cells = inward.shape[1] // 2
     unpool = pool_matrix(1, (cells, 4 * cells))
     fine = jnp.concatenate(
         [dot(inward[:, n * cells : (n + 1) * cells], unpool) for n in range(2)], axis=1
@@ -201,9 +253,9 @@
     grads = jnp.concatenate(
         [(fine * slope_ref[0]).astype(BF16), (fine * slope_ref[1]).astype(BF16)], axis=0
     )
-    rows = stack4_ref.shape[0] // 4
+    rows = stack_ref.shape[0] // 4
     for j in range(4):
-        plane = stack4_ref[pl.ds(j * rows, rows), :]
+        plane = stack_ref[pl.ds(j * rows, rows), :]
         if j == 0:
             acc_ref[pl.ds(0, rows), :] = dot_rows(plane, grads[:chans])
         elif j == 3:
@@ -213,48 +265,73 @@
             acc_ref[pl.ds(j * rows, rows), :] = both[:, :chans]
             acc_ref[pl.ds((j - 1) * rows, rows), :] += both[:, chans:]
     inner = rows // len(TAPS)
-    quarter = inner // 4
+    share = inner // 4
     for o in range(27):
         for k in range(2):
-            mine = pl.multiple_of(o * inner + core * (inner // 2) + k * quarter, quarter)
-            theirs = pl.multiple_of(o * inner + (1 - core) * (inner // 2) + k * quarter, quarter)
-            keep_ref[2 * o + k, pl.ds(64, quarter), :] = acc_ref[pl.ds(mine, quarter), :].astype(BF16)
-            send_ref[2 * o + k, pl.ds(64, quarter), :] = acc_ref[pl.ds(theirs, quarter), :].astype(BF16)
-    for slot in range(54, 64):
-        keep_ref[slot] = jnp.zeros(keep_ref.shape[1:], BF16)
-        send_ref[slot] = jnp.zeros(send_ref.shape[1:], BF16)
-
-
-def backward(grad, first, second, back, stack5, stack4, slope):
-    outer, lanes = grad.shape
-    return pl.pallas_call(
-        backward_kernel,
-        out_shape=(
-            jax.ShapeDtypeStruct((64, 80, 128), BF16),
-            jax.ShapeDtypeStruct((64, 80, 128), BF16),
-        ),
-        in_specs=[VMEM] * 7,
-        out_specs=(VMEM, VMEM),
-        scratch_shapes=[
-            pltpu.VMEM((27 * outer, lanes), BF16),
-            pltpu.VMEM((3 * stack4.shape[0] // 4, back.shape[1]), F32),
-        ],
-        name="backward",
-    )(grad, first, second, back, stack5, stack4, slope)
+            mine = pl.multiple_of(o * inner + core * 2 * share + k * share, share)
+            theirs = pl.multiple_of(o * inner + (1 - core) * 2 * share + k * share, share)
+            keep_ref[2 * o + k] = acc_ref[pl.ds(mine, share), :].astype(BF16)
+            send_ref[2 * o + k] = acc_ref[pl.ds(theirs, share), :].astype(BF16)
+
+
+def weight4_parts(inward, first, second, stack, slope):
+    chans = inward.shape[0]
+    return call(
+        weight4_kernel,
+        "weight4_parts",
+        (((54, 16, 128), BF16), ((54, 16, 128), BF16)),
+        (inward, first, second, stack, slope),
+        scratch=[pltpu.VMEM((3 * stack.shape[0] // 4, chans), F32)],
+        flops=3 * stack.size * chans,
+    )
+
+
+def pair_kernel(keep5_ref, got5_ref, keep4_ref, got4_ref, out_ref):
+    rows5, rows4 = keep5_ref.shape[1], keep4_ref.shape[1]
+    for keep_ref, got_ref, at, rows in (
+        (keep5_ref, got5_ref, 0, rows5),
+        (keep4_ref, got4_ref, rows5, rows4),
+    ):
+
+        @pl.loop(0, keep_ref.shape[0])
+        def _(i, keep_ref=keep_ref, got_ref=got_ref, at=at, rows=rows):
+            total = keep_ref[i].astype(F32) + got_ref[i].astype(F32)
+            out_ref[i, pl.ds(at, rows), :] = total.astype(BF16)
+
+    for slot in range(keep5_ref.shape[0], out_ref.shape[0]):
+        out_ref[slot] = jnp.zeros(out_ref.shape[1:], BF16)
+
+
+def paired(keep5, got5, keep4, got4):
+    (out,) = call(pair_kernel, "pairs", (((64, 80, 128), BF16),), (keep5, got5, keep4, got4))
+    return out
+
+
+def sum_kernel(parts_ref, rows4_ref, columns5_ref):
+    def step(i, acc):
+        return acc + parts_ref[i].astype(F32)
+
+    total = lax.fori_loop(1, parts_ref.shape[0], step, parts_ref[0].astype(F32), unroll=9)
+    columns5_ref[...] = total[:64].T.astype(BF16)
+    rows4_ref[...] = total[64:].astype(BF16)
+
+
+def summed(parts):
+    return call(sum_kernel, "sums", (((16, 128), BF16), ((128, 64), BF16)), (parts,))
 
 
 def per_device(volumes, cotangent, conv4_weight, conv5_weight):
-    space = lax.axis_index("space")
-    odd = space % 2
+    odd = lax.axis_index("space") % 2
     first4 = swapped(lax.dynamic_index_in_dim(volumes, 1 - odd, 0, keepdims=False), 0)
     second4 = swapped(lax.dynamic_index_in_dim(volumes, odd, 0, keepdims=False), 1)
     arranged4 = conv4_weight.transpose(1, 0, 2).reshape(conv4_weight.shape[1], -1)
-    back5 = conv5_weight.transpose(0, 2, 1)
     pooled, slope, stack4 = layer4(volumes, first4, second4, arranged4)
-    output5, grad, stack5 = layer5(
+    output5, grad, stack5, spread5, to_first, to_second = layer5(
         pooled, swapped(pooled, 0), swapped(pooled, 1), conv5_weight, cotangent[0]
     )
-    keep, send = backward(grad, swapped(grad, 0), swapped(grad, 1), back5, stack5, stack4, slope)
+    first, second = swapped(to_first, 0), swapped(to_second, 1)
+    inward, keep5, send5 = own_parts(grad, stack5, conv5_weight, spread5)
+    keep4, send4 = weight4_parts(inward, first, second, stack4, slope)
     axes = ("dp", "space")
     spaces, groups = lax.axis_size("space"), lax.axis_size("dp")
     per_core = [
@@ -267,14 +344,13 @@
             parts, axes, split_axis=0, concat_axis=0, tiled=True, axis_index_groups=per_core
         )
 
-    part = (keep.astype(F32) + other_core(send).astype(F32)).astype(BF16)
-    owned = exchange(part).astype(F32).sum(axis=0).astype(BF16)
-    rows5, rows4 = owned[:64], owned[64:]
-    columns = jnp.pad(rows5.T.reshape(spaces, -1, 64), ((0, 0), (0, 4), (0, 64)))
+    part = paired(keep5, other_core(send5), keep4, other_core(send4))
+    rows4, columns5 = summed(exchange(part))
+    columns5 = jnp.pad(columns5.reshape(spaces, -1, 64), ((0, 0), (0, 4), (0, 64)))
     outgoing = jnp.concatenate(
         [
             jnp.broadcast_to(rows4, (64, 16, 128)),
-            jnp.broadcast_to(columns, (2, spaces, 8, 128)).reshape(64, 8, 128),
+            jnp.broadcast_to(columns5, (2, spaces, 8, 128)).reshape(64, 8, 128),
         ],
         axis=1,
     )

time: 115 us -> 97.7 us (0.85)
  Pallas kernels: 18.9 us -> 8.03 us
  local copies, waits for them, and re-layouts: 9.36 us -> 5.87 us
  other arithmetic: 2.04 us -> 0.18 us
    pallas_call x3 -> x6, Pallas kernels: 18.9 us -> 8.03 us  [call(): pl.pallas_call(kernel, out_shape=tuple((pltpu.VMEM(shape, dtype) for shap...]
    unnamed x15 -> x7, local copies, waits for them, and re-layouts: 4.25 us -> 1.61 us
    ppermute x2 -> x3, waiting for transfers between devices: 4.22 us -> 1.8 us  [other_core(): return lax.ppermute(values, 'dp', [(i, i ^ 1) for i in range(count)])]
    ppermute x6, waiting for transfers between devices: 7.68 us -> 9.98 us  [swapped(): lax.ppermute(values, 'space', swap_pairs(lax.axis_size('space'), phase))]
    convert_element_type x1 -> x0, other arithmetic: 1.66 us -> none  [per_device(): part = (keep.astype(F32) + other_core(send).astype(F32)).astype(BF16)]
    ppermute x2 -> x3, starting transfers between devices: 6.5 us -> 6.52 us  [other_core(): return lax.ppermute(values, 'dp', [(i, i ^ 1) for i in range(count)])]
  transfers between devices with their start and end apart: 8 -> 9, of which waited for: 7 -> 7; matrix products, arithmetic and copies ran while one was open for 4% -> 2% of each run, Pallas kernels for 0% -> 2%
where the time goes in v2:
time: 97.7 us; the launch traced here: 97.4 us
  blocking collectives  43.1 us (44%)
  starting transfers between devices  27.7 us (28%)
  waiting for transfers between devices  11.8 us (12%)
  Pallas kernels  8.03 us (8%)
  local copies, waits for them, and re-layouts  5.87 us (6%)
    all_to_all x2, blocking collectives, exchange(): lax.all_to_all(parts, axes, split_axis=0, concat_axis=0, tiled=True, axis...  43.1 us
    ppermute x6, starting transfers between devices, swapped(): lax.ppermute(values, 'space', swap_pairs(lax.axis_size('space'), phase))  21.2 us
    ppermute x6, waiting for transfers between devices, swapped(): lax.ppermute(values, 'space', swap_pairs(lax.axis_size('space'), phase))  9.98 us
    pallas_call x6, Pallas kernels, call(): pl.pallas_call(kernel, out_shape=tuple((pltpu.VMEM(shape, dtype) for shap...  8.03 us
    ppermute x3, starting transfers between devices, other_core(): return lax.ppermute(values, 'dp', [(i, i ^ 1) for i in range(count)])  6.52 us
  transfers between devices with their start and end apart: 9, of which 7 were waited for; matrix products, arithmetic and copies ran while one was open for 2% of the time, Pallas kernels for 2%

profile of v2, /device:TPU:1, one launch (start us, length us, event | category | flops | bytes accessed | tf_op | source)
XLA Modules:
  0.0 97.4 jit_solution(17700531061609799996)
XLA Ops:
  0.6 1.0 %dynamic-slice_bitcast_fusion = (bf16[2,64,512]{2,1,0:T(8,128)(2,1)S(1)}, bf16[2,64,512]{2,1,0:T(8,128)(2,1)S(1)}) fusion(bf16[2,2,64,512]{3,2,1,0:T(8,128)(2,1)} %vol_ref.1, s32[]{:T(128)S(6)} %select_n.32, s32[]{:T(128)S(6)} %select_n.31), kind=kLoop, calls=%fused_computation.8 | loop fusion | bytes 524296 | tf_op jit(solution)/shard_map/jit(dynamic_index_in_dim)/squeeze | solution.py:326
  1.6 9.6 %collective-permute-start.1 = (bf16[2,64,512]{2,1,0:T(8,128)(2,1)S(1)}, bf16[2,64,512]{2,1,0:T(8,128)(2,1)S(1)}, u32[]{:S(2)}, u32[]{:S(2)}) collective-permute-start(bf16[2,64,512]{2,1,0:T(8,128)(2,1)S(1)} %get-tuple-element.37), channel_id=1, source_target_pairs={{1,2},{2,1},{3,4},{4,3},{5,6},{6,5},{7,8},{8,7},{9,10},{10,9},{11,... | collective-permute-start | bytes 393224 | tf_op jit(solution)/shard_map/ppermute | solution.py:39
  11.2 1.3 %copy.10.weight_ref = bf16[128,1728]{1,0:T(8,128)(2,1)S(1)} copy(bf16[128,1728]{0,1:T(8,128)(2,1)} %bitcast.29) | data formatting | bytes 884736 | tf_op jit(solution)/shard_map/reshape | solution.py:327
  12.5 2.0 %collective-permute-done.1.second_ref = bf16[2,64,512]{2,1,0:T(8,128)(2,1)S(1)} collective-permute-done((bf16[2,64,512]{2,1,0:T(8,128)(2,1)S(1)}, bf16[2,64,512]{2,1,0:T(8,128)(2,1)S(1)}, u32[]{:S(2)}, u32[]{:S(2)}) %collective-permute-start.1) | collective-permute-done | bytes 131104 | tf_op jit(solution)/shard_map/ppermute | solution.py:39
  14.4 0.8 collective-permute-done.first_ref
  15.3 0.9 copy-done.1
  16.2 2.5 %layer4.1 = (bf16[128,256]{1,0:T(8,128)(2,1)S(1)}, f32[2,128,1024]{2,1,0:T(8,128)S(1)}, bf16[2304,1024]{1,0:T(8,128)(2,1)S(1)}) custom-call(bf16[2,2,64,512]{3,2,1,0:T(8,128)(2,1)S(1)} %copy-done.1, bf16[2,64,512]{2,1,0:T(8,128)(2,1)S(1)} %collective-permute-done.first_ref, bf16[2,64,512]{2,1,0:T(8,128)(2,1)S(1)} %collective-permute-done.1.second_ref, ...), custom_call_target="tpu_custom_call" | custom-call | flops 905969664 | bytes 966656 | tf_op jit(solution)/shard_map/layer4/pallas_call | solution.py:18
  18.7 6.1 %collective-permute-start.3 = (bf16[128,256]{1,0:T(8,128)(2,1)S(1)}, bf16[128,256]{1,0:T(8,128)(2,1)S(1)}, u32[]{:S(2)}, u32[]{:S(2)}) collective-permute-start(bf16[128,256]{1,0:T(8,128)(2,1)S(1)} %get-tuple-element.19.pooled_ref), channel_id=1, source_target_pairs={{1,2},{2,1},{3,4},{4,3},{5,6},{6,5},{7,8},{8,7},{9,10},{10,9},{11,... | collective-permute-start | bytes 196616 | tf_op jit(solution)/shard_map/ppermute | solution.py:39
  24.9 2.8 %collective-permute-done.3.second_ref = bf16[128,256]{1,0:T(8,128)(2,1)S(1)} collective-permute-done((bf16[128,256]{1,0:T(8,128)(2,1)S(1)}, bf16[128,256]{1,0:T(8,128)(2,1)S(1)}, u32[]{:S(2)}, u32[]{:S(2)}) %collective-permute-start.3) | collective-permute-done | bytes 65568 | tf_op jit(solution)/shard_map/ppermute | solution.py:39
  28.3 2.0 %layer5.1 = (bf16[2,256,128]{2,1,0:T(8,128)(2,1)S(1)}, bf16[256,256]{1,0:T(8,128)(2,1)S(1)}, bf16[3456,256]{1,0:T(8,128)(2,1)S(1)}, bf16[2304,256]{1,0:T(8,128)(...) custom-call(bf16[128,256]{1,0:T(8,128)(2,1)S(1)} %get-tuple-element.19.pooled_ref, ...), custom_call_target="tpu_custom_call" | custom-call | flops 905969664 | bytes 2097152 | tf_op jit(solution)/shard_map/layer5/pallas_call | solution.py:18
  30.3 0.9 own_parts.1
  31.1 2.8 %collective-permute-start.4 = (bf16[54,64,128]{2,1,0:T(8,128)(2,1)S(1)}, bf16[54,64,128]{2,1,0:T(8,128)(2,1)S(1)}, u32[]{:S(2)}, u32[]{:S(2)}) collective-permute-start(bf16[54,64,128]{2,1,0:T(8,128)(2,1)S(1)} %get-tuple-element.25), channel_id=1, source_target_pairs={{0,32},{32,0},{64,96},{96,64},{1,33},{33,1},{65,97},{97,65},{2,34}... | collective-permute-start | bytes 2654216 | tf_op jit(solution)/shard_map/ppermute | solution.py:44
  33.9 5.5 %collective-permute-start.6 = (bf16[128,256]{1,0:T(8,128)(2,1)S(1)}, bf16[128,256]{1,0:T(8,128)(2,1)S(1)}, u32[]{:S(2)}, u32[]{:S(2)}) collective-permute-start(bf16[128,256]{1,0:T(8,128)(2,1)S(1)} %get-tuple-element.28), channel_id=1, source_target_pairs={{1,2},{2,1},{3,4},{4,3},{5,6},{6,5},{7,8},{8,7},{9,10},{10,9},{11,... | collective-permute-start | bytes 196616 | tf_op jit(solution)/shard_map/ppermute | solution.py:39
  39.3 3.8 %collective-permute-done.6.second_ref = bf16[128,256]{1,0:T(8,128)(2,1)S(1)} collective-permute-done((bf16[128,256]{1,0:T(8,128)(2,1)S(1)}, bf16[128,256]{1,0:T(8,128)(2,1)S(1)}, u32[]{:S(2)}, u32[]{:S(2)}) %collective-permute-start.6) | collective-permute-done | bytes 65568 | tf_op jit(solution)/shard_map/ppermute | solution.py:39
  43.1 1.6 %weight4_parts.1 = (bf16[54,16,128]{2,1,0:T(8,128)(2,1)S(1)}, bf16[54,16,128]{2,1,0:T(8,128)(2,1)S(1)}) custom-call(f32[128,256]{1,0:T(8,128)S(1)} %get-tuple-element.26.inward_ref, bf16[128,256]{1,0:T(8,128)(2,1)S(1)} %collective-permute-done.5.first_ref, bf16[128,256]{1,0:T(8,128)(2,1)S(1)} %collective-permute-done.6.second_ref, ...), custom_call_target="tpu_custom_call" | custom-call | flops 905969664 | bytes 6029312 | tf_op jit(solution)/shard_map/weight4_parts/pallas_call | solution.py:18
  44.7 1.1 %collective-permute-start.7 = (bf16[54,16,128]{2,1,0:T(8,128)(2,1)S(1)}, bf16[54,16,128]{2,1,0:T(8,128)(2,1)S(1)}, u32[]{:S(2)}, u32[]{:S(2)}) collective-permute-start(bf16[54,16,128]{2,1,0:T(8,128)(2,1)S(1)} %get-tuple-element.32), channel_id=1, source_target_pairs={{0,32},{32,0},{64,96},{96,64},{1,33},{33,1},{65,97},{97,65},{2,34}... | collective-permute-start | bytes 663560 | tf_op jit(solution)/shard_map/ppermute | solution.py:44
  45.8 1.1 %collective-permute-done.7.got4_ref = bf16[54,16,128]{2,1,0:T(8,128)(2,1)S(1)} collective-permute-done((bf16[54,16,128]{2,1,0:T(8,128)(2,1)S(1)}, bf16[54,16,128]{2,1,0:T(8,128)(2,1)S(1)}, u32[]{:S(2)}, u32[]{:S(2)}) %collective-permute-start.7) | collective-permute-done | bytes 221216 | tf_op jit(solution)/shard_map/ppermute | solution.py:44
  46.9 0.8 pairs.1
  47.7 27.0 %all_to_all.10.parts_ref = bf16[64,80,128]{2,1,0:T(8,128)(2,1)S(1)} all-to-all(bf16[64,80,128]{2,1,0:T(8,128)(2,1)S(1)} %pairs.1), channel_id=1, replica_groups={{0,1,2,3,4,5,6,7,8,9,10,11,12,13,14,15,16,17,18,19,20,21,22,23,24,25,26..., dimensions={0} | all-to-all | bytes 2621440 | tf_op jit(solution)/shard_map/all_to_all | solution.py:343
  75.1 16.2 %all_to_all.11 = bf16[64,24,128]{2,1,0:T(8,128)(2,1)S(1)} all-to-all(bf16[64,24,128]{2,1,0:T(8,128)(2,1)S(1)} %pad_maximum_fusion), channel_id=1, replica_groups={{0,1,2,3,4,5,6,7,8,9,10,11,12,13,14,15,16,17,18,19,20,21,22,23,24,25,26..., dimensions={0} | all-to-all | bytes 786432 | tf_op jit(solution)/shard_map/all_to_all | solution.py:343
  91.3 2.7 %collective-permute-start.8 = (bf16[64,24,128]{2,1,0:T(8,128)(2,1)S(1)}, bf16[64,24,128]{2,1,0:T(8,128)(2,1)S(1)}, u32[]{:S(2)}, u32[]{:S(2)}) collective-permute-start(bf16[64,24,128]{2,1,0:T(8,128)(2,1)S(1)} %all_to_all.11), channel_id=1, source_target_pairs={{0,32},{32,0},{64,96},{96,64},{1,33},{33,1},{65,97},{97,65},{2,34}... | collective-permute-start | bytes 1179656 | tf_op jit(solution)/shard_map/ppermute | solution.py:44
  94.6 0.7 collective-permute-done.8
  95.6 0.8 reshape.30
  96.5 1.0 %copy.11 = f32[27,128,2,2,16]{1,4,3,2,0:T(8,128)} copy(f32[27,128,2,2,16]{1,4,3,0,2:T(8,128)S(1)} %convert_bitcast_fusion) | data formatting | bytes 1769472 | tf_op jit(solution)/shard_map/convert_element_type | solution.py:363
  (21 shorter events, 1.9 us)
Async XLA Ops:
  1.6 12.8 %collective-permute-start.1 = (bf16[2,64,512]{2,1,0:T(8,128)(2,1)S(1)}, bf16[2,64,512]{2,1,0:T(8,128)(2,1)S(1)}, u32[]{:S(2)}, u32[]{:S(2)}) collective-permute-start(bf16[2,64,512]{2,1,0:T(8,128)(2,1)S(1)} %get-tuple-element.37), channel_id=1, source_target_pairs={{1,2},{2,1},{3,4},{4,3},{5,6},{6,5},{7,8},{8,7},{9,10},{10,9},{11,... | collective-permute-start | bytes 393224 | tf_op jit(solution)/shard_map/ppermute | solution.py:39
  11.2 4.1 %collective-permute-start = (bf16[2,64,512]{2,1,0:T(8,128)(2,1)S(1)}, bf16[2,64,512]{2,1,0:T(8,128)(2,1)S(1)}, u32[]{:S(2)}, u32[]{:S(2)}) collective-permute-start(bf16[2,64,512]{2,1,0:T(8,128)(2,1)S(1)} %get-tuple-element.38), channel_id=1, source_target_pairs={{0,1},{1,0},{2,3},{3,2},{4,5},{5,4},{6,7},{7,6},{8,9},{9,8},{10,11... | collective-permute-start | bytes 393224 | tf_op jit(solution)/shard_map/ppermute | solution.py:39
  11.2 17.1 %copy-start.2 = (bf16[1,2,256,128]{3,2,1,0:T(8,128)(2,1)S(1)}, bf16[1,2,256,128]{3,2,1,0:T(8,128)(2,1)}, u32[]{:S(2)}) copy-start(bf16[1,2,256,128]{3,2,1,0:T(8,128)(2,1)} %param.5) | copy-start | bytes 393220
  12.5 15.8 %copy-start = (bf16[27,256,128]{2,1,0:T(8,128)(2,1)S(1)}, bf16[27,256,128]{2,1,0:T(8,128)(2,1)}, u32[]{:S(2)}) copy-start(bf16[27,256,128]{2,1,0:T(8,128)(2,1)} %weight_ref.3) | copy-start | bytes 5308420
  15.3 1.0 copy-start.1
  18.7 8.9 %collective-permute-start.3 = (bf16[128,256]{1,0:T(8,128)(2,1)S(1)}, bf16[128,256]{1,0:T(8,128)(2,1)S(1)}, u32[]{:S(2)}, u32[]{:S(2)}) collective-permute-start(bf16[128,256]{1,0:T(8,128)(2,1)S(1)} %get-tuple-element.19.pooled_ref), channel_id=1, source_target_pairs={{1,2},{2,1},{3,4},{4,3},{5,6},{6,5},{7,8},{8,7},{9,10},{10,9},{11,... | collective-permute-start | bytes 196616 | tf_op jit(solution)/shard_map/ppermute | solution.py:39
  24.9 3.4 %collective-permute-start.2 = (bf16[128,256]{1,0:T(8,128)(2,1)S(1)}, bf16[128,256]{1,0:T(8,128)(2,1)S(1)}, u32[]{:S(2)}, u32[]{:S(2)}) collective-permute-start(bf16[128,256]{1,0:T(8,128)(2,1)S(1)} %get-tuple-element.19.pooled_ref), channel_id=1, source_target_pairs={{0,1},{1,0},{2,3},{3,2},{4,5},{5,4},{6,7},{7,6},{8,9},{9,8},{10,11... | collective-permute-start | bytes 196616 | tf_op jit(solution)/shard_map/ppermute | solution.py:39
  31.1 15.8 %collective-permute-start.4 = (bf16[54,64,128]{2,1,0:T(8,128)(2,1)S(1)}, bf16[54,64,128]{2,1,0:T(8,128)(2,1)S(1)}, u32[]{:S(2)}, u32[]{:S(2)}) collective-permute-start(bf16[54,64,128]{2,1,0:T(8,128)(2,1)S(1)} %get-tuple-element.25), channel_id=1, source_target_pairs={{0,32},{32,0},{64,96},{96,64},{1,33},{33,1},{65,97},{97,65},{2,34}... | collective-permute-start | bytes 2654216 | tf_op jit(solution)/shard_map/ppermute | solution.py:44
  33.9 5.5 %collective-permute-start.5 = (bf16[128,256]{1,0:T(8,128)(2,1)S(1)}, bf16[128,256]{1,0:T(8,128)(2,1)S(1)}, u32[]{:S(2)}, u32[]{:S(2)}) collective-permute-start(bf16[128,256]{1,0:T(8,128)(2,1)S(1)} %get-tuple-element.27), channel_id=1, source_target_pairs={{0,1},{1,0},{2,3},{3,2},{4,5},{5,4},{6,7},{7,6},{8,9},{9,8},{10,11... | collective-permute-start | bytes 196616 | tf_op jit(solution)/shard_map/ppermute | solution.py:39
  33.9 9.2 %collective-permute-start.6 = (bf16[128,256]{1,0:T(8,128)(2,1)S(1)}, bf16[128,256]{1,0:T(8,128)(2,1)S(1)}, u32[]{:S(2)}, u32[]{:S(2)}) collective-permute-start(bf16[128,256]{1,0:T(8,128)(2,1)S(1)} %get-tuple-element.28), channel_id=1, source_target_pairs={{1,2},{2,1},{3,4},{4,3},{5,6},{6,5},{7,8},{8,7},{9,10},{10,9},{11,... | collective-permute-start | bytes 196616 | tf_op jit(solution)/shard_map/ppermute | solution.py:39
  44.7 2.2 %collective-permute-start.7 = (bf16[54,16,128]{2,1,0:T(8,128)(2,1)S(1)}, bf16[54,16,128]{2,1,0:T(8,128)(2,1)S(1)}, u32[]{:S(2)}, u32[]{:S(2)}) collective-permute-start(bf16[54,16,128]{2,1,0:T(8,128)(2,1)S(1)} %get-tuple-element.32), channel_id=1, source_target_pairs={{0,32},{32,0},{64,96},{96,64},{1,33},{33,1},{65,97},{97,65},{2,34}... | collective-permute-start | bytes 663560 | tf_op jit(solution)/shard_map/ppermute | solution.py:44
  91.3 4.0 %collective-permute-start.8 = (bf16[64,24,128]{2,1,0:T(8,128)(2,1)S(1)}, bf16[64,24,128]{2,1,0:T(8,128)(2,1)S(1)}, u32[]{:S(2)}, u32[]{:S(2)}) collective-permute-start(bf16[64,24,128]{2,1,0:T(8,128)(2,1)S(1)} %all_to_all.11), channel_id=1, source_target_pairs={{0,32},{32,0},{64,96},{96,64},{1,33},{33,1},{65,97},{97,65},{2,34}... | collective-permute-start | bytes 1179656 | tf_op jit(solution)/shard_map/ppermute | solution.py:44

commit v3 on v2

v3 whole, which is shorter than its diff:
```python
import jax
import jax.numpy as jnp
from jax import lax
from jax.experimental import pallas as pl
from jax.experimental.pallas import tpu as pltpu
from jax.sharding import PartitionSpec as P

HEIGHT = 32
WIDTH = 16
TAPS = tuple((b, e) for b in (-1, 0, 1) for e in (-1, 0, 1))
BF16 = jnp.bfloat16
F32 = jnp.float32
VMEM = pl.BlockSpec(memory_space=pltpu.VMEM)


def call(kernel, name, outputs, operands, scratch=(), room=12, flops=0, aliases=None):
    moved = sum(x.size * x.dtype.itemsize for x in operands)
    return pl.pallas_call(
        kernel,
        out_shape=tuple(pltpu.VMEM(shape, dtype) for shape, dtype in outputs),
        in_specs=[VMEM] * len(operands),
        out_specs=tuple(VMEM for _ in outputs),
        scratch_shapes=list(scratch),
        input_output_aliases=aliases or {},
        compiler_params=pltpu.CompilerParams(vmem_limit_bytes=room * 2**20),
        cost_estimate=pl.CostEstimate(flops=flops, bytes_accessed=moved, transcendentals=0),
        name=name,
    )(*[pltpu.with_memory_space_constraint(x, pltpu.VMEM) for x in operands])


def swap_pairs(count, phase):
    pairs = []
    for low in range(phase, count, 2):
        high = (low + 1) % count
        pairs += [(low, high), (high, low)]
    return pairs


def swapped(values, phase):
    return lax.ppermute(values, "space", swap_pairs(lax.axis_size("space"), phase))


def other_core(values):
    count = lax.axis_size("dp")
    return lax.ppermute(values, "dp", [(i, i ^ 1) for i in range(count)])


def neighbours(first, second):
    here = lax.axis_index("space")
    odd = here % 2 == 1
    below = jnp.where(odd, first, second)
    above = jnp.where(odd, second, first)
    below = jnp.where(here == 0, jnp.zeros_like(below), below)
    above = jnp.where(here == lax.axis_size("space") - 1, jnp.zeros_like(above), above)
    return below, above


def keep_mask(b, e, row_len, length):
    lane = lax.broadcasted_iota(jnp.int32, (1, length), 1)
    column = lane % row_len + e
    row = lane // row_len + b
    inside = (column >= 0) & (column < row_len) & (row >= 0) & (row < length // row_len)
    return inside.astype(F32)


def tap(values, b, e, row_len):
    length = values.shape[1]
    offset = b * row_len + e
    if offset == 0:
        return values
    return pltpu.roll(values, -offset % length, 1) * keep_mask(b, e, row_len, length)


def dot(left, right):
    return jnp.dot(left, right, preferred_element_type=F32)


def dot_rows(left, right):
    return lax.dot_general(left, right, (((1,), (1,)), ((), ())), preferred_element_type=F32)


def pool_matrix(fine_axis, shape):
    fine = lax.broadcasted_iota(jnp.int32, shape, fine_axis)
    coarse = lax.broadcasted_iota(jnp.int32, shape, 1 - fine_axis)
    owner = (fine // (2 * WIDTH)) * (WIDTH // 2) + (fine % WIDTH) // 2
    return (owner == coarse).astype(BF16)


def stack_plane(plane, out_ref, j, n):
    chans, cells = plane.shape
    wide = plane.astype(F32)
    for t, (b, e) in enumerate(TAPS):
        out_ref[pl.ds((j * len(TAPS) + t) * chans, chans), pl.ds(n * cells, cells)] = tap(
            wide, b, e, WIDTH
        ).astype(BF16)


def own4_kernel(vol_ref, weight_ref, part_ref, stack_ref):
    rows = len(TAPS) * vol_ref.shape[2]
    for n in range(2):
        for d in range(2):
            stack_plane(vol_ref[d, n], stack_ref, 1 + d, n)
    for d in range(2):
        part_ref[d] = dot(
            weight_ref[:, (1 - d) * rows : (3 - d) * rows], stack_ref[pl.ds(rows, 2 * rows), :]
        )


def own4(volumes, weight):
    vols, chans, cells = volumes.shape[1:]
    return call(
        own4_kernel,
        "own4",
        (
            ((2, weight.shape[0], vols * cells), F32),
            ((4 * len(TAPS) * chans, vols * cells), BF16),
        ),
        (volumes, weight),
        flops=2 * weight.size * 2 * vols * cells,
    )


def layer4_kernel(
    first_ref, second_ref, weight_ref, part_ref, _, pooled_ref, slope_ref, stack_ref
):
    chans, cells = first_ref.shape[1:]
    rows = len(TAPS) * chans
    for n in range(2):
        below, above = neighbours(first_ref[n], second_ref[n])
        stack_plane(below, stack_ref, 0, n)
        stack_plane(above, stack_ref, 3, n)
    pool = pool_matrix(0, (cells, cells // 4))
    for n in range(2):
        lanes = pl.ds(n * cells, cells)
        total = None
        for d in range(2):
            preact = part_ref[d, :, lanes] + dot(
                weight_ref[:, 2 * d * rows : (2 * d + 1) * rows],
                stack_ref[pl.ds(3 * d * rows, rows), lanes],
            )
            sig = jax.nn.sigmoid(preact)
            slope_ref[d, :, lanes] = sig * (1.0 + preact * (1.0 - sig)) * 0.125
            active = preact * sig
            total = active if total is None else total + active
        high = total.astype(BF16)
        low = (total - high.astype(F32)).astype(BF16)
        pooled = (dot(high, pool) + dot(low, pool)) * 0.125
        pooled_ref[:, pl.ds(n * cells // 4, cells // 4)] = pooled.astype(BF16)


def layer4(first, second, weight, part, stack):
    lanes = stack.shape[1]
    return call(
        layer4_kernel,
        "layer4",
        (((weight.shape[0], lanes // 4), BF16), (part.shape, F32), (stack.shape, BF16)),
        (first, second, weight, part, stack),
        flops=2 * weight.size * lanes,
        aliases={3: 1, 4: 2},
    )


def spread_taps(planes, out_ref, row_len, cells, sign):
    chans = planes[0].shape[0]
    for j, plane in enumerate(planes):
        for n in range(plane.shape[1] // cells):
            wide = plane[:, n * cells : (n + 1) * cells].astype(F32)
            for t, (b, e) in enumerate(TAPS):
                out_ref[pl.ds((j * len(TAPS) + t) * chans, chans), pl.ds(n * cells, cells)] = tap(
                    wide, sign * b, sign * e, row_len
                ).astype(BF16)


def inward_part(weight_ref, spread_ref, a):
    outer = weight_ref.shape[1]
    total = None
    for t in range(len(TAPS)):
        part = lax.dot_general(
            weight_ref[(a + 1) * len(TAPS) + t],
            spread_ref[pl.ds(t * outer, outer), :],
            (((0,), (0,)), ((), ())),
            preferred_element_type=F32,
        )
        total = part if total is None else total + part
    return total


def convolved5(weight_ref, stack_ref, a):
    chans = weight_ref.shape[2]
    first = (a + 1) * len(TAPS)
    total = None
    for o in range(first, first + len(TAPS), 2):
        if o + 1 < first + len(TAPS):
            weight = jnp.concatenate([weight_ref[o], weight_ref[o + 1]], axis=1)
        else:
            weight = weight_ref[o]
        part = dot(weight, stack_ref[pl.ds(o * chans, weight.shape[1]), :])
        total = part if total is None else total + part
    return total


def own5_kernel(pooled_ref, weight_ref, part_ref, stack_ref):
    rows = len(TAPS) * pooled_ref.shape[0]
    cells = pooled_ref.shape[1] // 2
    spread_taps((pooled_ref[...],), stack_ref.at[pl.ds(rows, rows), :], WIDTH // 2, cells, 1)
    part_ref[...] = convolved5(weight_ref, stack_ref, 0)


def own5(pooled, weight):
    chans, lanes = pooled.shape
    return call(
        own5_kernel,
        "own5",
        (((weight.shape[1], lanes), F32), ((27 * chans, lanes), BF16)),
        (pooled, weight),
        flops=2 * weight.size * lanes // 3,
    )


def layer5_kernel(
    pooled_ref, first_ref, second_ref, weight_ref, cot_ref, part_ref, _,
    out_ref, grad_ref, stack_ref, spread_ref, to_first_ref, to_second_ref, share_ref,
):
    chans = pooled_ref.shape[0]
    outer = grad_ref.shape[0]
    cells = cot_ref.shape[2]
    rows = len(TAPS) * chans
    below, above = neighbours(first_ref[...], second_ref[...])
    spread_taps((below,), stack_ref.at[pl.ds(0, rows), :], WIDTH // 2, cells, 1)
    spread_taps((above,), stack_ref.at[pl.ds(2 * rows, rows), :], WIDTH // 2, cells, 1)
    preact = part_ref[...]
    preact += convolved5(weight_ref, stack_ref, -1)
    preact += convolved5(weight_ref, stack_ref, 1)
    sig = jax.nn.sigmoid(preact)
    active = preact * sig
    slope = sig * (1.0 + preact * (1.0 - sig))
    for n in range(cot_ref.shape[0]):
        lanes = slice(n * cells, (n + 1) * cells)
        out_ref[n] = active[:, lanes].astype(BF16)
        grad_ref[:, lanes] = (cot_ref[n].astype(F32) * slope[:, lanes]).astype(BF16)
    spread_taps((grad_ref[...],), spread_ref, WIDTH // 2, cells, -1)
    down = inward_part(weight_ref, spread_ref, -1).astype(BF16)
    up = inward_part(weight_ref, spread_ref, 1).astype(BF16)
    odd = lax.axis_index("space") % 2 == 1
    to_first_ref[...] = jnp.where(odd, down, up)
    to_second_ref[...] = jnp.where(odd, up, down)
    core = lax.axis_index("dp") % 2
    half = outer // 2
    share_ref[pl.ds(0, half), :] = grad_ref[pl.ds(pl.multiple_of((1 - core) * half, half), half), :]
    share_ref[pl.ds(half, chans), :] = below
    share_ref[pl.ds(half + chans, chans), :] = pooled_ref[...]
    share_ref[pl.ds(half + 2 * chans, chans), :] = above


def layer5(pooled, first, second, weight, cot, part, stack):
    vols, outer, cells = cot.shape
    chans, lanes = pooled.shape
    return call(
        layer5_kernel,
        "layer5",
        (
            ((vols, outer, cells), BF16),
            ((outer, lanes), BF16),
            (stack.shape, BF16),
            ((len(TAPS) * outer, lanes), BF16),
            ((chans, lanes), BF16),
            ((chans, lanes), BF16),
            ((outer // 2 + 3 * chans, lanes), BF16),
        ),
        (pooled, first, second, weight, cot, part, stack),
        flops=3 * weight.size * lanes,
        aliases={6: 2},
    )


def inward_kernel(weight_ref, spread_ref, inward_ref):
    inward_ref[...] = inward_part(weight_ref, spread_ref, 0)


def own_inward(weight, spread):
    (inward,) = call(
        inward_kernel,
        "own_inward",
        (((weight.shape[2], spread.shape[1]), F32),),
        (weight, spread),
        flops=2 * weight.size * spread.shape[1] // 3,
    )
    return inward


def weight5_kernel(grad_ref, stack_ref, got_ref, part_ref, other_ref):
    core = lax.axis_index("dp") % 2
    half = grad_ref.shape[0] // 2
    chans = stack_ref.shape[0] // 27
    cells = grad_ref.shape[1] // 2
    planes = tuple(got_ref[pl.ds(half + j * chans, chans), :] for j in range(3))
    spread_taps(planes, other_ref, WIDTH // 2, cells, 1)
    mine = grad_ref[pl.ds(pl.multiple_of(core * half, half), half), :]
    theirs = got_ref[pl.ds(0, half), :]
    block = part_ref.shape[1] - 16
    rows = len(TAPS) * chans
    for j in range(3):
        at = pl.ds(j * rows, rows)
        total = dot_rows(stack_ref[at, :], mine) + dot_rows(other_ref[at, :], theirs)
        total = total.astype(BF16)
        for k in range(rows // block):
            part_ref[j * (rows // block) + k, pl.ds(0, block), :] = total[k * block : (k + 1) * block]


def weight5_part(grad, stack, got):
    (part,) = call(
        weight5_kernel,
        "weight5",
        (((64, 80, 128), BF16),),
        (grad, stack, got),
        scratch=[pltpu.VMEM(stack.shape, BF16)],
        flops=2 * grad.size * stack.shape[0],
    )
    return part


def weight4_kernel(
    inward_ref, first_ref, second_ref, stack_ref, slope_ref, keep_ref, send_ref, acc_ref
):
    core = lax.axis_index("dp") % 2
    below, above = neighbours(first_ref[...], second_ref[...])
    inward = (inward_ref[...] + below.astype(F32) + above.astype(F32)).astype(BF16)
    chans = inward.shape[0]
    cells = inward.shape[1] // 2
    unpool = pool_matrix(1, (cells, 4 * cells))
    fine = jnp.concatenate(
        [dot(inward[:, n * cells : (n + 1) * cells], unpool) for n in range(2)], axis=1
    )
    grads = jnp.concatenate(
        [(fine * slope_ref[0]).astype(BF16), (fine * slope_ref[1]).astype(BF16)], axis=0
    )
    rows = stack_ref.shape[0] // 4
    for j in range(4):
        plane = stack_ref[pl.ds(j * rows, rows), :]
        if j == 0:
            acc_ref[pl.ds(0, rows), :] = dot_rows(plane, grads[:chans])
        elif j == 3:
            acc_ref[pl.ds(2 * rows, rows), :] += dot_rows(plane, grads[chans:])
        else:
            both = dot_rows(plane, grads)
            acc_ref[pl.ds(j * rows, rows), :] = both[:, :chans]
            acc_ref[pl.ds((j - 1) * rows, rows), :] += both[:, chans:]
    inner = rows // len(TAPS)
    share = inner // 4
    for o in range(27):
        for k in range(2):
            mine = pl.multiple_of(o * inner + core * 2 * share + k * share, share)
            theirs = pl.multiple_of(o * inner + (1 - core) * 2 * share + k * share, share)
            keep_ref[2 * o + k] = acc_ref[pl.ds(mine, share), :]
            send_ref[2 * o + k] = acc_ref[pl.ds(theirs, share), :].astype(BF16)


def weight4_parts(inward, first, second, stack, slope):
    chans = inward.shape[0]
    return call(
        weight4_kernel,
        "weight4_parts",
        (((54, 16, 128), F32), ((54, 16, 128), BF16)),
        (inward, first, second, stack, slope),
        scratch=[pltpu.VMEM((3 * stack.shape[0] // 4, chans), F32)],
        flops=3 * stack.size * chans,
    )


def pair_kernel(keep_ref, got_ref, _, part_ref):
    filled, rows = keep_ref.shape[:2]
    first = part_ref.shape[1] - rows
    for i in range(filled):
        part_ref[i, pl.ds(first, rows), :] = (keep_ref[i] + got_ref[i].astype(F32)).astype(BF16)
    for i in range(filled, part_ref.shape[0]):
        part_ref[i] = jnp.zeros(part_ref.shape[1:], BF16)


def paired(keep, got, part):
    (part,) = call(pair_kernel, "pairs", ((part.shape, BF16),), (keep, got, part), aliases={2: 0})
    return part


def sum_kernel(parts_ref, rows4_ref, rows5_ref):
    def step(i, acc):
        return acc + parts_ref[i].astype(F32)

    total = lax.fori_loop(1, parts_ref.shape[0], step, parts_ref[0].astype(F32), unroll=9)
    rows5_ref[...] = total[:64].astype(BF16)
    rows4_ref[...] = total[64:].astype(BF16)


def summed(parts):
    return call(sum_kernel, "sums", (((16, 128), BF16), ((64, 128), BF16)), (parts,))


def finish_kernel(mine_ref, theirs_ref, weight4_ref, weight5_ref):
    core = lax.axis_index("dp") % 2
    upper = lax.axis_index("space") // 16
    for o in range(27):
        for side, ref in ((core, mine_ref), (1 - core, theirs_ref)):
            for k in range(2):
                at = pl.multiple_of(side * 32 + k * 16, 16)
                weight4_ref[o, pl.ds(at, 16), :] = ref[2 * o + k].astype(F32)[:16]
            at = pl.multiple_of(side * 128, 128)
            weight5_ref[o, :, pl.ds(at, 128)] = ref[2 * o + upper].astype(F32)[16:20]


def finished(mine, theirs):
    weight4, weight5 = pl.pallas_call(
        finish_kernel,
        out_shape=(
            jax.ShapeDtypeStruct((27, 64, 128), F32),
            jax.ShapeDtypeStruct((27, 4, 256), F32),
        ),
        in_specs=[VMEM] * 2,
        out_specs=(VMEM, VMEM),
        name="finish",
    )(*[pltpu.with_memory_space_constraint(x, pltpu.VMEM) for x in (mine, theirs)])
    return weight4.transpose(0, 2, 1), weight5.transpose(0, 2, 1)


def per_device(volumes, cotangent, conv4_weight, conv5_weight):
    odd = lax.axis_index("space") % 2
    first4 = swapped(lax.dynamic_index_in_dim(volumes, 1 - odd, 0, keepdims=False), 0)
    second4 = swapped(lax.dynamic_index_in_dim(volumes, odd, 0, keepdims=False), 1)
    arranged4 = conv4_weight.transpose(1, 0, 2).reshape(conv4_weight.shape[1], -1)
    part4, stack4 = own4(volumes, arranged4)
    pooled, slope, stack4 = layer4(first4, second4, arranged4, part4, stack4)
    part5, stack5 = own5(pooled, conv5_weight)
    output5, grad, stack5, spread5, to_first, to_second, share = layer5(
        pooled, swapped(pooled, 0), swapped(pooled, 1), conv5_weight, cotangent[0], part5, stack5
    )
    first, second = swapped(to_first, 0), swapped(to_second, 1)
    inward = own_inward(conv5_weight, spread5)
    part = weight5_part(grad, stack5, other_core(share))
    keep, send = weight4_parts(inward, first, second, stack4, slope)
    axes = ("dp", "space")
    spaces, groups = lax.axis_size("space"), lax.axis_size("dp")
    per_core = [
        [dp * spaces + s for dp in range(core, groups, 2) for s in range(spaces)]
        for core in range(2)
    ]

    def exchange(parts):
        return lax.all_to_all(
            parts, axes, split_axis=0, concat_axis=0, tiled=True, axis_index_groups=per_core
        )

    rows4, rows5 = summed(exchange(paired(keep, other_core(send), part)))
    rows5 = jnp.pad(rows5.reshape(spaces // 2, 4, 128), ((0, 0), (0, 4), (0, 0)))
    outgoing = jnp.concatenate(
        [
            jnp.broadcast_to(rows4, (64, 16, 128)),
            jnp.broadcast_to(rows5, (4, spaces // 2, 8, 128)).reshape(64, 8, 128),
        ],
        axis=1,
    )
    mine = exchange(outgoing)
    weight4, weight5 = finished(mine, other_core(mine))
    return (output5[None], weight4, weight5)


def solution(mesh):
    placed = (P("space", "dp", None, None), P("space", "dp", None, None), P(), P())
    return jax.shard_map(
        per_device,
        mesh=mesh,
        in_specs=placed,
        out_specs=(P("space", "dp", None, None), P(), P(None, None, "space")),
        check_vma=False,
    )
```

time: 97.7 us -> 93.1 us (0.953)
  waiting for transfers between devices: 11.8 us -> 4.15 us
  starting transfers between devices: 27.7 us -> 30.8 us
  local copies, waits for them, and re-layouts: 5.87 us -> 3.88 us
  Pallas kernels: 8.03 us -> 9.89 us
    ppermute x6, waiting for transfers between devices: 9.98 us -> 3.45 us  [swapped(): lax.ppermute(values, 'space', swap_pairs(lax.axis_size('space'), phase))]
    ppermute x3, starting transfers between devices: 6.52 us -> 9.53 us  [other_core(): return lax.ppermute(values, 'dp', [(i, i ^ 1) for i in range(count)])]
    convert_element_type x3 -> x0, local copies, waits for them, and re-layouts: 1.95 us -> none  [the longest x1 0.99 us: per_device(): both[:, :, :, :16].transpose(1, 4, 0, 2, 3).reshape(27, 128, 64).astype(F32)]
    ppermute x3, waiting for transfers between devices: 1.8 us -> 0.7 us  [other_core(): return lax.ppermute(values, 'dp', [(i, i ^ 1) for i in range(count)])]
    pallas_call x0 -> x1, Pallas kernels: none -> 1.01 us  [finished(): pl.pallas_call(finish_kernel, out_shape=(jax.ShapeDtypeStruct((27, 64, 12...]
    pallas_call x6 -> x9, Pallas kernels: 8.03 us -> 8.87 us  [call(): pl.pallas_call(kernel, out_shape=tuple((pltpu.VMEM(shape, dtype) for shap...]
  transfers between devices with their start and end apart: 9 -> 9, of which waited for: 7 -> 4; matrix products, arithmetic and copies ran while one was open for 2% -> 2% of each run, Pallas kernels for 2% -> 5%
where the time goes in v3:
time: 93.1 us; the launch traced here: 92.8 us
  blocking collectives  43.2 us (46%)
  starting transfers between devices  30.8 us (33%)
  Pallas kernels  9.89 us (11%)
  waiting for transfers between devices  4.15 us (4%)
  local copies, waits for them, and re-layouts  3.88 us (4%)
    all_to_all x2, blocking collectives, exchange(): lax.all_to_all(parts, axes, split_axis=0, concat_axis=0, tiled=True, axis...  43.2 us
    ppermute x6, starting transfers between devices, swapped(): lax.ppermute(values, 'space', swap_pairs(lax.axis_size('space'), phase))  21.3 us
    ppermute x3, starting transfers between devices, other_core(): return lax.ppermute(values, 'dp', [(i, i ^ 1) for i in range(count)])  9.53 us
    pallas_call x9, Pallas kernels, call(): pl.pallas_call(kernel, out_shape=tuple((pltpu.VMEM(shape, dtype) for shap...  8.87 us
    ppermute x6, waiting for transfers between devices, swapped(): lax.ppermute(values, 'space', swap_pairs(lax.axis_size('space'), phase))  3.45 us
  transfers between devices with their start and end apart: 9, of which 4 were waited for; matrix products, arithmetic and copies ran while one was open for 2% of the time, Pallas kernels for 5%

profile of v3, /device:TPU:1, one launch (start us, length us, event | category | flops | bytes accessed | tf_op | source)
XLA Modules:
  0.0 92.8 jit_solution(10799181328756415762)
XLA Ops:
  0.6 1.0 %dynamic-slice_bitcast_fusion = (bf16[2,64,512]{2,1,0:T(8,128)(2,1)S(1)}, bf16[2,64,512]{2,1,0:T(8,128)(2,1)S(1)}) fusion(bf16[2,2,64,512]{3,2,1,0:T(8,128)(2,1)} %vol_ref.1, s32[]{:T(128)S(6)} %select_n.16, s32[]{:T(128)S(6)} %select_n.15), kind=kLoop, calls=%fused_computation.1 | loop fusion | bytes 524296 | tf_op jit(solution)/shard_map/jit(dynamic_index_in_dim)/squeeze | solution.py:426
  1.6 9.6 %collective-permute-start.1 = (bf16[2,64,512]{2,1,0:T(8,128)(2,1)S(1)}, bf16[2,64,512]{2,1,0:T(8,128)(2,1)S(1)}, u32[]{:S(2)}, u32[]{:S(2)}) collective-permute-start(bf16[2,64,512]{2,1,0:T(8,128)(2,1)S(1)} %get-tuple-element.43), channel_id=1, source_target_pairs={{1,2},{2,1},{3,4},{4,3},{5,6},{6,5},{7,8},{8,7},{9,10},{10,9},{11,... | collective-permute-start | bytes 393224 | tf_op jit(solution)/shard_map/ppermute | solution.py:40
  11.2 1.2 %copy.13.weight_ref = bf16[128,1728]{1,0:T(8,128)(2,1)S(1)} copy(bf16[128,1728]{0,1:T(8,128)(2,1)} %bitcast.17) | data formatting | bytes 884736 | tf_op jit(solution)/shard_map/reshape | solution.py:427
  12.5 0.9 %copy-done.1 = bf16[2,2,64,512]{3,2,1,0:T(8,128)(2,1)S(1)} copy-done((bf16[2,2,64,512]{3,2,1,0:T(8,128)(2,1)S(1)}, bf16[2,2,64,512]{3,2,1,0:T(8,128)(2,1)}, u32[]{:S(2)}) %copy-start.1) | copy-done | bytes 262168
  13.4 1.4 %own4.1 = (f32[2,128,1024]{2,1,0:T(8,128)S(1)}, bf16[2304,1024]{1,0:T(8,128)(2,1)S(1)}) custom-call(bf16[2,2,64,512]{3,2,1,0:T(8,128)(2,1)S(1)} %copy-done.1, bf16[128,1728]{1,0:T(8,128)(2,1)S(1)} %copy.13.weight_ref), custom_call_target="tpu_custom_call" | custom-call | flops 905969664 | bytes 704512 | tf_op jit(solution)/shard_map/own4/pallas_call | solution.py:18
  14.8 0.5 collective-permute-done.first_ref
  15.3 1.7 %layer4.1 = (bf16[128,256]{1,0:T(8,128)(2,1)S(1)}, f32[2,128,1024]{2,1,0:T(8,128)S(1)}, bf16[2304,1024]{1,0:T(8,128)(2,1)S(1)}) custom-call(bf16[2,64,512]{2,1,0:T(8,128)(2,1)S(1)} %collective-permute-done.first_ref, bf16[2,64,512]{2,1,0:T(8,128)(2,1)S(1)} %collective-permute-done.1.second_ref, ...), custom_call_target="tpu_custom_call", output_to_operand_aliasing={{1}: (3, {}), {2}: (4, {})} | custom-call | flops 452984832 | bytes 6471680 | tf_op jit(solution)/shard_map/layer4/pallas_call | solution.py:18
  17.0 6.1 %collective-permute-start.3 = (bf16[128,256]{1,0:T(8,128)(2,1)S(1)}, bf16[128,256]{1,0:T(8,128)(2,1)S(1)}, u32[]{:S(2)}, u32[]{:S(2)}) collective-permute-start(bf16[128,256]{1,0:T(8,128)(2,1)S(1)} %get-tuple-element.25.pooled_ref), channel_id=1, source_target_pairs={{1,2},{2,1},{3,4},{4,3},{5,6},{6,5},{7,8},{8,7},{9,10},{10,9},{11,... | collective-permute-start | bytes 196616 | tf_op jit(solution)/shard_map/ppermute | solution.py:40
  23.1 0.5 own5.1
  23.6 2.3 %collective-permute-done.3.second_ref = bf16[128,256]{1,0:T(8,128)(2,1)S(1)} collective-permute-done((bf16[128,256]{1,0:T(8,128)(2,1)S(1)}, bf16[128,256]{1,0:T(8,128)(2,1)S(1)}, u32[]{:S(2)}, u32[]{:S(2)}) %collective-permute-start.3) | collective-permute-done | bytes 65568 | tf_op jit(solution)/shard_map/ppermute | solution.py:40
  25.9 0.6 collective-permute-done.2.first_ref
  26.5 1.9 %layer5.1 = (bf16[2,256,128]{2,1,0:T(8,128)(2,1)S(1)}, bf16[256,256]{1,0:T(8,128)(2,1)S(1)}, bf16[3456,256]{1,0:T(8,128)(2,1)S(1)}, bf16[2304,256]{1,0:T(8,128)(...) custom-call(bf16[128,256]{1,0:T(8,128)(2,1)S(1)} %get-tuple-element., ...), custom_call_target="tpu_custom_call", output_to_operand_aliasing={{2}: (6, {})} | custom-call | flops 679477248 | bytes 4128768 | tf_op jit(solution)/shard_map/layer5/pallas_call | solution.py:18
  28.5 5.5 %collective-permute-start.5 = (bf16[128,256]{1,0:T(8,128)(2,1)S(1)}, bf16[128,256]{1,0:T(8,128)(2,1)S(1)}, u32[]{:S(2)}, u32[]{:S(2)}) collective-permute-start(bf16[128,256]{1,0:T(8,128)(2,1)S(1)} %get-tuple-element.31), channel_id=1, source_target_pairs={{1,2},{2,1},{3,4},{4,3},{5,6},{6,5},{7,8},{8,7},{9,10},{10,9},{11,... | collective-permute-start | bytes 196616 | tf_op jit(solution)/shard_map/ppermute | solution.py:40
  34.0 3.0 %collective-permute-start.7 = (bf16[512,256]{1,0:T(8,128)(2,1)S(1)}, bf16[512,256]{1,0:T(8,128)(2,1)S(1)}, u32[]{:S(2)}, u32[]{:S(2)}) collective-permute-start(bf16[512,256]{1,0:T(8,128)(2,1)S(1)} %get-tuple-element.38), channel_id=1, source_target_pairs={{0,32},{32,0},{64,96},{96,64},{1,33},{33,1},{65,97},{97,65},{2,34}... | collective-permute-start | bytes 786440 | tf_op jit(solution)/shard_map/ppermute | solution.py:45
  37.0 0.4 own_inward.1.inward_ref
  37.4 1.7 %weight4_parts.1 = (f32[54,16,128]{2,1,0:T(8,128)S(1)}, bf16[54,16,128]{2,1,0:T(8,128)(2,1)S(1)}) custom-call(f32[128,256]{1,0:T(8,128)S(1)} %own_inward.1.inward_ref, bf16[128,256]{1,0:T(8,128)(2,1)S(1)} %collective-permute-done.4.first_ref, bf16[128,256]{1,0:T(8,128)(2,1)S(1)} %collective-permute-done.5.second_ref, ...), custom_call_target="tpu_custom_call" | custom-call | flops 905969664 | bytes 6029312 | tf_op jit(solution)/shard_map/weight4_parts/pallas_call | solution.py:18
  39.1 3.9 %collective-permute-start.6 = (bf16[54,16,128]{2,1,0:T(8,128)(2,1)S(1)}, bf16[54,16,128]{2,1,0:T(8,128)(2,1)S(1)}, u32[]{:S(2)}, u32[]{:S(2)}) collective-permute-start(bf16[54,16,128]{2,1,0:T(8,128)(2,1)S(1)} %get-tuple-element.35), channel_id=1, source_target_pairs={{0,32},{32,0},{64,96},{96,64},{1,33},{33,1},{65,97},{97,65},{2,34}... | collective-permute-start | bytes 663560 | tf_op jit(solution)/shard_map/ppermute | solution.py:45
  43.0 1.1 %weight5.1._ = bf16[64,80,128]{2,1,0:T(8,128)(2,1)S(1)} custom-call(bf16[256,256]{1,0:T(8,128)(2,1)S(1)} %get-tuple-element.36.grad_ref, bf16[3456,256]{1,0:T(8,128)(2,1)S(1)} %get-tuple-element.37.stack_ref, bf16[512,256]{1,0:T(8,128)(2,1)S(1)} %collective-permute-done.7.got_ref), custom_call_target="tpu_custom_call" | custom-call | flops 452984832 | bytes 2162688 | tf_op jit(solution)/shard_map/weight5/pallas_call | solution.py:18
  44.2 27.0 %all_to_all.10.parts_ref = bf16[64,80,128]{2,1,0:T(8,128)(2,1)S(1)} all-to-all(bf16[64,80,128]{2,1,0:T(8,128)(2,1)S(1)} %pairs.1), channel_id=1, replica_groups={{0,1,2,3,4,5,6,7,8,9,10,11,12,13,14,15,16,17,18,19,20,21,22,23,24,25,26..., dimensions={0} | all-to-all | bytes 2621440 | tf_op jit(solution)/shard_map/all_to_all | solution.py:446
  71.6 16.2 %all_to_all.11.mine_ref = bf16[64,24,128]{2,1,0:T(8,128)(2,1)S(1)} all-to-all(bf16[64,24,128]{2,1,0:T(8,128)(2,1)S(1)} %pad_maximum_fusion), channel_id=1, replica_groups={{0,1,2,3,4,5,6,7,8,9,10,11,12,13,14,15,16,17,18,19,20,21,22,23,24,25,26..., dimensions={0} | all-to-all | bytes 786432 | tf_op jit(solution)/shard_map/all_to_all | solution.py:446
  87.8 2.7 %collective-permute-start.8 = (bf16[64,24,128]{2,1,0:T(8,128)(2,1)S(1)}, bf16[64,24,128]{2,1,0:T(8,128)(2,1)S(1)}, u32[]{:S(2)}, u32[]{:S(2)}) collective-permute-start(bf16[64,24,128]{2,1,0:T(8,128)(2,1)S(1)} %all_to_all.11.mine_ref), channel_id=1, source_target_pairs={{0,32},{32,0},{64,96},{96,64},{1,33},{33,1},{65,97},{97,65},{2,34}... | collective-permute-start | bytes 1179656 | tf_op jit(solution)/shard_map/ppermute | solution.py:45
  90.5 0.7 copy.18
  91.1 0.7 collective-permute-done.8.theirs_ref
  91.8 1.0 %finish.1 = (f32[27,64,128]{2,1,0:T(8,128)}, f32[27,4,256]{2,1,0:T(4,128)}) custom-call(bf16[64,24,128]{2,1,0:T(8,128)(2,1)S(1)} %all_to_all.11.mine_ref, bf16[64,24,128]{2,1,0:T(8,128)(2,1)S(1)} %collective-permute-done.8.theirs_ref), custom_call_target="tpu_custom_call" | custom-call | tf_op jit(solution)/shard_map/finish/pallas_call | solution.py:410
  (19 shorter events, 0.5 us)
Async XLA Ops:
  1.6 13.1 %collective-permute-start.1 = (bf16[2,64,512]{2,1,0:T(8,128)(2,1)S(1)}, bf16[2,64,512]{2,1,0:T(8,128)(2,1)S(1)}, u32[]{:S(2)}, u32[]{:S(2)}) collective-permute-start(bf16[2,64,512]{2,1,0:T(8,128)(2,1)S(1)} %get-tuple-element.43), channel_id=1, source_target_pairs={{1,2},{2,1},{3,4},{4,3},{5,6},{6,5},{7,8},{8,7},{9,10},{10,9},{11,... | collective-permute-start | bytes 393224 | tf_op jit(solution)/shard_map/ppermute | solution.py:40
  11.2 4.1 %collective-permute-start = (bf16[2,64,512]{2,1,0:T(8,128)(2,1)S(1)}, bf16[2,64,512]{2,1,0:T(8,128)(2,1)S(1)}, u32[]{:S(2)}, u32[]{:S(2)}) collective-permute-start(bf16[2,64,512]{2,1,0:T(8,128)(2,1)S(1)} %get-tuple-element.44), channel_id=1, source_target_pairs={{0,1},{1,0},{2,3},{3,2},{4,5},{5,4},{6,7},{7,6},{8,9},{9,8},{10,11... | collective-permute-start | bytes 393224 | tf_op jit(solution)/shard_map/ppermute | solution.py:40
  12.4 1.0 %copy-start.1 = (bf16[2,2,64,512]{3,2,1,0:T(8,128)(2,1)S(1)}, bf16[2,2,64,512]{3,2,1,0:T(8,128)(2,1)}, u32[]{:S(2)}) copy-start(bf16[2,2,64,512]{3,2,1,0:T(8,128)(2,1)} %vol_ref.1) | copy-start | bytes 786436
  15.3 7.8 %copy-start = (bf16[27,256,128]{2,1,0:T(8,128)(2,1)S(1)}, bf16[27,256,128]{2,1,0:T(8,128)(2,1)}, u32[]{:S(2)}) copy-start(bf16[27,256,128]{2,1,0:T(8,128)(2,1)} %weight_ref.5) | copy-start | bytes 5308420
  17.0 9.5 %copy-start.2 = (bf16[1,2,256,128]{3,2,1,0:T(8,128)(2,1)S(1)}, bf16[1,2,256,128]{3,2,1,0:T(8,128)(2,1)}, u32[]{:S(2)}) copy-start(bf16[1,2,256,128]{3,2,1,0:T(8,128)(2,1)} %param.5) | copy-start | bytes 393220
  17.0 8.9 %collective-permute-start.3 = (bf16[128,256]{1,0:T(8,128)(2,1)S(1)}, bf16[128,256]{1,0:T(8,128)(2,1)S(1)}, u32[]{:S(2)}, u32[]{:S(2)}) collective-permute-start(bf16[128,256]{1,0:T(8,128)(2,1)S(1)} %get-tuple-element.25.pooled_ref), channel_id=1, source_target_pairs={{1,2},{2,1},{3,4},{4,3},{5,6},{6,5},{7,8},{8,7},{9,10},{10,9},{11,... | collective-permute-start | bytes 196616 | tf_op jit(solution)/shard_map/ppermute | solution.py:40
  23.1 3.4 %collective-permute-start.2 = (bf16[128,256]{1,0:T(8,128)(2,1)S(1)}, bf16[128,256]{1,0:T(8,128)(2,1)S(1)}, u32[]{:S(2)}, u32[]{:S(2)}) collective-permute-start(bf16[128,256]{1,0:T(8,128)(2,1)S(1)} %get-tuple-element.25.pooled_ref), channel_id=1, source_target_pairs={{0,1},{1,0},{2,3},{3,2},{4,5},{5,4},{6,7},{7,6},{8,9},{9,8},{10,11... | collective-permute-start | bytes 196616 | tf_op jit(solution)/shard_map/ppermute | solution.py:40
  28.4 9.0 %collective-permute-start.4 = (bf16[128,256]{1,0:T(8,128)(2,1)S(1)}, bf16[128,256]{1,0:T(8,128)(2,1)S(1)}, u32[]{:S(2)}, u32[]{:S(2)}) collective-permute-start(bf16[128,256]{1,0:T(8,128)(2,1)S(1)} %get-tuple-element.30), channel_id=1, source_target_pairs={{0,1},{1,0},{2,3},{3,2},{4,5},{5,4},{6,7},{7,6},{8,9},{9,8},{10,11... | collective-permute-start | bytes 196616 | tf_op jit(solution)/shard_map/ppermute | solution.py:40
  28.5 8.9 %collective-permute-start.5 = (bf16[128,256]{1,0:T(8,128)(2,1)S(1)}, bf16[128,256]{1,0:T(8,128)(2,1)S(1)}, u32[]{:S(2)}, u32[]{:S(2)}) collective-permute-start(bf16[128,256]{1,0:T(8,128)(2,1)S(1)} %get-tuple-element.31), channel_id=1, source_target_pairs={{1,2},{2,1},{3,4},{4,3},{5,6},{6,5},{7,8},{8,7},{9,10},{10,9},{11,... | collective-permute-start | bytes 196616 | tf_op jit(solution)/shard_map/ppermute | solution.py:40
  34.0 9.0 %collective-permute-start.7 = (bf16[512,256]{1,0:T(8,128)(2,1)S(1)}, bf16[512,256]{1,0:T(8,128)(2,1)S(1)}, u32[]{:S(2)}, u32[]{:S(2)}) collective-permute-start(bf16[512,256]{1,0:T(8,128)(2,1)S(1)} %get-tuple-element.38), channel_id=1, source_target_pairs={{0,32},{32,0},{64,96},{96,64},{1,33},{33,1},{65,97},{97,65},{2,34}... | collective-permute-start | bytes 786440 | tf_op jit(solution)/shard_map/ppermute | solution.py:45
  39.1 5.0 %collective-permute-start.6 = (bf16[54,16,128]{2,1,0:T(8,128)(2,1)S(1)}, bf16[54,16,128]{2,1,0:T(8,128)(2,1)S(1)}, u32[]{:S(2)}, u32[]{:S(2)}) collective-permute-start(bf16[54,16,128]{2,1,0:T(8,128)(2,1)S(1)} %get-tuple-element.35), channel_id=1, source_target_pairs={{0,32},{32,0},{64,96},{96,64},{1,33},{33,1},{65,97},{97,65},{2,34}... | collective-permute-start | bytes 663560 | tf_op jit(solution)/shard_map/ppermute | solution.py:45
  87.8 4.0 %collective-permute-start.8 = (bf16[64,24,128]{2,1,0:T(8,128)(2,1)S(1)}, bf16[64,24,128]{2,1,0:T(8,128)(2,1)S(1)}, u32[]{:S(2)}, u32[]{:S(2)}) collective-permute-start(bf16[64,24,128]{2,1,0:T(8,128)(2,1)S(1)} %all_to_all.11.mine_ref), channel_id=1, source_target_pairs={{0,32},{32,0},{64,96},{96,64},{1,33},{33,1},{65,97},{97,65},{2,34}... | collective-permute-start | bytes 1179656 | tf_op jit(solution)/shard_map/ppermute | solution.py:45

commit v4 on v3

--- a/solution.py
+++ b/solution.py
@@ -43,6 +43,11 @@
 def other_core(values):
     count = lax.axis_size("dp")
     return lax.ppermute(values, "dp", [(i, i ^ 1) for i in range(count)])
+
+
+def other_chip(values):
+    count = lax.axis_size("dp")
+    return lax.ppermute(values, "dp", [(i, i ^ 2) for i in range(count)])
 
 
 def neighbours(first, second):
@@ -187,72 +192,75 @@
 
 def convolved5(weight_ref, stack_ref, a):
     chans = weight_ref.shape[2]
-    first = (a + 1) * len(TAPS)
+    taps = len(TAPS)
+    first = (a + 1) * taps
     total = None
-    for o in range(first, first + len(TAPS), 2):
-        if o + 1 < first + len(TAPS):
-            weight = jnp.concatenate([weight_ref[o], weight_ref[o + 1]], axis=1)
+    for t in range(0, taps, 2):
+        if t + 1 < taps:
+            weight = jnp.concatenate([weight_ref[first + t], weight_ref[first + t + 1]], axis=1)
         else:
-            weight = weight_ref[o]
-        part = dot(weight, stack_ref[pl.ds(o * chans, weight.shape[1]), :])
+            weight = weight_ref[first + t]
+        part = dot(weight, stack_ref[pl.ds(t * chans, weight.shape[1]), :])
         total = part if total is None else total + part
     return total
 
 
 def own5_kernel(pooled_ref, weight_ref, part_ref, stack_ref):
-    rows = len(TAPS) * pooled_ref.shape[0]
     cells = pooled_ref.shape[1] // 2
-    spread_taps((pooled_ref[...],), stack_ref.at[pl.ds(rows, rows), :], WIDTH // 2, cells, 1)
+    spread_taps((pooled_ref[...],), stack_ref, WIDTH // 2, cells, 1)
     part_ref[...] = convolved5(weight_ref, stack_ref, 0)
 
 
 def own5(pooled, weight):
     chans, lanes = pooled.shape
-    return call(
+    (part,) = call(
         own5_kernel,
         "own5",
-        (((weight.shape[1], lanes), F32), ((27 * chans, lanes), BF16)),
+        (((weight.shape[1], lanes), F32),),
         (pooled, weight),
+        scratch=[pltpu.VMEM((len(TAPS) * chans, lanes), BF16)],
         flops=2 * weight.size * lanes // 3,
     )
+    return part
 
 
 def layer5_kernel(
-    pooled_ref, first_ref, second_ref, weight_ref, cot_ref, part_ref, _,
-    out_ref, grad_ref, stack_ref, spread_ref, to_first_ref, to_second_ref, share_ref,
+    pooled_ref, first_ref, second_ref, weight_ref, cot_ref, part_ref,
+    out_ref, spread_ref, to_first_ref, to_second_ref, mine_ref, share_ref, stack_ref,
 ):
     chans = pooled_ref.shape[0]
-    outer = grad_ref.shape[0]
+    outer = part_ref.shape[0]
     cells = cot_ref.shape[2]
-    rows = len(TAPS) * chans
     below, above = neighbours(first_ref[...], second_ref[...])
-    spread_taps((below,), stack_ref.at[pl.ds(0, rows), :], WIDTH // 2, cells, 1)
-    spread_taps((above,), stack_ref.at[pl.ds(2 * rows, rows), :], WIDTH // 2, cells, 1)
     preact = part_ref[...]
-    preact += convolved5(weight_ref, stack_ref, -1)
-    preact += convolved5(weight_ref, stack_ref, 1)
+    spread_taps((below,), stack_ref.at[0], WIDTH // 2, cells, 1)
+    preact += convolved5(weight_ref, stack_ref.at[0], -1)
+    spread_taps((above,), stack_ref.at[1], WIDTH // 2, cells, 1)
+    preact += convolved5(weight_ref, stack_ref.at[1], 1)
     sig = jax.nn.sigmoid(preact)
     active = preact * sig
     slope = sig * (1.0 + preact * (1.0 - sig))
     for n in range(cot_ref.shape[0]):
         lanes = slice(n * cells, (n + 1) * cells)
         out_ref[n] = active[:, lanes].astype(BF16)
-        grad_ref[:, lanes] = (cot_ref[n].astype(F32) * slope[:, lanes]).astype(BF16)
-    spread_taps((grad_ref[...],), spread_ref, WIDTH // 2, cells, -1)
+        grad = (cot_ref[n].astype(F32) * slope[:, lanes]).astype(BF16)
+        mine_ref[pl.ds(0, outer), lanes] = grad
+        share_ref[pl.ds(0, outer), lanes] = grad
+    spread_taps((mine_ref[pl.ds(0, outer), :],), spread_ref, WIDTH // 2, cells, -1)
     down = inward_part(weight_ref, spread_ref, -1).astype(BF16)
     up = inward_part(weight_ref, spread_ref, 1).astype(BF16)
     odd = lax.axis_index("space") % 2 == 1
     to_first_ref[...] = jnp.where(odd, down, up)
     to_second_ref[...] = jnp.where(odd, up, down)
-    core = lax.axis_index("dp") % 2
-    half = outer // 2
-    share_ref[pl.ds(0, half), :] = grad_ref[pl.ds(pl.multiple_of((1 - core) * half, half), half), :]
-    share_ref[pl.ds(half, chans), :] = below
-    share_ref[pl.ds(half + chans, chans), :] = pooled_ref[...]
-    share_ref[pl.ds(half + 2 * chans, chans), :] = above
-
-
-def layer5(pooled, first, second, weight, cot, part, stack):
+    chip = lax.axis_index("dp") // 2
+    half = chans // 2
+    for j, plane in enumerate((below, pooled_ref[...], above)):
+        at = pl.ds(outer + j * half, half)
+        mine_ref[at, :] = jnp.where(chip == 0, plane[:half], plane[half:])
+        share_ref[at, :] = jnp.where(chip == 0, plane[half:], plane[:half])
+
+
+def layer5(pooled, first, second, weight, cot, part):
     vols, outer, cells = cot.shape
     chans, lanes = pooled.shape
     return call(
@@ -260,16 +268,15 @@
         "layer5",
         (
             ((vols, outer, cells), BF16),
-            ((outer, lanes), BF16),
-            (stack.shape, BF16),
             ((len(TAPS) * outer, lanes), BF16),
             ((chans, lanes), BF16),
             ((chans, lanes), BF16),
-            ((outer // 2 + 3 * chans, lanes), BF16),
+            ((outer + 3 * chans // 2, lanes), BF16),
+            ((outer + 3 * chans // 2, lanes), BF16),
         ),
-        (pooled, first, second, weight, cot, part, stack),
+        (pooled, first, second, weight, cot, part),
+        scratch=[pltpu.VMEM((2, len(TAPS) * chans, lanes), BF16)],
         flops=3 * weight.size * lanes,
-        aliases={6: 2},
     )
 
 
@@ -288,33 +295,62 @@
     return inward
 
 
-def weight5_kernel(grad_ref, stack_ref, got_ref, part_ref, other_ref):
+def regroup_kernel(mine_ref, got_ref, send_ref):
     core = lax.axis_index("dp") % 2
-    half = grad_ref.shape[0] // 2
-    chans = stack_ref.shape[0] // 27
-    cells = grad_ref.shape[1] // 2
-    planes = tuple(got_ref[pl.ds(half + j * chans, chans), :] for j in range(3))
-    spread_taps(planes, other_ref, WIDTH // 2, cells, 1)
-    mine = grad_ref[pl.ds(pl.multiple_of(core * half, half), half), :]
-    theirs = got_ref[pl.ds(0, half), :]
-    block = part_ref.shape[1] - 16
-    rows = len(TAPS) * chans
+    rows = send_ref.shape[0] // 2
+    half = mine_ref.shape[0] - rows
+    for i, ref in enumerate((mine_ref, got_ref)):
+        start = pl.multiple_of((1 - core) * half, half)
+        send_ref[pl.ds(i * rows, half), :] = ref[pl.ds(start, half), :]
+        send_ref[pl.ds(i * rows + half, rows - half), :] = ref[pl.ds(2 * half, rows - half), :]
+
+
+def regrouped(mine, got, outer):
+    rows = mine.shape[0] - outer // 2
+    (send,) = call(regroup_kernel, "regroup", (((2 * rows, mine.shape[1]), BF16),), (mine, got))
+    return send
+
+
+def weight5_kernel(mine_ref, chip_ref, core_ref, part_ref, stack_ref, total_ref):
+    core = lax.axis_index("dp") % 2
+    lanes = mine_ref.shape[1]
+    rows = core_ref.shape[0] // 2
+    half = mine_ref.shape[0] - rows
+    own = pl.ds(pl.multiple_of(core * half, half), half)
+    grads = []
+    for i, (ref, at, first) in enumerate((
+        (mine_ref, own, 2 * half),
+        (chip_ref, own, 2 * half),
+        (core_ref, pl.ds(0, half), half),
+        (core_ref, pl.ds(rows, half), rows + half),
+    )):
+        grads.append(ref[at, :])
+        chans = (rows - half) // 3
+        planes = tuple(ref[pl.ds(first + j * chans, chans), :] for j in range(3))
+        spread_taps(planes, stack_ref.at[:, pl.ds(i * lanes, lanes)], WIDTH // 2, lanes // 2, 1)
+    grads = jnp.concatenate(grads, axis=1)
+    block = stack_ref.shape[0] // 3
     for j in range(3):
-        at = pl.ds(j * rows, rows)
-        total = dot_rows(stack_ref[at, :], mine) + dot_rows(other_ref[at, :], theirs)
-        total = total.astype(BF16)
-        for k in range(rows // block):
-            part_ref[j * (rows // block) + k, pl.ds(0, block), :] = total[k * block : (k + 1) * block]
-
-
-def weight5_part(grad, stack, got):
+        at = pl.ds(j * block, block)
+        total_ref[at, :] = dot_rows(stack_ref[at, :], grads)
+    total_ref[pl.ds(3 * block, 8), :] = jnp.zeros((8, half), F32)
+    owners = part_ref.shape[0]
+    for owner in range(owners):
+        part_ref[owner, pl.ds(16, 32), :] = total_ref[
+            pl.ds(owner * (3 * block // owners), 32), :
+        ].astype(BF16)
+
+
+def weight5_part(mine, chip, core, outer):
+    lanes = mine.shape[1]
+    rows = 9 * (mine.shape[0] - outer)
     (part,) = call(
         weight5_kernel,
         "weight5",
-        (((64, 80, 128), BF16),),
-        (grad, stack, got),
-        scratch=[pltpu.VMEM(stack.shape, BF16)],
-        flops=2 * grad.size * stack.shape[0],
+        (((64, 48, 128), BF16),),
+        (mine, chip, core),
+        scratch=[pltpu.VMEM((rows, 4 * lanes), BF16), pltpu.VMEM((rows + 8, outer // 2), F32)],
+        flops=4 * rows * lanes * outer,
     )
     return part
 
@@ -369,11 +405,10 @@
 
 def pair_kernel(keep_ref, got_ref, _, part_ref):
     filled, rows = keep_ref.shape[:2]
-    first = part_ref.shape[1] - rows
     for i in range(filled):
-        part_ref[i, pl.ds(first, rows), :] = (keep_ref[i] + got_ref[i].astype(F32)).astype(BF16)
+        part_ref[i, pl.ds(0, rows), :] = (keep_ref[i] + got_ref[i].astype(F32)).astype(BF16)
     for i in range(filled, part_ref.shape[0]):
-        part_ref[i] = jnp.zeros(part_ref.shape[1:], BF16)
+        part_ref[i, pl.ds(0, rows), :] = jnp.zeros((rows, part_ref.shape[2]), BF16)
 
 
 def paired(keep, got, part):
@@ -385,25 +420,43 @@
     def step(i, acc):
         return acc + parts_ref[i].astype(F32)
 
-    total = lax.fori_loop(1, parts_ref.shape[0], step, parts_ref[0].astype(F32), unroll=9)
-    rows5_ref[...] = total[:64].astype(BF16)
-    rows4_ref[...] = total[64:].astype(BF16)
+    owners = parts_ref.shape[0]
+    sides = [
+        lax.fori_loop(1, owners // 2, lambda i, acc, at=at: step(at + i, acc), parts_ref[at].astype(F32))
+        for at in (0, owners // 2)
+    ]
+    rows4_ref[...] = (sides[0][:16] + sides[1][:16]).astype(BF16)
+    half = rows5_ref.shape[0] // 2
+    owner = lax.axis_index("dp") // 2 * (owners // 2) + lax.axis_index("space")
+    start = owner * (27 * half // owners) % half
+    empty = jnp.zeros((half + 16 - parts_ref.shape[1], parts_ref.shape[2]), F32)
+    for i, side in enumerate(sides):
+        rows5 = jnp.concatenate([side[16:], empty], axis=0)
+        rows5_ref[pl.ds(i * half, half), :] = pltpu.roll(rows5, start, 0).astype(BF16)
 
 
 def summed(parts):
-    return call(sum_kernel, "sums", (((16, 128), BF16), ((64, 128), BF16)), (parts,))
+    return call(sum_kernel, "sums", (((16, 128), BF16), ((128, 128), BF16)), (parts,))
 
 
 def finish_kernel(mine_ref, theirs_ref, weight4_ref, weight5_ref):
     core = lax.axis_index("dp") % 2
-    upper = lax.axis_index("space") // 16
+    first = lax.axis_index("space") % 16 * 4
+    share = 27 * 64 // mine_ref.shape[0]
+    row = lax.broadcasted_iota(jnp.int32, (4, 128), 0)
     for o in range(27):
         for side, ref in ((core, mine_ref), (1 - core, theirs_ref)):
             for k in range(2):
                 at = pl.multiple_of(side * 32 + k * 16, 16)
                 weight4_ref[o, pl.ds(at, 16), :] = ref[2 * o + k].astype(F32)[:16]
+            start = o * 64 + first
+            owner = start // share
+            low = ref[owner].astype(F32)[16:20]
+            high = ref[(start + 3) // share].astype(F32)[16:20]
             at = pl.multiple_of(side * 128, 128)
-            weight5_ref[o, :, pl.ds(at, 128)] = ref[2 * o + upper].astype(F32)[16:20]
+            weight5_ref[o, :, pl.ds(at, 128)] = jnp.where(
+                row < (owner + 1) * share - start, low, high
+            )
 
 
 def finished(mine, theirs):
@@ -427,13 +480,16 @@
     arranged4 = conv4_weight.transpose(1, 0, 2).reshape(conv4_weight.shape[1], -1)
     part4, stack4 = own4(volumes, arranged4)
     pooled, slope, stack4 = layer4(first4, second4, arranged4, part4, stack4)
-    part5, stack5 = own5(pooled, conv5_weight)
-    output5, grad, stack5, spread5, to_first, to_second, share = layer5(
-        pooled, swapped(pooled, 0), swapped(pooled, 1), conv5_weight, cotangent[0], part5, stack5
+    part5 = own5(pooled, conv5_weight)
+    output5, spread5, to_first, to_second, mine5, share5 = layer5(
+        pooled, swapped(pooled, 0), swapped(pooled, 1), conv5_weight, cotangent[0], part5
     )
     first, second = swapped(to_first, 0), swapped(to_second, 1)
     inward = own_inward(conv5_weight, spread5)
-    part = weight5_part(grad, stack5, other_core(share))
+    outer = conv5_weight.shape[1]
+    chip5 = other_chip(share5)
+    core5 = other_core(regrouped(mine5, chip5, outer))
+    part = weight5_part(mine5, chip5, core5, outer)
     keep, send = weight4_parts(inward, first, second, stack4, slope)
     axes = ("dp", "space")
     spaces, groups = lax.axis_size("space"), lax.axis_size("dp")
@@ -448,11 +504,11 @@
         )
 
     rows4, rows5 = summed(exchange(paired(keep, other_core(send), part)))
-    rows5 = jnp.pad(rows5.reshape(spaces // 2, 4, 128), ((0, 0), (0, 4), (0, 0)))
+    rows5 = jnp.pad(rows5.reshape(spaces, 4, 128), ((0, 0), (0, 4), (0, 0)))
     outgoing = jnp.concatenate(
         [
             jnp.broadcast_to(rows4, (64, 16, 128)),
-            jnp.broadcast_to(rows5, (4, spaces // 2, 8, 128)).reshape(64, 8, 128),
+            jnp.broadcast_to(rows5, (2, spaces, 8, 128)).reshape(64, 8, 128),
         ],
         axis=1,
     )

time: 93.1 us -> 89.3 us (0.959)
  blocking collectives: 43.2 us -> 37 us
  starting transfers between devices: 30.8 us -> 32.1 us
    all_to_all x2, blocking collectives: 43.2 us -> 37 us  [exchange(): lax.all_to_all(parts, axes, split_axis=0, concat_axis=0, tiled=True, axis...]
    pallas_call x9 -> x10, Pallas kernels: 8.87 us -> 9.57 us  [call(): pl.pallas_call(kernel, out_shape=tuple((pltpu.VMEM(shape, dtype) for shap...]
  transfers between devices with their start and end apart: 9 -> 10, of which waited for: 4 -> 5; matrix products, arithmetic and copies ran while one was open for 2% -> 2% of each run, Pallas kernels for 5% -> 6%
where the time goes in v4:
time: 89.3 us; the launch traced here: 89.1 us
  blocking collectives  37 us (41%)
  starting transfers between devices  32.1 us (36%)
  Pallas kernels  10.8 us (12%)
  waiting for transfers between devices  4.44 us (5%)
  local copies, waits for them, and re-layouts  3.88 us (4%)
    all_to_all x2, blocking collectives, exchange(): lax.all_to_all(parts, axes, split_axis=0, concat_axis=0, tiled=True, axis...  37 us
    ppermute x6, starting transfers between devices, swapped(): lax.ppermute(values, 'space', swap_pairs(lax.axis_size('space'), phase))  21.7 us
    ppermute x3, starting transfers between devices, other_core(): return lax.ppermute(values, 'dp', [(i, i ^ 1) for i in range(count)])  9.97 us
    pallas_call x10, Pallas kernels, call(): pl.pallas_call(kernel, out_shape=tuple((pltpu.VMEM(shape, dtype) for shap...  9.57 us
    ppermute x6, waiting for transfers between devices, swapped(): lax.ppermute(values, 'space', swap_pairs(lax.axis_size('space'), phase))  3.74 us
  transfers between devices with their start and end apart: 10, of which 5 were waited for; matrix products, arithmetic and copies ran while one was open for 2% of the time, Pallas kernels for 6%

profile of v4, /device:TPU:1, one launch (start us, length us, event | category | flops | bytes accessed | tf_op | source)
XLA Modules:
  0.0 89.1 jit_solution(5221052394837069985)
XLA Ops:
  0.6 1.0 %dynamic-slice_bitcast_fusion = (bf16[2,64,512]{2,1,0:T(8,128)(2,1)S(1)}, bf16[2,64,512]{2,1,0:T(8,128)(2,1)S(1)}) fusion(bf16[2,2,64,512]{3,2,1,0:T(8,128)(2,1)} %vol_ref.1, s32[]{:T(128)S(6)} %select_n.16, s32[]{:T(128)S(6)} %select_n.15), kind=kLoop, calls=%fused_computation.1 | loop fusion | bytes 524296 | tf_op jit(solution)/shard_map/jit(dynamic_index_in_dim)/squeeze | solution.py:479
  1.6 9.6 %collective-permute-start.1 = (bf16[2,64,512]{2,1,0:T(8,128)(2,1)S(1)}, bf16[2,64,512]{2,1,0:T(8,128)(2,1)S(1)}, u32[]{:S(2)}, u32[]{:S(2)}) collective-permute-start(bf16[2,64,512]{2,1,0:T(8,128)(2,1)S(1)} %get-tuple-element.37), channel_id=1, source_target_pairs={{1,2},{2,1},{3,4},{4,3},{5,6},{6,5},{7,8},{8,7},{9,10},{10,9},{11,... | collective-permute-start | bytes 393224 | tf_op jit(solution)/shard_map/ppermute | solution.py:40
  11.2 1.2 %copy.12.weight_ref = bf16[128,1728]{1,0:T(8,128)(2,1)S(1)} copy(bf16[128,1728]{0,1:T(8,128)(2,1)} %bitcast.17) | data formatting | bytes 884736 | tf_op jit(solution)/shard_map/reshape | solution.py:480
  12.5 0.9 %copy-done.1 = bf16[2,2,64,512]{3,2,1,0:T(8,128)(2,1)S(1)} copy-done((bf16[2,2,64,512]{3,2,1,0:T(8,128)(2,1)S(1)}, bf16[2,2,64,512]{3,2,1,0:T(8,128)(2,1)}, u32[]{:S(2)}) %copy-start.1) | copy-done | bytes 262168
  13.4 1.4 %own4.1 = (f32[2,128,1024]{2,1,0:T(8,128)S(1)}, bf16[2304,1024]{1,0:T(8,128)(2,1)S(1)}) custom-call(bf16[2,2,64,512]{3,2,1,0:T(8,128)(2,1)S(1)} %copy-done.1, bf16[128,1728]{1,0:T(8,128)(2,1)S(1)} %copy.12.weight_ref), custom_call_target="tpu_custom_call" | custom-call | flops 905969664 | bytes 704512 | tf_op jit(solution)/shard_map/own4/pallas_call | solution.py:18
  14.8 0.5 collective-permute-done.first_ref
  15.3 1.7 %layer4.1 = (bf16[128,256]{1,0:T(8,128)(2,1)S(1)}, f32[2,128,1024]{2,1,0:T(8,128)S(1)}, bf16[2304,1024]{1,0:T(8,128)(2,1)S(1)}) custom-call(bf16[2,64,512]{2,1,0:T(8,128)(2,1)S(1)} %collective-permute-done.first_ref, bf16[2,64,512]{2,1,0:T(8,128)(2,1)S(1)} %collective-permute-done.1.second_ref, ...), custom_call_target="tpu_custom_call", output_to_operand_aliasing={{1}: (3, {}), {2}: (4, {})} | custom-call | flops 452984832 | bytes 6471680 | tf_op jit(solution)/shard_map/layer4/pallas_call | solution.py:18
  16.9 6.1 %collective-permute-start.3 = (bf16[128,256]{1,0:T(8,128)(2,1)S(1)}, bf16[128,256]{1,0:T(8,128)(2,1)S(1)}, u32[]{:S(2)}, u32[]{:S(2)}) collective-permute-start(bf16[128,256]{1,0:T(8,128)(2,1)S(1)} %get-tuple-element.22.pooled_ref), channel_id=1, source_target_pairs={{1,2},{2,1},{3,4},{4,3},{5,6},{6,5},{7,8},{8,7},{9,10},{10,9},{11,... | collective-permute-start | bytes 196616 | tf_op jit(solution)/shard_map/ppermute | solution.py:40
  23.1 0.5 own5.1.part_ref
  23.6 2.3 %collective-permute-done.3.second_ref = bf16[128,256]{1,0:T(8,128)(2,1)S(1)} collective-permute-done((bf16[128,256]{1,0:T(8,128)(2,1)S(1)}, bf16[128,256]{1,0:T(8,128)(2,1)S(1)}, u32[]{:S(2)}, u32[]{:S(2)}) %collective-permute-start.3) | collective-permute-done | bytes 65568 | tf_op jit(solution)/shard_map/ppermute | solution.py:40
  25.9 0.6 collective-permute-done.2.first_ref
  26.5 1.9 %layer5.1 = (bf16[2,256,128]{2,1,0:T(8,128)(2,1)S(1)}, bf16[2304,256]{1,0:T(8,128)(2,1)S(1)}, bf16[128,256]{1,0:T(8,128)(2,1)S(1)}, bf16[128,256]{1,0:T(8,128)(2...) custom-call(bf16[128,256]{1,0:T(8,128)(2,1)S(1)} %get-tuple-element.22.pooled_ref, ...), custom_call_target="tpu_custom_call" | custom-call | flops 679477248 | bytes 2359296 | tf_op jit(solution)/shard_map/layer5/pallas_call | solution.py:18
  28.8 6.0 %collective-permute-start.5 = (bf16[128,256]{1,0:T(8,128)(2,1)S(1)}, bf16[128,256]{1,0:T(8,128)(2,1)S(1)}, u32[]{:S(2)}, u32[]{:S(2)}) collective-permute-start(bf16[128,256]{1,0:T(8,128)(2,1)S(1)} %get-tuple-element.26), channel_id=1, source_target_pairs={{1,2},{2,1},{3,4},{4,3},{5,6},{6,5},{7,8},{8,7},{9,10},{10,9},{11,... | collective-permute-start | bytes 196616 | tf_op jit(solution)/shard_map/ppermute | solution.py:40
  34.8 3.3 %collective-permute-start.8 = (bf16[640,256]{1,0:T(8,128)(2,1)S(1)}, bf16[640,256]{1,0:T(8,128)(2,1)S(1)}, u32[]{:S(2)}, u32[]{:S(2)}) collective-permute-start(bf16[640,256]{1,0:T(8,128)(2,1)S(1)} %regroup.1), channel_id=1, source_target_pairs={{0,32},{32,0},{64,96},{96,64},{1,33},{33,1},{65,97},{97,65},{2,34}... | collective-permute-start | bytes 983048 | tf_op jit(solution)/shard_map/ppermute | solution.py:45
  38.9 1.7 %weight4_parts.1 = (f32[54,16,128]{2,1,0:T(8,128)S(1)}, bf16[54,16,128]{2,1,0:T(8,128)(2,1)S(1)}) custom-call(f32[128,256]{1,0:T(8,128)S(1)} %own_inward.1.inward_ref, bf16[128,256]{1,0:T(8,128)(2,1)S(1)} %collective-permute-done.4.first_ref, bf16[128,256]{1,0:T(8,128)(2,1)S(1)} %collective-permute-done.5.second_ref, ...), custom_call_target="tpu_custom_call" | custom-call | flops 905969664 | bytes 6029312 | tf_op jit(solution)/shard_map/weight4_parts/pallas_call | solution.py:18
  40.6 3.9 %collective-permute-start.6 = (bf16[54,16,128]{2,1,0:T(8,128)(2,1)S(1)}, bf16[54,16,128]{2,1,0:T(8,128)(2,1)S(1)}, u32[]{:S(2)}, u32[]{:S(2)}) collective-permute-start(bf16[54,16,128]{2,1,0:T(8,128)(2,1)S(1)} %get-tuple-element.30), channel_id=1, source_target_pairs={{0,32},{32,0},{64,96},{96,64},{1,33},{33,1},{65,97},{97,65},{2,34}... | collective-permute-start | bytes 663560 | tf_op jit(solution)/shard_map/ppermute | solution.py:45
  44.5 1.6 %weight5.1._ = bf16[64,48,128]{2,1,0:T(8,128)(2,1)S(1)} custom-call(bf16[448,256]{1,0:T(8,128)(2,1)S(1)} %get-tuple-element.31.mine_ref, bf16[448,256]{1,0:T(8,128)(2,1)S(1)} %collective-permute-done.7.got_ref.chip_ref, bf16[640,256]{1,0:T(8,128)(2,1)S(1)} %collective-permute-done.8.core_ref), custom_call_target="tpu_custom_call" | custom-call | flops 452984832 | bytes 786432 | tf_op jit(solution)/shard_map/weight5/pallas_call | solution.py:18
  46.2 21.4 %all_to_all.10.parts_ref = bf16[64,48,128]{2,1,0:T(8,128)(2,1)S(1)} all-to-all(bf16[64,48,128]{2,1,0:T(8,128)(2,1)S(1)} %pairs.1), channel_id=1, replica_groups={{0,1,2,3,4,5,6,7,8,9,10,11,12,13,14,15,16,17,18,19,20,21,22,23,24,25,26..., dimensions={0} | all-to-all | bytes 1572864 | tf_op jit(solution)/shard_map/all_to_all | solution.py:502
  67.6 0.4 sums.1
  68.1 15.6 %all_to_all.11.mine_ref = bf16[64,24,128]{2,1,0:T(8,128)(2,1)S(1)} all-to-all(bf16[64,24,128]{2,1,0:T(8,128)(2,1)S(1)} %pad_maximum_fusion), channel_id=1, replica_groups={{0,1,2,3,4,5,6,7,8,9,10,11,12,13,14,15,16,17,18,19,20,21,22,23,24,25,26..., dimensions={0} | all-to-all | bytes 786432 | tf_op jit(solution)/shard_map/all_to_all | solution.py:502
  83.8 2.7 %collective-permute-start.9 = (bf16[64,24,128]{2,1,0:T(8,128)(2,1)S(1)}, bf16[64,24,128]{2,1,0:T(8,128)(2,1)S(1)}, u32[]{:S(2)}, u32[]{:S(2)}) collective-permute-start(bf16[64,24,128]{2,1,0:T(8,128)(2,1)S(1)} %all_to_all.11.mine_ref), channel_id=1, source_target_pairs={{0,32},{32,0},{64,96},{96,64},{1,33},{33,1},{65,97},{97,65},{2,34}... | collective-permute-start | bytes 1179656 | tf_op jit(solution)/shard_map/ppermute | solution.py:45
  86.5 0.7 copy.16
  87.1 0.7 collective-permute-done.9.theirs_ref
  87.8 1.3 %finish.1 = (f32[27,64,128]{2,1,0:T(8,128)}, f32[27,4,256]{2,1,0:T(4,128)}) custom-call(bf16[64,24,128]{2,1,0:T(8,128)(2,1)S(1)} %all_to_all.11.mine_ref, bf16[64,24,128]{2,1,0:T(8,128)(2,1)S(1)} %collective-permute-done.9.theirs_ref), custom_call_target="tpu_custom_call" | custom-call | tf_op jit(solution)/shard_map/finish/pallas_call | solution.py:463
  (22 shorter events, 1.3 us)
Async XLA Ops:
  1.6 13.2 %collective-permute-start.1 = (bf16[2,64,512]{2,1,0:T(8,128)(2,1)S(1)}, bf16[2,64,512]{2,1,0:T(8,128)(2,1)S(1)}, u32[]{:S(2)}, u32[]{:S(2)}) collective-permute-start(bf16[2,64,512]{2,1,0:T(8,128)(2,1)S(1)} %get-tuple-element.37), channel_id=1, source_target_pairs={{1,2},{2,1},{3,4},{4,3},{5,6},{6,5},{7,8},{8,7},{9,10},{10,9},{11,... | collective-permute-start | bytes 393224 | tf_op jit(solution)/shard_map/ppermute | solution.py:40
  11.2 4.1 %collective-permute-start = (bf16[2,64,512]{2,1,0:T(8,128)(2,1)S(1)}, bf16[2,64,512]{2,1,0:T(8,128)(2,1)S(1)}, u32[]{:S(2)}, u32[]{:S(2)}) collective-permute-start(bf16[2,64,512]{2,1,0:T(8,128)(2,1)S(1)} %get-tuple-element.38), channel_id=1, source_target_pairs={{0,1},{1,0},{2,3},{3,2},{4,5},{5,4},{6,7},{7,6},{8,9},{9,8},{10,11... | collective-permute-start | bytes 393224 | tf_op jit(solution)/shard_map/ppermute | solution.py:40
  12.4 1.0 %copy-start.1 = (bf16[2,2,64,512]{3,2,1,0:T(8,128)(2,1)S(1)}, bf16[2,2,64,512]{3,2,1,0:T(8,128)(2,1)}, u32[]{:S(2)}) copy-start(bf16[2,2,64,512]{3,2,1,0:T(8,128)(2,1)} %vol_ref.1) | copy-start | bytes 786436
  13.4 9.7 %copy-start = (bf16[27,256,128]{2,1,0:T(8,128)(2,1)S(1)}, bf16[27,256,128]{2,1,0:T(8,128)(2,1)}, u32[]{:S(2)}) copy-start(bf16[27,256,128]{2,1,0:T(8,128)(2,1)} %weight_ref.5) | copy-start | bytes 5308420
  14.8 11.7 %copy-start.2 = (bf16[1,2,256,128]{3,2,1,0:T(8,128)(2,1)S(1)}, bf16[1,2,256,128]{3,2,1,0:T(8,128)(2,1)}, u32[]{:S(2)}) copy-start(bf16[1,2,256,128]{3,2,1,0:T(8,128)(2,1)} %param.5) | copy-start | bytes 393220
  16.9 8.9 %collective-permute-start.3 = (bf16[128,256]{1,0:T(8,128)(2,1)S(1)}, bf16[128,256]{1,0:T(8,128)(2,1)S(1)}, u32[]{:S(2)}, u32[]{:S(2)}) collective-permute-start(bf16[128,256]{1,0:T(8,128)(2,1)S(1)} %get-tuple-element.22.pooled_ref), channel_id=1, source_target_pairs={{1,2},{2,1},{3,4},{4,3},{5,6},{6,5},{7,8},{8,7},{9,10},{10,9},{11,... | collective-permute-start | bytes 196616 | tf_op jit(solution)/shard_map/ppermute | solution.py:40
  23.1 3.4 %collective-permute-start.2 = (bf16[128,256]{1,0:T(8,128)(2,1)S(1)}, bf16[128,256]{1,0:T(8,128)(2,1)S(1)}, u32[]{:S(2)}, u32[]{:S(2)}) collective-permute-start(bf16[128,256]{1,0:T(8,128)(2,1)S(1)} %get-tuple-element.22.pooled_ref), channel_id=1, source_target_pairs={{0,1},{1,0},{2,3},{3,2},{4,5},{5,4},{6,7},{7,6},{8,9},{9,8},{10,11... | collective-permute-start | bytes 196616 | tf_op jit(solution)/shard_map/ppermute | solution.py:40
  28.4 6.4 %collective-permute-start.7 = (bf16[448,256]{1,0:T(8,128)(2,1)S(1)}, bf16[448,256]{1,0:T(8,128)(2,1)S(1)}, u32[]{:S(2)}, u32[]{:S(2)}) collective-permute-start(bf16[448,256]{1,0:T(8,128)(2,1)S(1)} %get-tuple-element.32), channel_id=1, source_target_pairs={{0,64},{32,96},{64,0},{96,32},{1,65},{33,97},{65,1},{97,33},{2,66}... | collective-permute-start | bytes 688136 | tf_op jit(solution)/shard_map/ppermute | solution.py:50
  28.8 9.8 %collective-permute-start.4 = (bf16[128,256]{1,0:T(8,128)(2,1)S(1)}, bf16[128,256]{1,0:T(8,128)(2,1)S(1)}, u32[]{:S(2)}, u32[]{:S(2)}) collective-permute-start(bf16[128,256]{1,0:T(8,128)(2,1)S(1)} %get-tuple-element.25), channel_id=1, source_target_pairs={{0,1},{1,0},{2,3},{3,2},{4,5},{5,4},{6,7},{7,6},{8,9},{9,8},{10,11... | collective-permute-start | bytes 196616 | tf_op jit(solution)/shard_map/ppermute | solution.py:40
  28.8 10.1 %collective-permute-start.5 = (bf16[128,256]{1,0:T(8,128)(2,1)S(1)}, bf16[128,256]{1,0:T(8,128)(2,1)S(1)}, u32[]{:S(2)}, u32[]{:S(2)}) collective-permute-start(bf16[128,256]{1,0:T(8,128)(2,1)S(1)} %get-tuple-element.26), channel_id=1, source_target_pairs={{1,2},{2,1},{3,4},{4,3},{5,6},{6,5},{7,8},{8,7},{9,10},{10,9},{11,... | collective-permute-start | bytes 196616 | tf_op jit(solution)/shard_map/ppermute | solution.py:40
  34.8 9.7 %collective-permute-start.8 = (bf16[640,256]{1,0:T(8,128)(2,1)S(1)}, bf16[640,256]{1,0:T(8,128)(2,1)S(1)}, u32[]{:S(2)}, u32[]{:S(2)}) collective-permute-start(bf16[640,256]{1,0:T(8,128)(2,1)S(1)} %regroup.1), channel_id=1, source_target_pairs={{0,32},{32,0},{64,96},{96,64},{1,33},{33,1},{65,97},{97,65},{2,34}... | collective-permute-start | bytes 983048 | tf_op jit(solution)/shard_map/ppermute | solution.py:45
  40.6 5.6 %collective-permute-start.6 = (bf16[54,16,128]{2,1,0:T(8,128)(2,1)S(1)}, bf16[54,16,128]{2,1,0:T(8,128)(2,1)S(1)}, u32[]{:S(2)}, u32[]{:S(2)}) collective-permute-start(bf16[54,16,128]{2,1,0:T(8,128)(2,1)S(1)} %get-tuple-element.30), channel_id=1, source_target_pairs={{0,32},{32,0},{64,96},{96,64},{1,33},{33,1},{65,97},{97,65},{2,34}... | collective-permute-start | bytes 663560 | tf_op jit(solution)/shard_map/ppermute | solution.py:45
  83.8 4.1 %collective-permute-start.9 = (bf16[64,24,128]{2,1,0:T(8,128)(2,1)S(1)}, bf16[64,24,128]{2,1,0:T(8,128)(2,1)S(1)}, u32[]{:S(2)}, u32[]{:S(2)}) collective-permute-start(bf16[64,24,128]{2,1,0:T(8,128)(2,1)S(1)} %all_to_all.11.mine_ref), channel_id=1, source_target_pairs={{0,32},{32,0},{64,96},{96,64},{1,33},{33,1},{65,97},{97,65},{2,34}... | collective-permute-start | bytes 1179656 | tf_op jit(solution)/shard_map/ppermute | solution.py:45

commit v5 on v4

--- a/solution.py
+++ b/solution.py
@@ -28,16 +28,21 @@
     )(*[pltpu.with_memory_space_constraint(x, pltpu.VMEM) for x in operands])
 
 
-def swap_pairs(count, phase):
+def swap_pairs(groups, count, phase):
     pairs = []
-    for low in range(phase, count, 2):
-        high = (low + 1) % count
-        pairs += [(low, high), (high, low)]
+    for group in range(groups):
+        for here in range(count):
+            there = here + 1 if here % 2 == phase else here - 1
+            if 0 <= there < count:
+                pairs.append((group * count + here, group * count + there))
+            else:
+                pairs.append((group * count + here, (group ^ 1) * count + here))
     return pairs
 
 
 def swapped(values, phase):
-    return lax.ppermute(values, "space", swap_pairs(lax.axis_size("space"), phase))
+    pairs = swap_pairs(lax.axis_size("dp"), lax.axis_size("space"), phase)
+    return lax.ppermute(values, ("dp", "space"), pairs)
 
 
 def other_core(values):
@@ -65,7 +70,7 @@
     column = lane % row_len + e
     row = lane // row_len + b
     inside = (column >= 0) & (column < row_len) & (row >= 0) & (row < length // row_len)
-    return inside.astype(F32)
+    return inside.astype(F32).astype(BF16)
 
 
 def tap(values, b, e, row_len):
@@ -93,11 +98,10 @@
 
 def stack_plane(plane, out_ref, j, n):
     chans, cells = plane.shape
-    wide = plane.astype(F32)
     for t, (b, e) in enumerate(TAPS):
         out_ref[pl.ds((j * len(TAPS) + t) * chans, chans), pl.ds(n * cells, cells)] = tap(
-            wide, b, e, WIDTH
-        ).astype(BF16)
+            plane, b, e, WIDTH
+        )
 
 
 def own4_kernel(vol_ref, weight_ref, part_ref, stack_ref):
@@ -169,86 +173,82 @@
     chans = planes[0].shape[0]
     for j, plane in enumerate(planes):
         for n in range(plane.shape[1] // cells):
-            wide = plane[:, n * cells : (n + 1) * cells].astype(F32)
+            part = plane[:, n * cells : (n + 1) * cells]
             for t, (b, e) in enumerate(TAPS):
                 out_ref[pl.ds((j * len(TAPS) + t) * chans, chans), pl.ds(n * cells, cells)] = tap(
-                    wide, sign * b, sign * e, row_len
-                ).astype(BF16)
-
-
-def inward_part(weight_ref, spread_ref, a):
-    outer = weight_ref.shape[1]
+                    part, sign * b, sign * e, row_len
+                )
+
+
+def tapped(plane, row_len, cells, b, e):
+    parts = [
+        tap(plane[:, at : at + cells], b, e, row_len) for at in range(0, plane.shape[1], cells)
+    ]
+    return jnp.concatenate(parts, axis=1)
+
+
+def convolved5(weight_ref, plane, cells, a):
+    first = (a + 1) * len(TAPS)
     total = None
-    for t in range(len(TAPS)):
-        part = lax.dot_general(
-            weight_ref[(a + 1) * len(TAPS) + t],
-            spread_ref[pl.ds(t * outer, outer), :],
-            (((0,), (0,)), ((), ())),
-            preferred_element_type=F32,
+    for t in range(0, len(TAPS), 2):
+        group = range(t, min(t + 2, len(TAPS)))
+        weight = jnp.concatenate([weight_ref[first + i] for i in group], axis=1)
+        shifts = jnp.concatenate(
+            [tapped(plane, WIDTH // 2, cells, *TAPS[i]) for i in group], axis=0
         )
+        part = dot(weight, shifts)
         total = part if total is None else total + part
     return total
 
 
-def convolved5(weight_ref, stack_ref, a):
-    chans = weight_ref.shape[2]
-    taps = len(TAPS)
-    first = (a + 1) * taps
-    total = None
-    for t in range(0, taps, 2):
-        if t + 1 < taps:
-            weight = jnp.concatenate([weight_ref[first + t], weight_ref[first + t + 1]], axis=1)
-        else:
-            weight = weight_ref[first + t]
-        part = dot(weight, stack_ref[pl.ds(t * chans, weight.shape[1]), :])
-        total = part if total is None else total + part
-    return total
-
-
-def own5_kernel(pooled_ref, weight_ref, part_ref, stack_ref):
+def own5_kernel(pooled_ref, weight_ref, part_ref, back_ref):
+    chans = pooled_ref.shape[0]
     cells = pooled_ref.shape[1] // 2
-    spread_taps((pooled_ref[...],), stack_ref, WIDTH // 2, cells, 1)
-    part_ref[...] = convolved5(weight_ref, stack_ref, 0)
+    part_ref[...] = convolved5(weight_ref, pooled_ref[...], cells, 0)
+    for o in range(27):
+        a, t = divmod(o, len(TAPS))
+        back_ref[t, pl.ds(a * chans, chans), :] = weight_ref[o].T
 
 
 def own5(pooled, weight):
     chans, lanes = pooled.shape
-    (part,) = call(
+    outer = weight.shape[1]
+    return call(
         own5_kernel,
         "own5",
-        (((weight.shape[1], lanes), F32),),
+        (((outer, lanes), F32), ((len(TAPS), 3 * chans, outer), BF16)),
         (pooled, weight),
-        scratch=[pltpu.VMEM((len(TAPS) * chans, lanes), BF16)],
         flops=2 * weight.size * lanes // 3,
     )
-    return part
 
 
 def layer5_kernel(
-    pooled_ref, first_ref, second_ref, weight_ref, cot_ref, part_ref,
-    out_ref, spread_ref, to_first_ref, to_second_ref, mine_ref, share_ref, stack_ref,
+    pooled_ref, first_ref, second_ref, weight_ref, cot_ref, part_ref, back_ref,
+    out_ref, inward_ref, to_first_ref, to_second_ref, mine_ref, share_ref,
 ):
     chans = pooled_ref.shape[0]
     outer = part_ref.shape[0]
     cells = cot_ref.shape[2]
     below, above = neighbours(first_ref[...], second_ref[...])
-    preact = part_ref[...]
-    spread_taps((below,), stack_ref.at[0], WIDTH // 2, cells, 1)
-    preact += convolved5(weight_ref, stack_ref.at[0], -1)
-    spread_taps((above,), stack_ref.at[1], WIDTH // 2, cells, 1)
-    preact += convolved5(weight_ref, stack_ref.at[1], 1)
+    preact = part_ref[...] + convolved5(weight_ref, below, cells, -1)
+    preact += convolved5(weight_ref, above, cells, 1)
     sig = jax.nn.sigmoid(preact)
     active = preact * sig
     slope = sig * (1.0 + preact * (1.0 - sig))
+    grads = []
     for n in range(cot_ref.shape[0]):
         lanes = slice(n * cells, (n + 1) * cells)
         out_ref[n] = active[:, lanes].astype(BF16)
-        grad = (cot_ref[n].astype(F32) * slope[:, lanes]).astype(BF16)
-        mine_ref[pl.ds(0, outer), lanes] = grad
-        share_ref[pl.ds(0, outer), lanes] = grad
-    spread_taps((mine_ref[pl.ds(0, outer), :],), spread_ref, WIDTH // 2, cells, -1)
-    down = inward_part(weight_ref, spread_ref, -1).astype(BF16)
-    up = inward_part(weight_ref, spread_ref, 1).astype(BF16)
+        grads.append((cot_ref[n].astype(F32) * slope[:, lanes]).astype(BF16))
+    grad = jnp.concatenate(grads, axis=1)
+    mine_ref[pl.ds(0, outer), :] = grad
+    share_ref[pl.ds(0, outer), :] = grad
+    inward = None
+    for t, (b, e) in enumerate(TAPS):
+        part = dot(back_ref[t], tapped(grad, WIDTH // 2, cells, -b, -e))
+        inward = part if inward is None else inward + part
+    down, up = inward[:chans].astype(BF16), inward[2 * chans :].astype(BF16)
+    inward_ref[...] = inward[chans : 2 * chans]
     odd = lax.axis_index("space") % 2 == 1
     to_first_ref[...] = jnp.where(odd, down, up)
     to_second_ref[...] = jnp.where(odd, up, down)
@@ -260,7 +260,7 @@
         share_ref[at, :] = jnp.where(chip == 0, plane[half:], plane[:half])
 
 
-def layer5(pooled, first, second, weight, cot, part):
+def layer5(pooled, first, second, weight, cot, part, back):
     vols, outer, cells = cot.shape
     chans, lanes = pooled.shape
     return call(
@@ -268,31 +268,15 @@
         "layer5",
         (
             ((vols, outer, cells), BF16),
-            ((len(TAPS) * outer, lanes), BF16),
+            ((chans, lanes), F32),
             ((chans, lanes), BF16),
             ((chans, lanes), BF16),
             ((outer + 3 * chans // 2, lanes), BF16),
             ((outer + 3 * chans // 2, lanes), BF16),
         ),
-        (pooled, first, second, weight, cot, part),
-        scratch=[pltpu.VMEM((2, len(TAPS) * chans, lanes), BF16)],
+        (pooled, first, second, weight, cot, part, back),
         flops=3 * weight.size * lanes,
     )
-
-
-def inward_kernel(weight_ref, spread_ref, inward_ref):
-    inward_ref[...] = inward_part(weight_ref, spread_ref, 0)
-
-
-def own_inward(weight, spread):
-    (inward,) = call(
-        inward_kernel,
-        "own_inward",
-        (((weight.shape[2], spread.shape[1]), F32),),
-        (weight, spread),
-        flops=2 * weight.size * spread.shape[1] // 3,
-    )
-    return inward
 
 
 def regroup_kernel(mine_ref, got_ref, send_ref):
@@ -370,15 +354,16 @@
     grads = jnp.concatenate(
         [(fine * slope_ref[0]).astype(BF16), (fine * slope_ref[1]).astype(BF16)], axis=0
     )
+    grads = grads.T
     rows = stack_ref.shape[0] // 4
     for j in range(4):
         plane = stack_ref[pl.ds(j * rows, rows), :]
         if j == 0:
-            acc_ref[pl.ds(0, rows), :] = dot_rows(plane, grads[:chans])
+            acc_ref[pl.ds(0, rows), :] = dot(plane, grads[:, :chans])
         elif j == 3:
-            acc_ref[pl.ds(2 * rows, rows), :] += dot_rows(plane, grads[chans:])
+            acc_ref[pl.ds(2 * rows, rows), :] += dot(plane, grads[:, chans:])
         else:
-            both = dot_rows(plane, grads)
+            both = dot(plane, grads)
             acc_ref[pl.ds(j * rows, rows), :] = both[:, :chans]
             acc_ref[pl.ds((j - 1) * rows, rows), :] += both[:, chans:]
     inner = rows // len(TAPS)
@@ -480,12 +465,11 @@
     arranged4 = conv4_weight.transpose(1, 0, 2).reshape(conv4_weight.shape[1], -1)
     part4, stack4 = own4(volumes, arranged4)
     pooled, slope, stack4 = layer4(first4, second4, arranged4, part4, stack4)
-    part5 = own5(pooled, conv5_weight)
-    output5, spread5, to_first, to_second, mine5, share5 = layer5(
-        pooled, swapped(pooled, 0), swapped(pooled, 1), conv5_weight, cotangent[0], part5
+    part5, back5 = own5(pooled, conv5_weight)
+    output5, inward, to_first, to_second, mine5, share5 = layer5(
+        pooled, swapped(pooled, 0), swapped(pooled, 1), conv5_weight, cotangent[0], part5, back5
     )
     first, second = swapped(to_first, 0), swapped(to_second, 1)
-    inward = own_inward(conv5_weight, spread5)
     outer = conv5_weight.shape[1]
     chip5 = other_chip(share5)
     core5 = other_core(regrouped(mine5, chip5, outer))

time: 89.3 us -> 85.1 us (0.953)
  starting transfers between devices: 32.1 us -> 18.6 us
  blocking collectives: 37 us -> 49.6 us
  waiting for transfers between devices: 4.44 us -> 1.79 us
    all_to_all x2, blocking collectives: 37 us -> 49.6 us  [exchange(): lax.all_to_all(parts, axes, split_axis=0, concat_axis=0, tiled=True, axis...]
    ppermute x6, starting transfers between devices: 21.7 us -> 11.5 us  [swapped(): return lax.ppermute(values, ('dp', 'space'), pairs)]
    ppermute x3, starting transfers between devices: 9.97 us -> 6.49 us  [other_core(): return lax.ppermute(values, 'dp', [(i, i ^ 1) for i in range(count)])]
    ppermute x6, waiting for transfers between devices: 3.74 us -> 0.96 us  [swapped(): return lax.ppermute(values, ('dp', 'space'), pairs)]
    pallas_call x10 -> x9, Pallas kernels: 9.57 us -> 8.9 us  [call(): pl.pallas_call(kernel, out_shape=tuple((pltpu.VMEM(shape, dtype) for shap...]
  transfers between devices with their start and end apart: 10 -> 10, of which waited for: 5 -> 3; matrix products, arithmetic and copies ran while one was open for 2% -> 2% of each run, Pallas kernels for 6% -> 6%
where the time goes in v5:
time: 85.1 us; the launch traced here: 84.8 us
  blocking collectives  49.6 us (58%)
  starting transfers between devices  18.6 us (22%)
  Pallas kernels  10.2 us (12%)
  local copies, waits for them, and re-layouts  3.88 us (5%)
  waiting for transfers between devices  1.79 us (2%)
    all_to_all x2, blocking collectives, exchange(): lax.all_to_all(parts, axes, split_axis=0, concat_axis=0, tiled=True, axis...  49.6 us
    ppermute x6, starting transfers between devices, swapped(): return lax.ppermute(values, ('dp', 'space'), pairs)  11.5 us
    pallas_call x9, Pallas kernels, call(): pl.pallas_call(kernel, out_shape=tuple((pltpu.VMEM(shape, dtype) for shap...  8.9 us
    ppermute x3, starting transfers between devices, other_core(): return lax.ppermute(values, 'dp', [(i, i ^ 1) for i in range(count)])  6.49 us
  transfers between devices with their start and end apart: 10, of which 3 were waited for; matrix products, arithmetic and copies ran while one was open for 2% of the time, Pallas kernels for 6%

profile of v5, /device:TPU:1, one launch (start us, length us, event | category | flops | bytes accessed | tf_op | source)
XLA Modules:
  0.0 84.8 jit_solution(2000670112264470403)
XLA Ops:
  0.6 1.0 %dynamic-slice_bitcast_fusion = (bf16[2,64,512]{2,1,0:T(8,128)(2,1)S(1)}, bf16[2,64,512]{2,1,0:T(8,128)(2,1)S(1)}) fusion(bf16[2,2,64,512]{3,2,1,0:T(8,128)(2,1)} %vol_ref.1, s32[]{:T(128)S(6)} %select_n.16, s32[]{:T(128)S(6)} %select_n.15), kind=kLoop, calls=%fused_computation.1 | loop fusion | bytes 524296 | tf_op jit(solution)/shard_map/jit(dynamic_index_in_dim)/squeeze | solution.py:464
  1.6 1.5 %collective-permute-start.1 = (bf16[2,64,512]{2,1,0:T(8,128)(2,1)S(1)}, bf16[2,64,512]{2,1,0:T(8,128)(2,1)S(1)}, u32[]{:S(2)}, u32[]{:S(2)}) collective-permute-start(bf16[2,64,512]{2,1,0:T(8,128)(2,1)S(1)} %get-tuple-element.41), channel_id=1, source_target_pairs={{0,32},{1,2},{2,1},{3,4},{4,3},{5,6},{6,5},{7,8},{8,7},{9,10},{10,... | collective-permute-start | bytes 393224 | tf_op jit(solution)/shard_map/ppermute | solution.py:45
  3.1 2.0 %collective-permute-start = (bf16[2,64,512]{2,1,0:T(8,128)(2,1)S(1)}, bf16[2,64,512]{2,1,0:T(8,128)(2,1)S(1)}, u32[]{:S(2)}, u32[]{:S(2)}) collective-permute-start(bf16[2,64,512]{2,1,0:T(8,128)(2,1)S(1)} %get-tuple-element.42), channel_id=1, source_target_pairs={{0,1},{1,0},{2,3},{3,2},{4,5},{5,4},{6,7},{7,6},{8,9},{9,8},{10,11... | collective-permute-start | bytes 393224 | tf_op jit(solution)/shard_map/ppermute | solution.py:45
  5.1 1.2 %copy.12.weight_ref = bf16[128,1728]{1,0:T(8,128)(2,1)S(1)} copy(bf16[128,1728]{0,1:T(8,128)(2,1)} %bitcast.17) | data formatting | bytes 884736 | tf_op jit(solution)/shard_map/reshape | solution.py:465
  6.4 0.9 %copy-done.1 = bf16[2,2,64,512]{3,2,1,0:T(8,128)(2,1)S(1)} copy-done((bf16[2,2,64,512]{3,2,1,0:T(8,128)(2,1)S(1)}, bf16[2,2,64,512]{3,2,1,0:T(8,128)(2,1)}, u32[]{:S(2)}) %copy-start.1) | copy-done | bytes 262168
  7.3 1.3 %own4.1 = (f32[2,128,1024]{2,1,0:T(8,128)S(1)}, bf16[2304,1024]{1,0:T(8,128)(2,1)S(1)}) custom-call(bf16[2,2,64,512]{3,2,1,0:T(8,128)(2,1)S(1)} %copy-done.1, bf16[128,1728]{1,0:T(8,128)(2,1)S(1)} %copy.12.weight_ref), custom_call_target="tpu_custom_call" | custom-call | flops 905969664 | bytes 704512 | tf_op jit(solution)/shard_map/own4/pallas_call | solution.py:18
  8.6 1.5 %layer4.1 = (bf16[128,256]{1,0:T(8,128)(2,1)S(1)}, f32[2,128,1024]{2,1,0:T(8,128)S(1)}, bf16[2304,1024]{1,0:T(8,128)(2,1)S(1)}) custom-call(bf16[2,64,512]{2,1,0:T(8,128)(2,1)S(1)} %collective-permute-done.first_ref, bf16[2,64,512]{2,1,0:T(8,128)(2,1)S(1)} %collective-permute-done.1.second_ref, ...), custom_call_target="tpu_custom_call", output_to_operand_aliasing={{1}: (3, {}), {2}: (4, {})} | custom-call | flops 452984832 | bytes 6471680 | tf_op jit(solution)/shard_map/layer4/pallas_call | solution.py:18
  10.2 1.3 %collective-permute-start.3 = (bf16[128,256]{1,0:T(8,128)(2,1)S(1)}, bf16[128,256]{1,0:T(8,128)(2,1)S(1)}, u32[]{:S(2)}, u32[]{:S(2)}) collective-permute-start(bf16[128,256]{1,0:T(8,128)(2,1)S(1)} %get-tuple-element.24.pooled_ref), channel_id=1, source_target_pairs={{0,32},{1,2},{2,1},{3,4},{4,3},{5,6},{6,5},{7,8},{8,7},{9,10},{10,... | collective-permute-start | bytes 196616 | tf_op jit(solution)/shard_map/ppermute | solution.py:45
  11.5 2.2 %collective-permute-start.2 = (bf16[128,256]{1,0:T(8,128)(2,1)S(1)}, bf16[128,256]{1,0:T(8,128)(2,1)S(1)}, u32[]{:S(2)}, u32[]{:S(2)}) collective-permute-start(bf16[128,256]{1,0:T(8,128)(2,1)S(1)} %get-tuple-element.24.pooled_ref), channel_id=1, source_target_pairs={{0,1},{1,0},{2,3},{3,2},{4,5},{5,4},{6,7},{7,6},{8,9},{9,8},{10,11... | collective-permute-start | bytes 196616 | tf_op jit(solution)/shard_map/ppermute | solution.py:45
  13.7 0.7 own5.1
  14.4 0.9 %collective-permute-done.2.first_ref = bf16[128,256]{1,0:T(8,128)(2,1)S(1)} collective-permute-done((bf16[128,256]{1,0:T(8,128)(2,1)S(1)}, bf16[128,256]{1,0:T(8,128)(2,1)S(1)}, u32[]{:S(2)}, u32[]{:S(2)}) %collective-permute-start.2) | collective-permute-done | bytes 65568 | tf_op jit(solution)/shard_map/ppermute | solution.py:45
  15.3 1.9 %layer5.1 = (bf16[2,256,128]{2,1,0:T(8,128)(2,1)S(1)}, f32[128,256]{1,0:T(8,128)S(1)}, bf16[128,256]{1,0:T(8,128)(2,1)S(1)}, bf16[128,256]{1,0:T(8,128)(2,1)S(1)...) custom-call(bf16[128,256]{1,0:T(8,128)(2,1)S(1)} %get-tuple-element.24.pooled_ref, ...), custom_call_target="tpu_custom_call" | custom-call | flops 679477248 | bytes 4128768 | tf_op jit(solution)/shard_map/layer5/pallas_call | solution.py:18
  17.3 0.6 collective-permute-start.7
  17.9 1.6 %collective-permute-start.4 = (bf16[128,256]{1,0:T(8,128)(2,1)S(1)}, bf16[128,256]{1,0:T(8,128)(2,1)S(1)}, u32[]{:S(2)}, u32[]{:S(2)}) collective-permute-start(bf16[128,256]{1,0:T(8,128)(2,1)S(1)} %get-tuple-element.29), channel_id=1, source_target_pairs={{0,1},{1,0},{2,3},{3,2},{4,5},{5,4},{6,7},{7,6},{8,9},{9,8},{10,11... | collective-permute-start | bytes 196616 | tf_op jit(solution)/shard_map/ppermute | solution.py:45
  19.4 2.9 %collective-permute-start.5 = (bf16[128,256]{1,0:T(8,128)(2,1)S(1)}, bf16[128,256]{1,0:T(8,128)(2,1)S(1)}, u32[]{:S(2)}, u32[]{:S(2)}) collective-permute-start(bf16[128,256]{1,0:T(8,128)(2,1)S(1)} %get-tuple-element.30), channel_id=1, source_target_pairs={{0,32},{1,2},{2,1},{3,4},{4,3},{5,6},{6,5},{7,8},{8,7},{9,10},{10,... | collective-permute-start | bytes 196616 | tf_op jit(solution)/shard_map/ppermute | solution.py:45
  22.4 3.5 %collective-permute-start.8 = (bf16[640,256]{1,0:T(8,128)(2,1)S(1)}, bf16[640,256]{1,0:T(8,128)(2,1)S(1)}, u32[]{:S(2)}, u32[]{:S(2)}) collective-permute-start(bf16[640,256]{1,0:T(8,128)(2,1)S(1)} %regroup.1), channel_id=1, source_target_pairs={{0,32},{32,0},{64,96},{96,64},{1,33},{33,1},{65,97},{97,65},{2,34}... | collective-permute-start | bytes 983048 | tf_op jit(solution)/shard_map/ppermute | solution.py:50
  25.9 1.7 %weight4_parts.1 = (f32[54,16,128]{2,1,0:T(8,128)S(1)}, bf16[54,16,128]{2,1,0:T(8,128)(2,1)S(1)}) custom-call(f32[128,256]{1,0:T(8,128)S(1)} %get-tuple-element.28.inward_ref, bf16[128,256]{1,0:T(8,128)(2,1)S(1)} %collective-permute-done.4.first_ref, bf16[128,256]{1,0:T(8,128)(2,1)S(1)} %collective-permute-done.5.second_ref, ...), custom_call_target="tpu_custom_call" | custom-call | flops 905969664 | bytes 6029312 | tf_op jit(solution)/shard_map/weight4_parts/pallas_call | solution.py:18
  27.6 1.3 %weight5.1._ = bf16[64,48,128]{2,1,0:T(8,128)(2,1)S(1)} custom-call(bf16[448,256]{1,0:T(8,128)(2,1)S(1)} %get-tuple-element.35.mine_ref, bf16[448,256]{1,0:T(8,128)(2,1)S(1)} %collective-permute-done.7.got_ref.chip_ref, bf16[640,256]{1,0:T(8,128)(2,1)S(1)} %collective-permute-done.8.core_ref), custom_call_target="tpu_custom_call" | custom-call | flops 452984832 | bytes 786432 | tf_op jit(solution)/shard_map/weight5/pallas_call | solution.py:18
  29.1 34.0 %all_to_all.10.parts_ref = bf16[64,48,128]{2,1,0:T(8,128)(2,1)S(1)} all-to-all(bf16[64,48,128]{2,1,0:T(8,128)(2,1)S(1)} %pairs.1), channel_id=1, replica_groups={{0,1,2,3,4,5,6,7,8,9,10,11,12,13,14,15,16,17,18,19,20,21,22,23,24,25,26..., dimensions={0} | all-to-all | bytes 1572864 | tf_op jit(solution)/shard_map/all_to_all | solution.py:486
  63.7 15.6 %all_to_all.11.mine_ref = bf16[64,24,128]{2,1,0:T(8,128)(2,1)S(1)} all-to-all(bf16[64,24,128]{2,1,0:T(8,128)(2,1)S(1)} %pad_maximum_fusion), channel_id=1, replica_groups={{0,1,2,3,4,5,6,7,8,9,10,11,12,13,14,15,16,17,18,19,20,21,22,23,24,25,26..., dimensions={0} | all-to-all | bytes 786432 | tf_op jit(solution)/shard_map/all_to_all | solution.py:486
  79.3 2.9 %collective-permute-start.9 = (bf16[64,24,128]{2,1,0:T(8,128)(2,1)S(1)}, bf16[64,24,128]{2,1,0:T(8,128)(2,1)S(1)}, u32[]{:S(2)}, u32[]{:S(2)}) collective-permute-start(bf16[64,24,128]{2,1,0:T(8,128)(2,1)S(1)} %all_to_all.11.mine_ref), channel_id=1, source_target_pairs={{0,32},{32,0},{64,96},{96,64},{1,33},{33,1},{65,97},{97,65},{2,34}... | collective-permute-start | bytes 1179656 | tf_op jit(solution)/shard_map/ppermute | solution.py:50
  82.2 0.7 copy.16
  82.9 0.7 collective-permute-done.9.theirs_ref
  83.6 1.3 %finish.1 = (f32[27,64,128]{2,1,0:T(8,128)}, f32[27,4,256]{2,1,0:T(4,128)}) custom-call(bf16[64,24,128]{2,1,0:T(8,128)(2,1)S(1)} %all_to_all.11.mine_ref, bf16[64,24,128]{2,1,0:T(8,128)(2,1)S(1)} %collective-permute-done.9.theirs_ref), custom_call_target="tpu_custom_call" | custom-call | tf_op jit(solution)/shard_map/finish/pallas_call | solution.py:448
  (21 shorter events, 0.8 us)
Async XLA Ops:
  1.6 7.0 %collective-permute-start.1 = (bf16[2,64,512]{2,1,0:T(8,128)(2,1)S(1)}, bf16[2,64,512]{2,1,0:T(8,128)(2,1)S(1)}, u32[]{:S(2)}, u32[]{:S(2)}) collective-permute-start(bf16[2,64,512]{2,1,0:T(8,128)(2,1)S(1)} %get-tuple-element.41), channel_id=1, source_target_pairs={{0,32},{1,2},{2,1},{3,4},{4,3},{5,6},{6,5},{7,8},{8,7},{9,10},{10,... | collective-permute-start | bytes 393224 | tf_op jit(solution)/shard_map/ppermute | solution.py:45
  3.1 5.5 %collective-permute-start = (bf16[2,64,512]{2,1,0:T(8,128)(2,1)S(1)}, bf16[2,64,512]{2,1,0:T(8,128)(2,1)S(1)}, u32[]{:S(2)}, u32[]{:S(2)}) collective-permute-start(bf16[2,64,512]{2,1,0:T(8,128)(2,1)S(1)} %get-tuple-element.42), channel_id=1, source_target_pairs={{0,1},{1,0},{2,3},{3,2},{4,5},{5,4},{6,7},{7,6},{8,9},{9,8},{10,11... | collective-permute-start | bytes 393224 | tf_op jit(solution)/shard_map/ppermute | solution.py:45
  6.4 1.0 %copy-start.1 = (bf16[2,2,64,512]{3,2,1,0:T(8,128)(2,1)S(1)}, bf16[2,2,64,512]{3,2,1,0:T(8,128)(2,1)}, u32[]{:S(2)}) copy-start(bf16[2,2,64,512]{3,2,1,0:T(8,128)(2,1)} %vol_ref.1) | copy-start | bytes 786436
  7.3 6.4 %copy-start = (bf16[27,256,128]{2,1,0:T(8,128)(2,1)S(1)}, bf16[27,256,128]{2,1,0:T(8,128)(2,1)}, u32[]{:S(2)}) copy-start(bf16[27,256,128]{2,1,0:T(8,128)(2,1)} %weight_ref.3) | copy-start | bytes 5308420
  8.6 6.7 %copy-start.2 = (bf16[1,2,256,128]{3,2,1,0:T(8,128)(2,1)S(1)}, bf16[1,2,256,128]{3,2,1,0:T(8,128)(2,1)}, u32[]{:S(2)}) copy-start(bf16[1,2,256,128]{3,2,1,0:T(8,128)(2,1)} %param.5) | copy-start | bytes 393220
  10.2 4.2 %collective-permute-start.3 = (bf16[128,256]{1,0:T(8,128)(2,1)S(1)}, bf16[128,256]{1,0:T(8,128)(2,1)S(1)}, u32[]{:S(2)}, u32[]{:S(2)}) collective-permute-start(bf16[128,256]{1,0:T(8,128)(2,1)S(1)} %get-tuple-element.24.pooled_ref), channel_id=1, source_target_pairs={{0,32},{1,2},{2,1},{3,4},{4,3},{5,6},{6,5},{7,8},{8,7},{9,10},{10,... | collective-permute-start | bytes 196616 | tf_op jit(solution)/shard_map/ppermute | solution.py:45
  11.5 3.8 %collective-permute-start.2 = (bf16[128,256]{1,0:T(8,128)(2,1)S(1)}, bf16[128,256]{1,0:T(8,128)(2,1)S(1)}, u32[]{:S(2)}, u32[]{:S(2)}) collective-permute-start(bf16[128,256]{1,0:T(8,128)(2,1)S(1)} %get-tuple-element.24.pooled_ref), channel_id=1, source_target_pairs={{0,1},{1,0},{2,3},{3,2},{4,5},{5,4},{6,7},{7,6},{8,9},{9,8},{10,11... | collective-permute-start | bytes 196616 | tf_op jit(solution)/shard_map/ppermute | solution.py:45
  17.3 5.1 %collective-permute-start.7 = (bf16[448,256]{1,0:T(8,128)(2,1)S(1)}, bf16[448,256]{1,0:T(8,128)(2,1)S(1)}, u32[]{:S(2)}, u32[]{:S(2)}) collective-permute-start(bf16[448,256]{1,0:T(8,128)(2,1)S(1)} %get-tuple-element.36), channel_id=1, source_target_pairs={{0,64},{32,96},{64,0},{96,32},{1,65},{33,97},{65,1},{97,33},{2,66}... | collective-permute-start | bytes 688136 | tf_op jit(solution)/shard_map/ppermute | solution.py:55
  17.9 8.0 %collective-permute-start.4 = (bf16[128,256]{1,0:T(8,128)(2,1)S(1)}, bf16[128,256]{1,0:T(8,128)(2,1)S(1)}, u32[]{:S(2)}, u32[]{:S(2)}) collective-permute-start(bf16[128,256]{1,0:T(8,128)(2,1)S(1)} %get-tuple-element.29), channel_id=1, source_target_pairs={{0,1},{1,0},{2,3},{3,2},{4,5},{5,4},{6,7},{7,6},{8,9},{9,8},{10,11... | collective-permute-start | bytes 196616 | tf_op jit(solution)/shard_map/ppermute | solution.py:45
  19.4 6.4 %collective-permute-start.5 = (bf16[128,256]{1,0:T(8,128)(2,1)S(1)}, bf16[128,256]{1,0:T(8,128)(2,1)S(1)}, u32[]{:S(2)}, u32[]{:S(2)}) collective-permute-start(bf16[128,256]{1,0:T(8,128)(2,1)S(1)} %get-tuple-element.30), channel_id=1, source_target_pairs={{0,32},{1,2},{2,1},{3,4},{4,3},{5,6},{6,5},{7,8},{8,7},{9,10},{10,... | collective-permute-start | bytes 196616 | tf_op jit(solution)/shard_map/ppermute | solution.py:45
  22.4 5.3 %collective-permute-start.8 = (bf16[640,256]{1,0:T(8,128)(2,1)S(1)}, bf16[640,256]{1,0:T(8,128)(2,1)S(1)}, u32[]{:S(2)}, u32[]{:S(2)}) collective-permute-start(bf16[640,256]{1,0:T(8,128)(2,1)S(1)} %regroup.1), channel_id=1, source_target_pairs={{0,32},{32,0},{64,96},{96,64},{1,33},{33,1},{65,97},{97,65},{2,34}... | collective-permute-start | bytes 983048 | tf_op jit(solution)/shard_map/ppermute | solution.py:50
  27.5 1.6 %collective-permute-start.6 = (bf16[54,16,128]{2,1,0:T(8,128)(2,1)S(1)}, bf16[54,16,128]{2,1,0:T(8,128)(2,1)S(1)}, u32[]{:S(2)}, u32[]{:S(2)}) collective-permute-start(bf16[54,16,128]{2,1,0:T(8,128)(2,1)S(1)} %get-tuple-element.34), channel_id=1, source_target_pairs={{0,32},{32,0},{64,96},{96,64},{1,33},{33,1},{65,97},{97,65},{2,34}... | collective-permute-start | bytes 663560 | tf_op jit(solution)/shard_map/ppermute | solution.py:50
  79.3 4.3 %collective-permute-start.9 = (bf16[64,24,128]{2,1,0:T(8,128)(2,1)S(1)}, bf16[64,24,128]{2,1,0:T(8,128)(2,1)S(1)}, u32[]{:S(2)}, u32[]{:S(2)}) collective-permute-start(bf16[64,24,128]{2,1,0:T(8,128)(2,1)S(1)} %all_to_all.11.mine_ref), channel_id=1, source_target_pairs={{0,32},{32,0},{64,96},{96,64},{1,33},{33,1},{65,97},{97,65},{2,34}... | collective-permute-start | bytes 1179656 | tf_op jit(solution)/shard_map/ppermute | solution.py:50

commit v6 on v5

--- a/solution.py
+++ b/solution.py
@@ -207,7 +207,7 @@
     part_ref[...] = convolved5(weight_ref, pooled_ref[...], cells, 0)
     for o in range(27):
         a, t = divmod(o, len(TAPS))
-        back_ref[t, pl.ds(a * chans, chans), :] = weight_ref[o].T
+        back_ref[t, pl.ds((0, 2, 1)[a] * chans, chans), :] = weight_ref[o].T
 
 
 def own5(pooled, weight):
@@ -222,9 +222,37 @@
     )
 
 
+def inward_part(back_ref, grad, cells, first, rows):
+    total = None
+    for t, (b, e) in enumerate(TAPS):
+        shifts = tapped(grad, WIDTH // 2, cells, -b, -e)
+        part = dot(back_ref[t, pl.ds(first, rows), :], shifts)
+        total = part if total is None else total + part
+    return total
+
+
+def own_inward_kernel(mine_ref, back_ref, inward_ref):
+    outer = back_ref.shape[2]
+    chans, lanes = inward_ref.shape
+    grad = mine_ref[pl.ds(0, outer), :]
+    inward_ref[...] = inward_part(back_ref, grad, lanes // 2, 2 * chans, chans)
+
+
+def own_inward(mine, back):
+    chans = back.shape[1] // 3
+    (inward,) = call(
+        own_inward_kernel,
+        "own_inward",
+        (((chans, mine.shape[1]), F32),),
+        (mine, back),
+        flops=2 * back.size * mine.shape[1] // 3,
+    )
+    return inward
+
+
 def layer5_kernel(
     pooled_ref, first_ref, second_ref, weight_ref, cot_ref, part_ref, back_ref,
-    out_ref, inward_ref, to_first_ref, to_second_ref, mine_ref, share_ref,
+    out_ref, to_first_ref, to_second_ref, mine_ref, share_ref,
 ):
     chans = pooled_ref.shape[0]
     outer = part_ref.shape[0]
@@ -243,12 +271,8 @@
     grad = jnp.concatenate(grads, axis=1)
     mine_ref[pl.ds(0, outer), :] = grad
     share_ref[pl.ds(0, outer), :] = grad
-    inward = None
-    for t, (b, e) in enumerate(TAPS):
-        part = dot(back_ref[t], tapped(grad, WIDTH // 2, cells, -b, -e))
-        inward = part if inward is None else inward + part
-    down, up = inward[:chans].astype(BF16), inward[2 * chans :].astype(BF16)
-    inward_ref[...] = inward[chans : 2 * chans]
+    inward = inward_part(back_ref, grad, cells, 0, 2 * chans)
+    down, up = inward[:chans].astype(BF16), inward[chans:].astype(BF16)
     odd = lax.axis_index("space") % 2 == 1
     to_first_ref[...] = jnp.where(odd, down, up)
     to_second_ref[...] = jnp.where(odd, up, down)
@@ -268,7 +292,6 @@
         "layer5",
         (
             ((vols, outer, cells), BF16),
-            ((chans, lanes), F32),
             ((chans, lanes), BF16),
             ((chans, lanes), BF16),
             ((outer + 3 * chans // 2, lanes), BF16),
@@ -279,7 +302,16 @@
     )
 
 
-def regroup_kernel(mine_ref, got_ref, send_ref):
+def stack_window(ref, first, rows, out_ref, i):
+    lanes = ref.shape[1]
+    chans = rows // 3
+    planes = tuple(ref[pl.ds(first + j * chans, chans), :] for j in range(3))
+    spread_taps(planes, out_ref.at[:, pl.ds(i * lanes, lanes)], WIDTH // 2, lanes // 2, 1)
+
+
+def regroup_kernel(mine_ref, got_ref, made_ref, send_ref, stack_ref, out_ref, sem):
+    copy = pltpu.make_async_copy(made_ref, out_ref, sem)
+    copy.start()
     core = lax.axis_index("dp") % 2
     rows = send_ref.shape[0] // 2
     half = mine_ref.shape[0] - rows
@@ -287,31 +319,36 @@
         start = pl.multiple_of((1 - core) * half, half)
         send_ref[pl.ds(i * rows, half), :] = ref[pl.ds(start, half), :]
         send_ref[pl.ds(i * rows + half, rows - half), :] = ref[pl.ds(2 * half, rows - half), :]
-
-
-def regrouped(mine, got, outer):
+        stack_window(ref, 2 * half, rows - half, stack_ref, i)
+    copy.wait()
+
+
+def regrouped(mine, got, made, outer):
     rows = mine.shape[0] - outer // 2
-    (send,) = call(regroup_kernel, "regroup", (((2 * rows, mine.shape[1]), BF16),), (mine, got))
-    return send
-
-
-def weight5_kernel(mine_ref, chip_ref, core_ref, part_ref, stack_ref, total_ref):
+    lanes = mine.shape[1]
+    return pl.pallas_call(
+        regroup_kernel,
+        out_shape=(
+            pltpu.VMEM((2 * rows, lanes), BF16),
+            pltpu.VMEM((9 * (mine.shape[0] - outer), 4 * lanes), BF16),
+            jax.ShapeDtypeStruct(made.shape, made.dtype),
+        ),
+        in_specs=[VMEM] * 3,
+        out_specs=(VMEM, VMEM, pl.BlockSpec(memory_space=pl.ANY)),
+        scratch_shapes=[pltpu.SemaphoreType.DMA],
+        compiler_params=pltpu.CompilerParams(vmem_limit_bytes=12 * 2**20),
+        name="regroup",
+    )(*[pltpu.with_memory_space_constraint(x, pltpu.VMEM) for x in (mine, got, made)])
+
+
+def weight5_kernel(mine_ref, chip_ref, core_ref, _, part_ref, stack_ref, total_ref):
     core = lax.axis_index("dp") % 2
-    lanes = mine_ref.shape[1]
     rows = core_ref.shape[0] // 2
     half = mine_ref.shape[0] - rows
     own = pl.ds(pl.multiple_of(core * half, half), half)
-    grads = []
-    for i, (ref, at, first) in enumerate((
-        (mine_ref, own, 2 * half),
-        (chip_ref, own, 2 * half),
-        (core_ref, pl.ds(0, half), half),
-        (core_ref, pl.ds(rows, half), rows + half),
-    )):
-        grads.append(ref[at, :])
-        chans = (rows - half) // 3
-        planes = tuple(ref[pl.ds(first + j * chans, chans), :] for j in range(3))
-        spread_taps(planes, stack_ref.at[:, pl.ds(i * lanes, lanes)], WIDTH // 2, lanes // 2, 1)
+    for i in range(2):
+        stack_window(core_ref, i * rows + half, rows - half, stack_ref, 2 + i)
+    grads = (mine_ref[own, :], chip_ref[own, :], core_ref[pl.ds(0, half), :], core_ref[pl.ds(rows, half), :])
     grads = jnp.concatenate(grads, axis=1)
     block = stack_ref.shape[0] // 3
     for j in range(3):
@@ -325,16 +362,15 @@
         ].astype(BF16)
 
 
-def weight5_part(mine, chip, core, outer):
-    lanes = mine.shape[1]
-    rows = 9 * (mine.shape[0] - outer)
-    (part,) = call(
+def weight5_part(mine, chip, core, stack, outer):
+    part, _ = call(
         weight5_kernel,
         "weight5",
-        (((64, 48, 128), BF16),),
-        (mine, chip, core),
-        scratch=[pltpu.VMEM((rows, 4 * lanes), BF16), pltpu.VMEM((rows + 8, outer // 2), F32)],
-        flops=4 * rows * lanes * outer,
+        (((64, 48, 128), BF16), (stack.shape, BF16)),
+        (mine, chip, core, stack),
+        scratch=[pltpu.VMEM((stack.shape[0] + 8, outer // 2), F32)],
+        flops=stack.size * outer,
+        aliases={3: 1},
     )
     return part
 
@@ -402,14 +438,13 @@
 
 
 def sum_kernel(parts_ref, rows4_ref, rows5_ref):
-    def step(i, acc):
-        return acc + parts_ref[i].astype(F32)
-
     owners = parts_ref.shape[0]
-    sides = [
-        lax.fori_loop(1, owners // 2, lambda i, acc, at=at: step(at + i, acc), parts_ref[at].astype(F32))
-        for at in (0, owners // 2)
-    ]
+    sides = []
+    for side in range(2):
+        total = parts_ref[side * owners // 2].astype(F32)
+        for i in range(1, owners // 2):
+            total += parts_ref[side * owners // 2 + i].astype(F32)
+        sides.append(total)
     rows4_ref[...] = (sides[0][:16] + sides[1][:16]).astype(BF16)
     half = rows5_ref.shape[0] // 2
     owner = lax.axis_index("dp") // 2 * (owners // 2) + lax.axis_index("space")
@@ -424,38 +459,55 @@
     return call(sum_kernel, "sums", (((16, 128), BF16), ((128, 128), BF16)), (parts,))
 
 
-def finish_kernel(mine_ref, theirs_ref, weight4_ref, weight5_ref):
-    core = lax.axis_index("dp") % 2
+def place_rows(rows_ref, weight4_ref, weight5_ref, side, half4_ref, half5_ref, sems):
     first = lax.axis_index("space") % 16 * 4
-    share = 27 * 64 // mine_ref.shape[0]
+    share = 27 * 64 // rows_ref.shape[0]
     row = lax.broadcasted_iota(jnp.int32, (4, 128), 0)
     for o in range(27):
-        for side, ref in ((core, mine_ref), (1 - core, theirs_ref)):
-            for k in range(2):
-                at = pl.multiple_of(side * 32 + k * 16, 16)
-                weight4_ref[o, pl.ds(at, 16), :] = ref[2 * o + k].astype(F32)[:16]
-            start = o * 64 + first
-            owner = start // share
-            low = ref[owner].astype(F32)[16:20]
-            high = ref[(start + 3) // share].astype(F32)[16:20]
-            at = pl.multiple_of(side * 128, 128)
-            weight5_ref[o, :, pl.ds(at, 128)] = jnp.where(
-                row < (owner + 1) * share - start, low, high
-            )
-
-
-def finished(mine, theirs):
-    weight4, weight5 = pl.pallas_call(
-        finish_kernel,
+        for k in range(2):
+            half4_ref[o, pl.ds(k * 16, 16), :] = rows_ref[2 * o + k].astype(F32)[:16]
+    at = pl.multiple_of(side * 32, 32)
+    copy4 = pltpu.make_async_copy(half4_ref, weight4_ref.at[:, pl.ds(at, 32), :], sems.at[0])
+    copy4.start()
+    for o in range(27):
+        start = o * 64 + first
+        owner = start // share
+        low = rows_ref[owner].astype(F32)[16:20]
+        high = rows_ref[(start + 3) // share].astype(F32)[16:20]
+        half5_ref[o] = jnp.where(row < (owner + 1) * share - start, low, high)
+    at = pl.multiple_of(side * 128, 128)
+    copy5 = pltpu.make_async_copy(half5_ref, weight5_ref.at[:, :, pl.ds(at, 128)], sems.at[1])
+    copy5.start()
+    copy4.wait()
+    copy5.wait()
+
+
+def first_half_kernel(rows_ref, weight4_ref, weight5_ref, *scratch):
+    place_rows(rows_ref, weight4_ref, weight5_ref, lax.axis_index("dp") % 2, *scratch)
+
+
+def second_half_kernel(rows_ref, _, __, weight4_ref, weight5_ref, *scratch):
+    place_rows(rows_ref, weight4_ref, weight5_ref, 1 - lax.axis_index("dp") % 2, *scratch)
+
+
+def placed_half(kernel, name, rows, *halves):
+    anywhere = pl.BlockSpec(memory_space=pl.ANY)
+    return pl.pallas_call(
+        kernel,
         out_shape=(
             jax.ShapeDtypeStruct((27, 64, 128), F32),
             jax.ShapeDtypeStruct((27, 4, 256), F32),
         ),
-        in_specs=[VMEM] * 2,
-        out_specs=(VMEM, VMEM),
-        name="finish",
-    )(*[pltpu.with_memory_space_constraint(x, pltpu.VMEM) for x in (mine, theirs)])
-    return weight4.transpose(0, 2, 1), weight5.transpose(0, 2, 1)
+        in_specs=[VMEM] + [anywhere] * len(halves),
+        out_specs=(anywhere, anywhere),
+        scratch_shapes=[
+            pltpu.VMEM((27, 32, 128), F32),
+            pltpu.VMEM((27, 4, 128), F32),
+            pltpu.SemaphoreType.DMA((2,)),
+        ],
+        input_output_aliases={i + 1: i for i in range(len(halves))},
+        name=name,
+    )(pltpu.with_memory_space_constraint(rows, pltpu.VMEM), *halves)
 
 
 def per_device(volumes, cotangent, conv4_weight, conv5_weight):
@@ -466,14 +518,15 @@
     part4, stack4 = own4(volumes, arranged4)
     pooled, slope, stack4 = layer4(first4, second4, arranged4, part4, stack4)
     part5, back5 = own5(pooled, conv5_weight)
-    output5, inward, to_first, to_second, mine5, share5 = layer5(
+    output5, to_first, to_second, mine5, share5 = layer5(
         pooled, swapped(pooled, 0), swapped(pooled, 1), conv5_weight, cotangent[0], part5, back5
     )
     first, second = swapped(to_first, 0), swapped(to_second, 1)
+    inward = own_inward(mine5, back5)
     outer = conv5_weight.shape[1]
     chip5 = other_chip(share5)
-    core5 = other_core(regrouped(mine5, chip5, outer))
-    part = weight5_part(mine5, chip5, core5, outer)
+    send5, chips5, output5 = regrouped(mine5, chip5, output5, outer)
+    part = weight5_part(mine5, chip5, other_core(send5), chips5, outer)
     keep, send = weight4_parts(inward, first, second, stack4, slope)
     axes = ("dp", "space")
     spaces, groups = lax.axis_size("space"), lax.axis_size("dp")
@@ -497,8 +550,9 @@
         axis=1,
     )
     mine = exchange(outgoing)
-    weight4, weight5 = finished(mine, other_core(mine))
-    return (output5[None], weight4, weight5)
+    halves = placed_half(first_half_kernel, "first_half", mine)
+    weight4, weight5 = placed_half(second_half_kernel, "second_half", other_core(mine), *halves)
+    return (output5[None], weight4.transpose(0, 2, 1), weight5.transpose(0, 2, 1))
 
 
 def solution(mesh):

time: 85.1 us -> 84.2 us (0.989)
  blocking collectives: 49.6 us -> 48.3 us
  Pallas kernels: 10.2 us -> 11.4 us
    pallas_call x1 -> x3, Pallas kernels: 1.26 us -> 2.61 us  [the longest x2 1.93 us: placed_half(): pl.pallas_call(kernel, out_shape=(jax.ShapeDtypeStruct((27, 64, 128), F32...]
    all_to_all x2, blocking collectives: 49.6 us -> 48.3 us  [exchange(): lax.all_to_all(parts, axes, split_axis=0, concat_axis=0, tiled=True, axis...]
  transfers between devices with their start and end apart: 10 -> 10, of which waited for: 3 -> 3; matrix products, arithmetic and copies ran while one was open for 2% -> 1% of each run, Pallas kernels for 6% -> 8%
where the time goes in v6:
time: 84.2 us; the launch traced here: 84 us
  blocking collectives  48.3 us (57%)
  starting transfers between devices  18.6 us (22%)
  Pallas kernels  11.4 us (14%)
  local copies, waits for them, and re-layouts  3.23 us (4%)
  waiting for transfers between devices  1.54 us (2%)
    all_to_all x2, blocking collectives, exchange(): lax.all_to_all(parts, axes, split_axis=0, concat_axis=0, tiled=True, axis...  48.3 us
    ppermute x6, starting transfers between devices, swapped(): return lax.ppermute(values, ('dp', 'space'), pairs)  11.5 us
    pallas_call x9, Pallas kernels, call(): pl.pallas_call(kernel, out_shape=tuple((pltpu.VMEM(shape, dtype) for shap...  8.84 us
    ppermute x3, starting transfers between devices, other_core(): return lax.ppermute(values, 'dp', [(i, i ^ 1) for i in range(count)])  6.56 us
    pallas_call x2, Pallas kernels, placed_half(): pl.pallas_call(kernel, out_shape=(jax.ShapeDtypeStruct((27, 64, 128), F32...  1.93 us
  transfers between devices with their start and end apart: 10, of which 3 were waited for; matrix products, arithmetic and copies ran while one was open for 1% of the time, Pallas kernels for 8%

profile of v6, /device:TPU:1, one launch (start us, length us, event | category | flops | bytes accessed | tf_op | source)
XLA Modules:
  0.0 84.0 jit_solution(17101382066867288838)
XLA Ops:
  0.6 1.0 %dynamic-slice_bitcast_fusion = (bf16[2,64,512]{2,1,0:T(8,128)(2,1)S(1)}, bf16[2,64,512]{2,1,0:T(8,128)(2,1)S(1)}) fusion(bf16[2,2,64,512]{3,2,1,0:T(8,128)(2,1)} %vol_ref.1, s32[]{:T(128)S(6)} %select_n.16, s32[]{:T(128)S(6)} %select_n.15), kind=kLoop, calls=%fused_computation.1 | loop fusion | bytes 524296 | tf_op jit(solution)/shard_map/jit(dynamic_index_in_dim)/squeeze | solution.py:516
  1.6 1.5 %collective-permute-start.1 = (bf16[2,64,512]{2,1,0:T(8,128)(2,1)S(1)}, bf16[2,64,512]{2,1,0:T(8,128)(2,1)S(1)}, u32[]{:S(2)}, u32[]{:S(2)}) collective-permute-start(bf16[2,64,512]{2,1,0:T(8,128)(2,1)S(1)} %get-tuple-element.51), channel_id=1, source_target_pairs={{0,32},{1,2},{2,1},{3,4},{4,3},{5,6},{6,5},{7,8},{8,7},{9,10},{10,... | collective-permute-start | bytes 393224 | tf_op jit(solution)/shard_map/ppermute | solution.py:45
  3.1 2.0 %collective-permute-start = (bf16[2,64,512]{2,1,0:T(8,128)(2,1)S(1)}, bf16[2,64,512]{2,1,0:T(8,128)(2,1)S(1)}, u32[]{:S(2)}, u32[]{:S(2)}) collective-permute-start(bf16[2,64,512]{2,1,0:T(8,128)(2,1)S(1)} %get-tuple-element.52), channel_id=1, source_target_pairs={{0,1},{1,0},{2,3},{3,2},{4,5},{5,4},{6,7},{7,6},{8,9},{9,8},{10,11... | collective-permute-start | bytes 393224 | tf_op jit(solution)/shard_map/ppermute | solution.py:45
  5.1 1.2 %copy.15.weight_ref = bf16[128,1728]{1,0:T(8,128)(2,1)S(1)} copy(bf16[128,1728]{0,1:T(8,128)(2,1)} %bitcast.17) | data formatting | bytes 884736 | tf_op jit(solution)/shard_map/reshape | solution.py:517
  6.4 0.9 %copy-done.1 = bf16[2,2,64,512]{3,2,1,0:T(8,128)(2,1)S(1)} copy-done((bf16[2,2,64,512]{3,2,1,0:T(8,128)(2,1)S(1)}, bf16[2,2,64,512]{3,2,1,0:T(8,128)(2,1)}, u32[]{:S(2)}) %copy-start.1) | copy-done | bytes 262168
  7.3 1.3 %own4.1 = (f32[2,128,1024]{2,1,0:T(8,128)S(1)}, bf16[2304,1024]{1,0:T(8,128)(2,1)S(1)}) custom-call(bf16[2,2,64,512]{3,2,1,0:T(8,128)(2,1)S(1)} %copy-done.1, bf16[128,1728]{1,0:T(8,128)(2,1)S(1)} %copy.15.weight_ref), custom_call_target="tpu_custom_call" | custom-call | flops 905969664 | bytes 704512 | tf_op jit(solution)/shard_map/own4/pallas_call | solution.py:18
  8.7 1.5 %layer4.1 = (bf16[128,256]{1,0:T(8,128)(2,1)S(1)}, f32[2,128,1024]{2,1,0:T(8,128)S(1)}, bf16[2304,1024]{1,0:T(8,128)(2,1)S(1)}) custom-call(bf16[2,64,512]{2,1,0:T(8,128)(2,1)S(1)} %collective-permute-done.first_ref, bf16[2,64,512]{2,1,0:T(8,128)(2,1)S(1)} %collective-permute-done.1.second_ref, ...), custom_call_target="tpu_custom_call", output_to_operand_aliasing={{1}: (3, {}), {2}: (4, {})} | custom-call | flops 452984832 | bytes 6471680 | tf_op jit(solution)/shard_map/layer4/pallas_call | solution.py:18
  10.2 1.3 %collective-permute-start.3 = (bf16[128,256]{1,0:T(8,128)(2,1)S(1)}, bf16[128,256]{1,0:T(8,128)(2,1)S(1)}, u32[]{:S(2)}, u32[]{:S(2)}) collective-permute-start(bf16[128,256]{1,0:T(8,128)(2,1)S(1)} %get-tuple-element.29.pooled_ref), channel_id=1, source_target_pairs={{0,32},{1,2},{2,1},{3,4},{4,3},{5,6},{6,5},{7,8},{8,7},{9,10},{10,... | collective-permute-start | bytes 196616 | tf_op jit(solution)/shard_map/ppermute | solution.py:45
  11.5 2.2 %collective-permute-start.2 = (bf16[128,256]{1,0:T(8,128)(2,1)S(1)}, bf16[128,256]{1,0:T(8,128)(2,1)S(1)}, u32[]{:S(2)}, u32[]{:S(2)}) collective-permute-start(bf16[128,256]{1,0:T(8,128)(2,1)S(1)} %get-tuple-element.29.pooled_ref), channel_id=1, source_target_pairs={{0,1},{1,0},{2,3},{3,2},{4,5},{5,4},{6,7},{7,6},{8,9},{9,8},{10,11... | collective-permute-start | bytes 196616 | tf_op jit(solution)/shard_map/ppermute | solution.py:45
  13.7 0.7 own5.1
  14.4 1.0 %collective-permute-done.2.first_ref = bf16[128,256]{1,0:T(8,128)(2,1)S(1)} collective-permute-done((bf16[128,256]{1,0:T(8,128)(2,1)S(1)}, bf16[128,256]{1,0:T(8,128)(2,1)S(1)}, u32[]{:S(2)}, u32[]{:S(2)}) %collective-permute-start.2) | collective-permute-done | bytes 65568 | tf_op jit(solution)/shard_map/ppermute | solution.py:45
  15.3 1.7 %layer5.1 = (bf16[2,256,128]{2,1,0:T(8,128)(2,1)S(1)}, bf16[128,256]{1,0:T(8,128)(2,1)S(1)}, bf16[128,256]{1,0:T(8,128)(2,1)S(1)}, bf16[448,256]{1,0:T(8,128)(2,1)S(1)}, bf16[448,256]{1,0:T(8,128)(2,1)S(1)}) custom-call(bf16[128,256]{1,0:T(8,128)(2,1)S(1)} %get-tuple-element.29.pooled_ref, bf16[128,256]{1,0:T(8,128)(2,1)S(1)} %collective-permute-done.2.first_ref, ...), custom_call_target="tpu_custom_call" | custom-call | flops 679477248 | bytes 4128768 | tf_op jit(solution)/shard_map/layer5/pallas_call | solution.py:18
  17.1 0.6 collective-permute-start.4
  17.7 1.6 %collective-permute-start.5 = (bf16[128,256]{1,0:T(8,128)(2,1)S(1)}, bf16[128,256]{1,0:T(8,128)(2,1)S(1)}, u32[]{:S(2)}, u32[]{:S(2)}) collective-permute-start(bf16[128,256]{1,0:T(8,128)(2,1)S(1)} %get-tuple-element.36), channel_id=1, source_target_pairs={{0,1},{1,0},{2,3},{3,2},{4,5},{5,4},{6,7},{7,6},{8,9},{9,8},{10,11... | collective-permute-start | bytes 196616 | tf_op jit(solution)/shard_map/ppermute | solution.py:45
  19.2 2.9 %collective-permute-start.6 = (bf16[128,256]{1,0:T(8,128)(2,1)S(1)}, bf16[128,256]{1,0:T(8,128)(2,1)S(1)}, u32[]{:S(2)}, u32[]{:S(2)}) collective-permute-start(bf16[128,256]{1,0:T(8,128)(2,1)S(1)} %get-tuple-element.37), channel_id=1, source_target_pairs={{0,32},{1,2},{2,1},{3,4},{4,3},{5,6},{6,5},{7,8},{8,7},{9,10},{10,... | collective-permute-start | bytes 196616 | tf_op jit(solution)/shard_map/ppermute | solution.py:45
  22.1 0.7 regroup.1
  22.8 3.5 %collective-permute-start.8 = (bf16[640,256]{1,0:T(8,128)(2,1)S(1)}, bf16[640,256]{1,0:T(8,128)(2,1)S(1)}, u32[]{:S(2)}, u32[]{:S(2)}) collective-permute-start(bf16[640,256]{1,0:T(8,128)(2,1)S(1)} %get-tuple-element.42), channel_id=1, source_target_pairs={{0,32},{32,0},{64,96},{96,64},{1,33},{33,1},{65,97},{97,65},{2,34}... | collective-permute-start | bytes 983048 | tf_op jit(solution)/shard_map/ppermute | solution.py:50
  26.9 1.7 %weight4_parts.1 = (f32[54,16,128]{2,1,0:T(8,128)S(1)}, bf16[54,16,128]{2,1,0:T(8,128)(2,1)S(1)}) custom-call(f32[128,256]{1,0:T(8,128)S(1)} %own_inward.1.inward_ref, bf16[128,256]{1,0:T(8,128)(2,1)S(1)} %collective-permute-done.5.first_ref, bf16[128,256]{1,0:T(8,128)(2,1)S(1)} %collective-permute-done.6.second_ref, ...), custom_call_target="tpu_custom_call" | custom-call | flops 905969664 | bytes 6029312 | tf_op jit(solution)/shard_map/weight4_parts/pallas_call | solution.py:18
  28.7 1.3 %weight5.1 = (bf16[64,48,128]{2,1,0:T(8,128)(2,1)S(1)}, bf16[1728,1024]{1,0:T(8,128)(2,1)S(1)}) custom-call(bf16[448,256]{1,0:T(8,128)(2,1)S(1)} %get-tuple-element.32.mine_ref, bf16[448,256]{1,0:T(8,128)(2,1)S(1)} %collective-permute-done.4.got_ref.chip_ref, bf16[640,256]{1,0:T(8,128)(2,1)S(1)} %collective-permute-done.8.core_ref, ...), custom_call_target="tpu_custom_call", output_to_operand_aliasing={{1}: (3, {})} | custom-call | flops 452984832 | bytes 4325376 | tf_op jit(solution)/shard_map/weight5/pallas_call | solution.py:18
  30.2 32.5 %all_to_all.10.parts_ref = bf16[64,48,128]{2,1,0:T(8,128)(2,1)S(1)} all-to-all(bf16[64,48,128]{2,1,0:T(8,128)(2,1)S(1)} %pairs.1), channel_id=1, replica_groups={{0,1,2,3,4,5,6,7,8,9,10,11,12,13,14,15,16,17,18,19,20,21,22,23,24,25,26..., dimensions={0} | all-to-all | bytes 1572864 | tf_op jit(solution)/shard_map/all_to_all | solution.py:539
  62.9 15.7 %all_to_all.11.rows_ref = bf16[64,24,128]{2,1,0:T(8,128)(2,1)S(1)} all-to-all(bf16[64,24,128]{2,1,0:T(8,128)(2,1)S(1)} %pad_maximum_fusion), channel_id=1, replica_groups={{0,1,2,3,4,5,6,7,8,9,10,11,12,13,14,15,16,17,18,19,20,21,22,23,24,25,26..., dimensions={0} | all-to-all | bytes 786432 | tf_op jit(solution)/shard_map/all_to_all | solution.py:539
  78.7 3.0 %collective-permute-start.9 = (bf16[64,24,128]{2,1,0:T(8,128)(2,1)S(1)}, bf16[64,24,128]{2,1,0:T(8,128)(2,1)S(1)}, u32[]{:S(2)}, u32[]{:S(2)}) collective-permute-start(bf16[64,24,128]{2,1,0:T(8,128)(2,1)S(1)} %all_to_all.11.rows_ref), channel_id=1, source_target_pairs={{0,32},{32,0},{64,96},{96,64},{1,33},{33,1},{65,97},{97,65},{2,34}... | collective-permute-start | bytes 1179656 | tf_op jit(solution)/shard_map/ppermute | solution.py:50
  81.6 1.0 %first_half.1 = (f32[27,64,128]{2,1,0:T(8,128)}, f32[27,4,256]{2,1,0:T(4,128)}) custom-call(bf16[64,24,128]{2,1,0:T(8,128)(2,1)S(1)} %all_to_all.11.rows_ref), custom_call_target="tpu_custom_call" | custom-call | tf_op jit(solution)/shard_map/first_half/pallas_call | solution.py:495
  83.0 1.0 %second_half.1 = (f32[27,64,128]{2,1,0:T(8,128)}, f32[27,4,256]{2,1,0:T(4,128)}) custom-call(bf16[64,24,128]{2,1,0:T(8,128)(2,1)S(1)} %collective-permute-done.9.rows_ref, f32[27,64,128]{2,1,0:T(8,128)} %get-tuple-element.47._, f32[27,4,256]{2,1,0:T(4,128)} %get-tuple-element.48.__), custom_call_target="tpu_custom_call", output_to_operand_aliasing={{0}: (1, {}), {1}: (2, {})} | custom-call | tf_op jit(solution)/shard_map/second_half/pallas_call | solution.py:495
  (22 shorter events, 1.5 us)
Async XLA Ops:
  1.6 7.0 %collective-permute-start.1 = (bf16[2,64,512]{2,1,0:T(8,128)(2,1)S(1)}, bf16[2,64,512]{2,1,0:T(8,128)(2,1)S(1)}, u32[]{:S(2)}, u32[]{:S(2)}) collective-permute-start(bf16[2,64,512]{2,1,0:T(8,128)(2,1)S(1)} %get-tuple-element.51), channel_id=1, source_target_pairs={{0,32},{1,2},{2,1},{3,4},{4,3},{5,6},{6,5},{7,8},{8,7},{9,10},{10,... | collective-permute-start | bytes 393224 | tf_op jit(solution)/shard_map/ppermute | solution.py:45
  3.1 5.5 %collective-permute-start = (bf16[2,64,512]{2,1,0:T(8,128)(2,1)S(1)}, bf16[2,64,512]{2,1,0:T(8,128)(2,1)S(1)}, u32[]{:S(2)}, u32[]{:S(2)}) collective-permute-start(bf16[2,64,512]{2,1,0:T(8,128)(2,1)S(1)} %get-tuple-element.52), channel_id=1, source_target_pairs={{0,1},{1,0},{2,3},{3,2},{4,5},{5,4},{6,7},{7,6},{8,9},{9,8},{10,11... | collective-permute-start | bytes 393224 | tf_op jit(solution)/shard_map/ppermute | solution.py:45
  6.4 1.0 %copy-start.1 = (bf16[2,2,64,512]{3,2,1,0:T(8,128)(2,1)S(1)}, bf16[2,2,64,512]{3,2,1,0:T(8,128)(2,1)}, u32[]{:S(2)}) copy-start(bf16[2,2,64,512]{3,2,1,0:T(8,128)(2,1)} %vol_ref.1) | copy-start | bytes 786436
  8.6 5.1 %copy-start = (bf16[27,256,128]{2,1,0:T(8,128)(2,1)S(1)}, bf16[27,256,128]{2,1,0:T(8,128)(2,1)}, u32[]{:S(2)}) copy-start(bf16[27,256,128]{2,1,0:T(8,128)(2,1)} %weight_ref.3) | copy-start | bytes 5308420
  8.6 6.7 %copy-start.2 = (bf16[1,2,256,128]{3,2,1,0:T(8,128)(2,1)S(1)}, bf16[1,2,256,128]{3,2,1,0:T(8,128)(2,1)}, u32[]{:S(2)}) copy-start(bf16[1,2,256,128]{3,2,1,0:T(8,128)(2,1)} %param.5) | copy-start | bytes 393220
  10.2 4.2 %collective-permute-start.3 = (bf16[128,256]{1,0:T(8,128)(2,1)S(1)}, bf16[128,256]{1,0:T(8,128)(2,1)S(1)}, u32[]{:S(2)}, u32[]{:S(2)}) collective-permute-start(bf16[128,256]{1,0:T(8,128)(2,1)S(1)} %get-tuple-element.29.pooled_ref), channel_id=1, source_target_pairs={{0,32},{1,2},{2,1},{3,4},{4,3},{5,6},{6,5},{7,8},{8,7},{9,10},{10,... | collective-permute-start | bytes 196616 | tf_op jit(solution)/shard_map/ppermute | solution.py:45
  11.5 3.8 %collective-permute-start.2 = (bf16[128,256]{1,0:T(8,128)(2,1)S(1)}, bf16[128,256]{1,0:T(8,128)(2,1)S(1)}, u32[]{:S(2)}, u32[]{:S(2)}) collective-permute-start(bf16[128,256]{1,0:T(8,128)(2,1)S(1)} %get-tuple-element.29.pooled_ref), channel_id=1, source_target_pairs={{0,1},{1,0},{2,3},{3,2},{4,5},{5,4},{6,7},{7,6},{8,9},{9,8},{10,11... | collective-permute-start | bytes 196616 | tf_op jit(solution)/shard_map/ppermute | solution.py:45
  17.1 5.1 %collective-permute-start.4 = (bf16[448,256]{1,0:T(8,128)(2,1)S(1)}, bf16[448,256]{1,0:T(8,128)(2,1)S(1)}, u32[]{:S(2)}, u32[]{:S(2)}) collective-permute-start(bf16[448,256]{1,0:T(8,128)(2,1)S(1)} %get-tuple-element.33), channel_id=1, source_target_pairs={{0,64},{32,96},{64,0},{96,32},{1,65},{33,97},{65,1},{97,33},{2,66}... | collective-permute-start | bytes 688136 | tf_op jit(solution)/shard_map/ppermute | solution.py:55
  17.7 9.2 %collective-permute-start.5 = (bf16[128,256]{1,0:T(8,128)(2,1)S(1)}, bf16[128,256]{1,0:T(8,128)(2,1)S(1)}, u32[]{:S(2)}, u32[]{:S(2)}) collective-permute-start(bf16[128,256]{1,0:T(8,128)(2,1)S(1)} %get-tuple-element.36), channel_id=1, source_target_pairs={{0,1},{1,0},{2,3},{3,2},{4,5},{5,4},{6,7},{7,6},{8,9},{9,8},{10,11... | collective-permute-start | bytes 196616 | tf_op jit(solution)/shard_map/ppermute | solution.py:45
  19.2 7.6 %collective-permute-start.6 = (bf16[128,256]{1,0:T(8,128)(2,1)S(1)}, bf16[128,256]{1,0:T(8,128)(2,1)S(1)}, u32[]{:S(2)}, u32[]{:S(2)}) collective-permute-start(bf16[128,256]{1,0:T(8,128)(2,1)S(1)} %get-tuple-element.37), channel_id=1, source_target_pairs={{0,32},{1,2},{2,1},{3,4},{4,3},{5,6},{6,5},{7,8},{8,7},{9,10},{10,... | collective-permute-start | bytes 196616 | tf_op jit(solution)/shard_map/ppermute | solution.py:45
  22.8 5.8 %collective-permute-start.8 = (bf16[640,256]{1,0:T(8,128)(2,1)S(1)}, bf16[640,256]{1,0:T(8,128)(2,1)S(1)}, u32[]{:S(2)}, u32[]{:S(2)}) collective-permute-start(bf16[640,256]{1,0:T(8,128)(2,1)S(1)} %get-tuple-element.42), channel_id=1, source_target_pairs={{0,32},{32,0},{64,96},{96,64},{1,33},{33,1},{65,97},{97,65},{2,34}... | collective-permute-start | bytes 983048 | tf_op jit(solution)/shard_map/ppermute | solution.py:50
  28.6 1.6 %collective-permute-start.7 = (bf16[54,16,128]{2,1,0:T(8,128)(2,1)S(1)}, bf16[54,16,128]{2,1,0:T(8,128)(2,1)S(1)}, u32[]{:S(2)}, u32[]{:S(2)}) collective-permute-start(bf16[54,16,128]{2,1,0:T(8,128)(2,1)S(1)} %get-tuple-element.41), channel_id=1, source_target_pairs={{0,32},{32,0},{64,96},{96,64},{1,33},{33,1},{65,97},{97,65},{2,34}... | collective-permute-start | bytes 663560 | tf_op jit(solution)/shard_map/ppermute | solution.py:50
  78.7 4.3 %collective-permute-start.9 = (bf16[64,24,128]{2,1,0:T(8,128)(2,1)S(1)}, bf16[64,24,128]{2,1,0:T(8,128)(2,1)S(1)}, u32[]{:S(2)}, u32[]{:S(2)}) collective-permute-start(bf16[64,24,128]{2,1,0:T(8,128)(2,1)S(1)} %all_to_all.11.rows_ref), channel_id=1, source_target_pairs={{0,32},{32,0},{64,96},{96,64},{1,33},{33,1},{65,97},{97,65},{2,34}... | collective-permute-start | bytes 1179656 | tf_op jit(solution)/shard_map/ppermute | solution.py:50

commit v7 on v6

--- a/solution.py
+++ b/solution.py
@@ -459,55 +459,57 @@
     return call(sum_kernel, "sums", (((16, 128), BF16), ((128, 128), BF16)), (parts,))
 
 
-def place_rows(rows_ref, weight4_ref, weight5_ref, side, half4_ref, half5_ref, sems):
+def place_rows(rows4_ref, rows5_ref, weight4_ref, weight5_ref, side, half4_ref, half5_ref, sems):
     first = lax.axis_index("space") % 16 * 4
-    share = 27 * 64 // rows_ref.shape[0]
-    row = lax.broadcasted_iota(jnp.int32, (4, 128), 0)
+    share = 27 * 64 // rows4_ref.shape[0]
+    row = lax.broadcasted_iota(jnp.int32, (8, 128), 0)
     for o in range(27):
         for k in range(2):
-            half4_ref[o, pl.ds(k * 16, 16), :] = rows_ref[2 * o + k].astype(F32)[:16]
+            half4_ref[o, pl.ds(k * 16, 16), :] = rows4_ref[2 * o + k].astype(F32)
     at = pl.multiple_of(side * 32, 32)
     copy4 = pltpu.make_async_copy(half4_ref, weight4_ref.at[:, pl.ds(at, 32), :], sems.at[0])
     copy4.start()
     for o in range(27):
         start = o * 64 + first
         owner = start // share
-        low = rows_ref[owner].astype(F32)[16:20]
-        high = rows_ref[(start + 3) // share].astype(F32)[16:20]
-        half5_ref[o] = jnp.where(row < (owner + 1) * share - start, low, high)
+        low, high = rows5_ref[owner], rows5_ref[(start + 3) // share]
+        half5_ref[o] = jnp.where(row < (owner + 1) * share - start, low, high)[:4]
     at = pl.multiple_of(side * 128, 128)
-    copy5 = pltpu.make_async_copy(half5_ref, weight5_ref.at[:, :, pl.ds(at, 128)], sems.at[1])
+    copy5 = pltpu.make_async_copy(
+        half5_ref.at[pl.ds(0, 27)], weight5_ref.at[:, :, pl.ds(at, 128)], sems.at[1]
+    )
     copy5.start()
     copy4.wait()
     copy5.wait()
 
 
-def first_half_kernel(rows_ref, weight4_ref, weight5_ref, *scratch):
-    place_rows(rows_ref, weight4_ref, weight5_ref, lax.axis_index("dp") % 2, *scratch)
-
-
-def second_half_kernel(rows_ref, _, __, weight4_ref, weight5_ref, *scratch):
-    place_rows(rows_ref, weight4_ref, weight5_ref, 1 - lax.axis_index("dp") % 2, *scratch)
+def first_half_kernel(rows4_ref, rows5_ref, weight4_ref, weight5_ref, *scratch):
+    place_rows(rows4_ref, rows5_ref, weight4_ref, weight5_ref, lax.axis_index("dp") % 2, *scratch)
+
+
+def second_half_kernel(rows4_ref, rows5_ref, _, __, weight4_ref, weight5_ref, *scratch):
+    place_rows(rows4_ref, rows5_ref, weight4_ref, weight5_ref, 1 - lax.axis_index("dp") % 2, *scratch)
 
 
 def placed_half(kernel, name, rows, *halves):
     anywhere = pl.BlockSpec(memory_space=pl.ANY)
+    near = [rows[:, :16], rows[:, 16:].astype(F32)]
     return pl.pallas_call(
         kernel,
         out_shape=(
             jax.ShapeDtypeStruct((27, 64, 128), F32),
             jax.ShapeDtypeStruct((27, 4, 256), F32),
         ),
-        in_specs=[VMEM] + [anywhere] * len(halves),
+        in_specs=[VMEM] * 2 + [anywhere] * len(halves),
         out_specs=(anywhere, anywhere),
         scratch_shapes=[
             pltpu.VMEM((27, 32, 128), F32),
-            pltpu.VMEM((27, 4, 128), F32),
+            pltpu.VMEM((32, 4, 128), F32),
             pltpu.SemaphoreType.DMA((2,)),
         ],
-        input_output_aliases={i + 1: i for i in range(len(halves))},
+        input_output_aliases={i + 2: i for i in range(len(halves))},
         name=name,
-    )(pltpu.with_memory_space_constraint(rows, pltpu.VMEM), *halves)
+    )(*[pltpu.with_memory_space_constraint(x, pltpu.VMEM) for x in near], *halves)
 
 
 def per_device(volumes, cotangent, conv4_weight, conv5_weight):

time: 84.2 us -> 84.3 us (level)
  no operation moved by 1% of the time
where the time goes in v7:
time: 84.3 us; the launch traced here: 84 us
  blocking collectives  48.3 us (57%)
  starting transfers between devices  18.6 us (22%)
  Pallas kernels  11.5 us (14%)
  local copies, waits for them, and re-layouts  3.26 us (4%)
  waiting for transfers between devices  1.49 us (2%)
  between operations  0.85 us (1%)
    all_to_all x2, blocking collectives, exchange(): lax.all_to_all(parts, axes, split_axis=0, concat_axis=0, tiled=True, axis...  48.3 us
    ppermute x6, starting transfers between devices, swapped(): return lax.ppermute(values, ('dp', 'space'), pairs)  11.5 us
    pallas_call x9, Pallas kernels, call(): pl.pallas_call(kernel, out_shape=tuple((pltpu.VMEM(shape, dtype) for shap...  8.84 us
    ppermute x3, starting transfers between devices, other_core(): return lax.ppermute(values, 'dp', [(i, i ^ 1) for i in range(count)])  6.56 us
    pallas_call x2, Pallas kernels, placed_half(): pl.pallas_call(kernel, out_shape=(jax.ShapeDtypeStruct((27, 64, 128), F32...  1.94 us
  transfers between devices with their start and end apart: 10, of which 3 were waited for; matrix products, arithmetic and copies ran while one was open for 1% of the time, Pallas kernels for 8%

profile of v7, /device:TPU:1, one launch (start us, length us, event | category | flops | bytes accessed | tf_op | source)
XLA Modules:
  0.0 84.0 jit_solution(15294514836378949342)
XLA Ops:
  0.6 1.0 %dynamic-slice_bitcast_fusion = (bf16[2,64,512]{2,1,0:T(8,128)(2,1)S(1)}, bf16[2,64,512]{2,1,0:T(8,128)(2,1)S(1)}) fusion(bf16[2,2,64,512]{3,2,1,0:T(8,128)(2,1)} %vol_ref.1, s32[]{:T(128)S(6)} %select_n.16, s32[]{:T(128)S(6)} %select_n.15), kind=kLoop, calls=%fused_computation.3 | loop fusion | bytes 524296 | tf_op jit(solution)/shard_map/jit(dynamic_index_in_dim)/squeeze | solution.py:518
  1.6 1.5 %collective-permute-start.1 = (bf16[2,64,512]{2,1,0:T(8,128)(2,1)S(1)}, bf16[2,64,512]{2,1,0:T(8,128)(2,1)S(1)}, u32[]{:S(2)}, u32[]{:S(2)}) collective-permute-start(bf16[2,64,512]{2,1,0:T(8,128)(2,1)S(1)} %get-tuple-element.51), channel_id=1, source_target_pairs={{0,32},{1,2},{2,1},{3,4},{4,3},{5,6},{6,5},{7,8},{8,7},{9,10},{10,... | collective-permute-start | bytes 393224 | tf_op jit(solution)/shard_map/ppermute | solution.py:45
  3.1 2.0 %collective-permute-start = (bf16[2,64,512]{2,1,0:T(8,128)(2,1)S(1)}, bf16[2,64,512]{2,1,0:T(8,128)(2,1)S(1)}, u32[]{:S(2)}, u32[]{:S(2)}) collective-permute-start(bf16[2,64,512]{2,1,0:T(8,128)(2,1)S(1)} %get-tuple-element.52), channel_id=1, source_target_pairs={{0,1},{1,0},{2,3},{3,2},{4,5},{5,4},{6,7},{7,6},{8,9},{9,8},{10,11... | collective-permute-start | bytes 393224 | tf_op jit(solution)/shard_map/ppermute | solution.py:45
  5.1 1.2 %copy.15.weight_ref = bf16[128,1728]{1,0:T(8,128)(2,1)S(1)} copy(bf16[128,1728]{0,1:T(8,128)(2,1)} %bitcast.17) | data formatting | bytes 884736 | tf_op jit(solution)/shard_map/reshape | solution.py:519
  6.4 0.9 %copy-done.1 = bf16[2,2,64,512]{3,2,1,0:T(8,128)(2,1)S(1)} copy-done((bf16[2,2,64,512]{3,2,1,0:T(8,128)(2,1)S(1)}, bf16[2,2,64,512]{3,2,1,0:T(8,128)(2,1)}, u32[]{:S(2)}) %copy-start.1) | copy-done | bytes 262168
  7.3 1.3 %own4.1 = (f32[2,128,1024]{2,1,0:T(8,128)S(1)}, bf16[2304,1024]{1,0:T(8,128)(2,1)S(1)}) custom-call(bf16[2,2,64,512]{3,2,1,0:T(8,128)(2,1)S(1)} %copy-done.1, bf16[128,1728]{1,0:T(8,128)(2,1)S(1)} %copy.15.weight_ref), custom_call_target="tpu_custom_call" | custom-call | flops 905969664 | bytes 704512 | tf_op jit(solution)/shard_map/own4/pallas_call | solution.py:18
  8.7 1.5 %layer4.1 = (bf16[128,256]{1,0:T(8,128)(2,1)S(1)}, f32[2,128,1024]{2,1,0:T(8,128)S(1)}, bf16[2304,1024]{1,0:T(8,128)(2,1)S(1)}) custom-call(bf16[2,64,512]{2,1,0:T(8,128)(2,1)S(1)} %collective-permute-done.first_ref, bf16[2,64,512]{2,1,0:T(8,128)(2,1)S(1)} %collective-permute-done.1.second_ref, ...), custom_call_target="tpu_custom_call", output_to_operand_aliasing={{1}: (3, {}), {2}: (4, {})} | custom-call | flops 452984832 | bytes 6471680 | tf_op jit(solution)/shard_map/layer4/pallas_call | solution.py:18
  10.2 1.3 %collective-permute-start.3 = (bf16[128,256]{1,0:T(8,128)(2,1)S(1)}, bf16[128,256]{1,0:T(8,128)(2,1)S(1)}, u32[]{:S(2)}, u32[]{:S(2)}) collective-permute-start(bf16[128,256]{1,0:T(8,128)(2,1)S(1)} %get-tuple-element.29.pooled_ref), channel_id=1, source_target_pairs={{0,32},{1,2},{2,1},{3,4},{4,3},{5,6},{6,5},{7,8},{8,7},{9,10},{10,... | collective-permute-start | bytes 196616 | tf_op jit(solution)/shard_map/ppermute | solution.py:45
  11.5 2.2 %collective-permute-start.2 = (bf16[128,256]{1,0:T(8,128)(2,1)S(1)}, bf16[128,256]{1,0:T(8,128)(2,1)S(1)}, u32[]{:S(2)}, u32[]{:S(2)}) collective-permute-start(bf16[128,256]{1,0:T(8,128)(2,1)S(1)} %get-tuple-element.29.pooled_ref), channel_id=1, source_target_pairs={{0,1},{1,0},{2,3},{3,2},{4,5},{5,4},{6,7},{7,6},{8,9},{9,8},{10,11... | collective-permute-start | bytes 196616 | tf_op jit(solution)/shard_map/ppermute | solution.py:45
  13.7 0.7 own5.1
  14.4 1.0 %collective-permute-done.2.first_ref = bf16[128,256]{1,0:T(8,128)(2,1)S(1)} collective-permute-done((bf16[128,256]{1,0:T(8,128)(2,1)S(1)}, bf16[128,256]{1,0:T(8,128)(2,1)S(1)}, u32[]{:S(2)}, u32[]{:S(2)}) %collective-permute-start.2) | collective-permute-done | bytes 65568 | tf_op jit(solution)/shard_map/ppermute | solution.py:45
  15.3 1.7 %layer5.1 = (bf16[2,256,128]{2,1,0:T(8,128)(2,1)S(1)}, bf16[128,256]{1,0:T(8,128)(2,1)S(1)}, bf16[128,256]{1,0:T(8,128)(2,1)S(1)}, bf16[448,256]{1,0:T(8,128)(2,1)S(1)}, bf16[448,256]{1,0:T(8,128)(2,1)S(1)}) custom-call(bf16[128,256]{1,0:T(8,128)(2,1)S(1)} %get-tuple-element.29.pooled_ref, bf16[128,256]{1,0:T(8,128)(2,1)S(1)} %collective-permute-done.2.first_ref, ...), custom_call_target="tpu_custom_call" | custom-call | flops 679477248 | bytes 4128768 | tf_op jit(solution)/shard_map/layer5/pallas_call | solution.py:18
  17.1 0.6 collective-permute-start.4
  17.7 1.6 %collective-permute-start.5 = (bf16[128,256]{1,0:T(8,128)(2,1)S(1)}, bf16[128,256]{1,0:T(8,128)(2,1)S(1)}, u32[]{:S(2)}, u32[]{:S(2)}) collective-permute-start(bf16[128,256]{1,0:T(8,128)(2,1)S(1)} %get-tuple-element.36), channel_id=1, source_target_pairs={{0,1},{1,0},{2,3},{3,2},{4,5},{5,4},{6,7},{7,6},{8,9},{9,8},{10,11... | collective-permute-start | bytes 196616 | tf_op jit(solution)/shard_map/ppermute | solution.py:45
  19.2 2.9 %collective-permute-start.6 = (bf16[128,256]{1,0:T(8,128)(2,1)S(1)}, bf16[128,256]{1,0:T(8,128)(2,1)S(1)}, u32[]{:S(2)}, u32[]{:S(2)}) collective-permute-start(bf16[128,256]{1,0:T(8,128)(2,1)S(1)} %get-tuple-element.37), channel_id=1, source_target_pairs={{0,32},{1,2},{2,1},{3,4},{4,3},{5,6},{6,5},{7,8},{8,7},{9,10},{10,... | collective-permute-start | bytes 196616 | tf_op jit(solution)/shard_map/ppermute | solution.py:45
  22.1 0.7 regroup.1
  22.8 3.5 %collective-permute-start.8 = (bf16[640,256]{1,0:T(8,128)(2,1)S(1)}, bf16[640,256]{1,0:T(8,128)(2,1)S(1)}, u32[]{:S(2)}, u32[]{:S(2)}) collective-permute-start(bf16[640,256]{1,0:T(8,128)(2,1)S(1)} %get-tuple-element.42), channel_id=1, source_target_pairs={{0,32},{32,0},{64,96},{96,64},{1,33},{33,1},{65,97},{97,65},{2,34}... | collective-permute-start | bytes 983048 | tf_op jit(solution)/shard_map/ppermute | solution.py:50
  26.9 1.7 %weight4_parts.1 = (f32[54,16,128]{2,1,0:T(8,128)S(1)}, bf16[54,16,128]{2,1,0:T(8,128)(2,1)S(1)}) custom-call(f32[128,256]{1,0:T(8,128)S(1)} %own_inward.1.inward_ref, bf16[128,256]{1,0:T(8,128)(2,1)S(1)} %collective-permute-done.5.first_ref, bf16[128,256]{1,0:T(8,128)(2,1)S(1)} %collective-permute-done.6.second_ref, ...), custom_call_target="tpu_custom_call" | custom-call | flops 905969664 | bytes 6029312 | tf_op jit(solution)/shard_map/weight4_parts/pallas_call | solution.py:18
  28.7 1.3 %weight5.1 = (bf16[64,48,128]{2,1,0:T(8,128)(2,1)S(1)}, bf16[1728,1024]{1,0:T(8,128)(2,1)S(1)}) custom-call(bf16[448,256]{1,0:T(8,128)(2,1)S(1)} %get-tuple-element.32.mine_ref, bf16[448,256]{1,0:T(8,128)(2,1)S(1)} %collective-permute-done.4.got_ref.chip_ref, bf16[640,256]{1,0:T(8,128)(2,1)S(1)} %collective-permute-done.8.core_ref, ...), custom_call_target="tpu_custom_call", output_to_operand_aliasing={{1}: (3, {})} | custom-call | flops 452984832 | bytes 4325376 | tf_op jit(solution)/shard_map/weight5/pallas_call | solution.py:18
  30.2 32.5 %all_to_all.10.parts_ref = bf16[64,48,128]{2,1,0:T(8,128)(2,1)S(1)} all-to-all(bf16[64,48,128]{2,1,0:T(8,128)(2,1)S(1)} %pairs.1), channel_id=1, replica_groups={{0,1,2,3,4,5,6,7,8,9,10,11,12,13,14,15,16,17,18,19,20,21,22,23,24,25,26..., dimensions={0} | all-to-all | bytes 1572864 | tf_op jit(solution)/shard_map/all_to_all | solution.py:541
  62.9 15.7 %all_to_all.11 = bf16[64,24,128]{2,1,0:T(8,128)(2,1)S(1)} all-to-all(bf16[64,24,128]{2,1,0:T(8,128)(2,1)S(1)} %pad_maximum_fusion), channel_id=1, replica_groups={{0,1,2,3,4,5,6,7,8,9,10,11,12,13,14,15,16,17,18,19,20,21,22,23,24,25,26..., dimensions={0} | all-to-all | bytes 786432 | tf_op jit(solution)/shard_map/all_to_all | solution.py:541
  78.7 3.0 %collective-permute-start.9 = (bf16[64,24,128]{2,1,0:T(8,128)(2,1)S(1)}, bf16[64,24,128]{2,1,0:T(8,128)(2,1)S(1)}, u32[]{:S(2)}, u32[]{:S(2)}) collective-permute-start(bf16[64,24,128]{2,1,0:T(8,128)(2,1)S(1)} %all_to_all.11), channel_id=1, source_target_pairs={{0,32},{32,0},{64,96},{96,64},{1,33},{33,1},{65,97},{97,65},{2,34}... | collective-permute-start | bytes 1179656 | tf_op jit(solution)/shard_map/ppermute | solution.py:50
  81.7 1.0 %first_half.1 = (f32[27,64,128]{2,1,0:T(8,128)}, f32[27,4,256]{2,1,0:T(4,128)}) custom-call(bf16[64,16,128]{2,1,0:T(8,128)(2,1)S(1)} %slice.18.rows4_ref, f32[64,8,128]{2,1,0:T(8,128)S(1)} %slice_convert_fusion.rows5_ref), custom_call_target="tpu_custom_call" | custom-call | tf_op jit(solution)/shard_map/first_half/pallas_call | solution.py:497
  83.0 1.0 %second_half.1 = (f32[27,64,128]{2,1,0:T(8,128)}, f32[27,4,256]{2,1,0:T(4,128)}) custom-call(bf16[64,16,128]{2,1,0:T(8,128)(2,1)S(1)} %slice.16.rows4_ref, f32[64,8,128]{2,1,0:T(8,128)S(1)} %slice_convert_fusion.1.rows5_ref, f32[27,64,128]{2,1,0:T(8,128)} %get-tuple-element.47._, ...), custom_call_target="tpu_custom_call", output_to_operand_aliasing={{0}: (2, {}), {1}: (3, {})} | custom-call | tf_op jit(solution)/shard_map/second_half/pallas_call | solution.py:497
  (26 shorter events, 1.5 us)
Async XLA Ops:
  1.6 7.0 %collective-permute-start.1 = (bf16[2,64,512]{2,1,0:T(8,128)(2,1)S(1)}, bf16[2,64,512]{2,1,0:T(8,128)(2,1)S(1)}, u32[]{:S(2)}, u32[]{:S(2)}) collective-permute-start(bf16[2,64,512]{2,1,0:T(8,128)(2,1)S(1)} %get-tuple-element.51), channel_id=1, source_target_pairs={{0,32},{1,2},{2,1},{3,4},{4,3},{5,6},{6,5},{7,8},{8,7},{9,10},{10,... | collective-permute-start | bytes 393224 | tf_op jit(solution)/shard_map/ppermute | solution.py:45
  3.1 5.5 %collective-permute-start = (bf16[2,64,512]{2,1,0:T(8,128)(2,1)S(1)}, bf16[2,64,512]{2,1,0:T(8,128)(2,1)S(1)}, u32[]{:S(2)}, u32[]{:S(2)}) collective-permute-start(bf16[2,64,512]{2,1,0:T(8,128)(2,1)S(1)} %get-tuple-element.52), channel_id=1, source_target_pairs={{0,1},{1,0},{2,3},{3,2},{4,5},{5,4},{6,7},{7,6},{8,9},{9,8},{10,11... | collective-permute-start | bytes 393224 | tf_op jit(solution)/shard_map/ppermute | solution.py:45
  6.4 1.0 %copy-start.1 = (bf16[2,2,64,512]{3,2,1,0:T(8,128)(2,1)S(1)}, bf16[2,2,64,512]{3,2,1,0:T(8,128)(2,1)}, u32[]{:S(2)}) copy-start(bf16[2,2,64,512]{3,2,1,0:T(8,128)(2,1)} %vol_ref.1) | copy-start | bytes 786436
  8.6 5.1 %copy-start = (bf16[27,256,128]{2,1,0:T(8,128)(2,1)S(1)}, bf16[27,256,128]{2,1,0:T(8,128)(2,1)}, u32[]{:S(2)}) copy-start(bf16[27,256,128]{2,1,0:T(8,128)(2,1)} %weight_ref.3) | copy-start | bytes 5308420
  8.6 6.7 %copy-start.2 = (bf16[1,2,256,128]{3,2,1,0:T(8,128)(2,1)S(1)}, bf16[1,2,256,128]{3,2,1,0:T(8,128)(2,1)}, u32[]{:S(2)}) copy-start(bf16[1,2,256,128]{3,2,1,0:T(8,128)(2,1)} %param.5) | copy-start | bytes 393220
  10.2 4.2 %collective-permute-start.3 = (bf16[128,256]{1,0:T(8,128)(2,1)S(1)}, bf16[128,256]{1,0:T(8,128)(2,1)S(1)}, u32[]{:S(2)}, u32[]{:S(2)}) collective-permute-start(bf16[128,256]{1,0:T(8,128)(2,1)S(1)} %get-tuple-element.29.pooled_ref), channel_id=1, source_target_pairs={{0,32},{1,2},{2,1},{3,4},{4,3},{5,6},{6,5},{7,8},{8,7},{9,10},{10,... | collective-permute-start | bytes 196616 | tf_op jit(solution)/shard_map/ppermute | solution.py:45
  11.5 3.8 %collective-permute-start.2 = (bf16[128,256]{1,0:T(8,128)(2,1)S(1)}, bf16[128,256]{1,0:T(8,128)(2,1)S(1)}, u32[]{:S(2)}, u32[]{:S(2)}) collective-permute-start(bf16[128,256]{1,0:T(8,128)(2,1)S(1)} %get-tuple-element.29.pooled_ref), channel_id=1, source_target_pairs={{0,1},{1,0},{2,3},{3,2},{4,5},{5,4},{6,7},{7,6},{8,9},{9,8},{10,11... | collective-permute-start | bytes 196616 | tf_op jit(solution)/shard_map/ppermute | solution.py:45
  17.1 5.1 %collective-permute-start.4 = (bf16[448,256]{1,0:T(8,128)(2,1)S(1)}, bf16[448,256]{1,0:T(8,128)(2,1)S(1)}, u32[]{:S(2)}, u32[]{:S(2)}) collective-permute-start(bf16[448,256]{1,0:T(8,128)(2,1)S(1)} %get-tuple-element.33), channel_id=1, source_target_pairs={{0,64},{32,96},{64,0},{96,32},{1,65},{33,97},{65,1},{97,33},{2,66}... | collective-permute-start | bytes 688136 | tf_op jit(solution)/shard_map/ppermute | solution.py:55
  17.7 9.2 %collective-permute-start.5 = (bf16[128,256]{1,0:T(8,128)(2,1)S(1)}, bf16[128,256]{1,0:T(8,128)(2,1)S(1)}, u32[]{:S(2)}, u32[]{:S(2)}) collective-permute-start(bf16[128,256]{1,0:T(8,128)(2,1)S(1)} %get-tuple-element.36), channel_id=1, source_target_pairs={{0,1},{1,0},{2,3},{3,2},{4,5},{5,4},{6,7},{7,6},{8,9},{9,8},{10,11... | collective-permute-start | bytes 196616 | tf_op jit(solution)/shard_map/ppermute | solution.py:45
  19.2 7.6 %collective-permute-start.6 = (bf16[128,256]{1,0:T(8,128)(2,1)S(1)}, bf16[128,256]{1,0:T(8,128)(2,1)S(1)}, u32[]{:S(2)}, u32[]{:S(2)}) collective-permute-start(bf16[128,256]{1,0:T(8,128)(2,1)S(1)} %get-tuple-element.37), channel_id=1, source_target_pairs={{0,32},{1,2},{2,1},{3,4},{4,3},{5,6},{6,5},{7,8},{8,7},{9,10},{10,... | collective-permute-start | bytes 196616 | tf_op jit(solution)/shard_map/ppermute | solution.py:45
  22.8 5.8 %collective-permute-start.8 = (bf16[640,256]{1,0:T(8,128)(2,1)S(1)}, bf16[640,256]{1,0:T(8,128)(2,1)S(1)}, u32[]{:S(2)}, u32[]{:S(2)}) collective-permute-start(bf16[640,256]{1,0:T(8,128)(2,1)S(1)} %get-tuple-element.42), channel_id=1, source_target_pairs={{0,32},{32,0},{64,96},{96,64},{1,33},{33,1},{65,97},{97,65},{2,34}... | collective-permute-start | bytes 983048 | tf_op jit(solution)/shard_map/ppermute | solution.py:50
  28.6 1.6 %collective-permute-start.7 = (bf16[54,16,128]{2,1,0:T(8,128)(2,1)S(1)}, bf16[54,16,128]{2,1,0:T(8,128)(2,1)S(1)}, u32[]{:S(2)}, u32[]{:S(2)}) collective-permute-start(bf16[54,16,128]{2,1,0:T(8,128)(2,1)S(1)} %get-tuple-element.41), channel_id=1, source_target_pairs={{0,32},{32,0},{64,96},{96,64},{1,33},{33,1},{65,97},{97,65},{2,34}... | collective-permute-start | bytes 663560 | tf_op jit(solution)/shard_map/ppermute | solution.py:50
  78.7 4.3 %collective-permute-start.9 = (bf16[64,24,128]{2,1,0:T(8,128)(2,1)S(1)}, bf16[64,24,128]{2,1,0:T(8,128)(2,1)S(1)}, u32[]{:S(2)}, u32[]{:S(2)}) collective-permute-start(bf16[64,24,128]{2,1,0:T(8,128)(2,1)S(1)} %all_to_all.11), channel_id=1, source_target_pairs={{0,32},{32,0},{64,96},{96,64},{1,33},{33,1},{65,97},{97,65},{2,34}... | collective-permute-start | bytes 1179656 | tf_op jit(solution)/shard_map/ppermute | solution.py:50

commit v8 on v7

--- a/solution.py
+++ b/solution.py
@@ -130,7 +130,7 @@
 
 
 def layer4_kernel(
-    first_ref, second_ref, weight_ref, part_ref, _, pooled_ref, slope_ref, stack_ref
+    first_ref, second_ref, weight_ref, part_ref, _, pooled_ref, preact_ref, stack_ref
 ):
     chans, cells = first_ref.shape[1:]
     rows = len(TAPS) * chans
@@ -147,9 +147,8 @@
                 weight_ref[:, 2 * d * rows : (2 * d + 1) * rows],
                 stack_ref[pl.ds(3 * d * rows, rows), lanes],
             )
-            sig = jax.nn.sigmoid(preact)
-            slope_ref[d, :, lanes] = sig * (1.0 + preact * (1.0 - sig)) * 0.125
-            active = preact * sig
+            preact_ref[d, :, lanes] = preact
+            active = preact * jax.nn.sigmoid(preact)
             total = active if total is None else total + active
         high = total.astype(BF16)
         low = (total - high.astype(F32)).astype(BF16)
@@ -201,7 +200,11 @@
     return total
 
 
-def own5_kernel(pooled_ref, weight_ref, part_ref, back_ref):
+def own5_kernel(pooled_ref, weight_ref, preact4_ref, part_ref, back_ref, slope_ref):
+    for d in range(2):
+        preact = preact4_ref[d]
+        sig = jax.nn.sigmoid(preact)
+        slope_ref[d] = sig * (1.0 + preact * (1.0 - sig)) * 0.125
     chans = pooled_ref.shape[0]
     cells = pooled_ref.shape[1] // 2
     part_ref[...] = convolved5(weight_ref, pooled_ref[...], cells, 0)
@@ -210,14 +213,15 @@
         back_ref[t, pl.ds((0, 2, 1)[a] * chans, chans), :] = weight_ref[o].T
 
 
-def own5(pooled, weight):
+def own5(pooled, weight, preact4):
     chans, lanes = pooled.shape
     outer = weight.shape[1]
     return call(
         own5_kernel,
         "own5",
-        (((outer, lanes), F32), ((len(TAPS), 3 * chans, outer), BF16)),
-        (pooled, weight),
+        (((outer, lanes), F32), ((len(TAPS), 3 * chans, outer), BF16), (preact4.shape, F32)),
+        (pooled, weight, preact4),
+        aliases={2: 2},
         flops=2 * weight.size * lanes // 3,
     )
 
@@ -229,25 +233,6 @@
         part = dot(back_ref[t, pl.ds(first, rows), :], shifts)
         total = part if total is None else total + part
     return total
-
-
-def own_inward_kernel(mine_ref, back_ref, inward_ref):
-    outer = back_ref.shape[2]
-    chans, lanes = inward_ref.shape
-    grad = mine_ref[pl.ds(0, outer), :]
-    inward_ref[...] = inward_part(back_ref, grad, lanes // 2, 2 * chans, chans)
-
-
-def own_inward(mine, back):
-    chans = back.shape[1] // 3
-    (inward,) = call(
-        own_inward_kernel,
-        "own_inward",
-        (((chans, mine.shape[1]), F32),),
-        (mine, back),
-        flops=2 * back.size * mine.shape[1] // 3,
-    )
-    return inward
 
 
 def layer5_kernel(
@@ -309,7 +294,7 @@
     spread_taps(planes, out_ref.at[:, pl.ds(i * lanes, lanes)], WIDTH // 2, lanes // 2, 1)
 
 
-def regroup_kernel(mine_ref, got_ref, made_ref, send_ref, stack_ref, out_ref, sem):
+def regroup_kernel(mine_ref, got_ref, made_ref, send_ref, out_ref, sem):
     copy = pltpu.make_async_copy(made_ref, out_ref, sem)
     copy.start()
     core = lax.axis_index("dp") % 2
@@ -319,7 +304,6 @@
         start = pl.multiple_of((1 - core) * half, half)
         send_ref[pl.ds(i * rows, half), :] = ref[pl.ds(start, half), :]
         send_ref[pl.ds(i * rows + half, rows - half), :] = ref[pl.ds(2 * half, rows - half), :]
-        stack_window(ref, 2 * half, rows - half, stack_ref, i)
     copy.wait()
 
 
@@ -330,47 +314,77 @@
         regroup_kernel,
         out_shape=(
             pltpu.VMEM((2 * rows, lanes), BF16),
-            pltpu.VMEM((9 * (mine.shape[0] - outer), 4 * lanes), BF16),
             jax.ShapeDtypeStruct(made.shape, made.dtype),
         ),
         in_specs=[VMEM] * 3,
-        out_specs=(VMEM, VMEM, pl.BlockSpec(memory_space=pl.ANY)),
+        out_specs=(VMEM, pl.BlockSpec(memory_space=pl.ANY)),
         scratch_shapes=[pltpu.SemaphoreType.DMA],
         compiler_params=pltpu.CompilerParams(vmem_limit_bytes=12 * 2**20),
         name="regroup",
     )(*[pltpu.with_memory_space_constraint(x, pltpu.VMEM) for x in (mine, got, made)])
 
 
-def weight5_kernel(mine_ref, chip_ref, core_ref, _, part_ref, stack_ref, total_ref):
-    core = lax.axis_index("dp") % 2
-    rows = core_ref.shape[0] // 2
-    half = mine_ref.shape[0] - rows
-    own = pl.ds(pl.multiple_of(core * half, half), half)
-    for i in range(2):
-        stack_window(core_ref, i * rows + half, rows - half, stack_ref, 2 + i)
-    grads = (mine_ref[own, :], chip_ref[own, :], core_ref[pl.ds(0, half), :], core_ref[pl.ds(rows, half), :])
-    grads = jnp.concatenate(grads, axis=1)
+def weight5_sums(sources, stack_ref, total_ref):
+    for i, (_, ref, first, rows) in enumerate(sources):
+        stack_window(ref, first, rows, stack_ref, i)
+    grads = jnp.concatenate([grad for grad, *_ in sources], axis=1)
     block = stack_ref.shape[0] // 3
     for j in range(3):
         at = pl.ds(j * block, block)
         total_ref[at, :] = dot_rows(stack_ref[at, :], grads)
-    total_ref[pl.ds(3 * block, 8), :] = jnp.zeros((8, half), F32)
+
+
+def own_kernel(mine_ref, chip_ref, back_ref, inward_ref, total_ref, stack_ref):
+    core = lax.axis_index("dp") % 2
+    outer = back_ref.shape[2]
+    chans, lanes = inward_ref.shape
+    grad = mine_ref[pl.ds(0, outer), :]
+    inward_ref[...] = inward_part(back_ref, grad, lanes // 2, 2 * chans, chans)
+    own = pl.ds(pl.multiple_of(core * (outer // 2), outer // 2), outer // 2)
+    rows = mine_ref.shape[0] - outer
+    weight5_sums([(ref[own, :], ref, outer, rows) for ref in (mine_ref, chip_ref)], stack_ref, total_ref)
+
+
+def own_parts(mine, chip, back):
+    lanes = mine.shape[1]
+    chans, outer = back.shape[1] // 3, back.shape[2]
+    rows = 9 * (mine.shape[0] - outer)
+    return call(
+        own_kernel,
+        "own_parts",
+        (((chans, lanes), F32), ((rows, outer // 2), F32)),
+        (mine, chip, back),
+        scratch=[pltpu.VMEM((rows, 2 * lanes), BF16)],
+        flops=2 * back.size * lanes // 3 + 2 * rows * lanes * outer,
+    )
+
+
+def weight5_kernel(core_ref, first_ref, part_ref, stack_ref, total_ref):
+    rows, half = core_ref.shape[0] // 2, total_ref.shape[1]
+    sources = [
+        (core_ref[pl.ds(i * rows, half), :], core_ref, i * rows + half, rows - half)
+        for i in range(2)
+    ]
+    weight5_sums(sources, stack_ref, total_ref)
+    filled = first_ref.shape[0]
+    total_ref[pl.ds(0, filled), :] += first_ref[...]
+    total_ref[pl.ds(filled, 8), :] = jnp.zeros((8, half), F32)
     owners = part_ref.shape[0]
     for owner in range(owners):
-        part_ref[owner, pl.ds(16, 32), :] = total_ref[
-            pl.ds(owner * (3 * block // owners), 32), :
-        ].astype(BF16)
-
-
-def weight5_part(mine, chip, core, stack, outer):
-    part, _ = call(
+        part_ref[owner, pl.ds(16, 32), :] = total_ref[pl.ds(owner * (filled // owners), 32), :].astype(
+            BF16
+        )
+
+
+def weight5_part(core, first):
+    rows, half = first.shape
+    (part,) = call(
         weight5_kernel,
         "weight5",
-        (((64, 48, 128), BF16), (stack.shape, BF16)),
-        (mine, chip, core, stack),
-        scratch=[pltpu.VMEM((stack.shape[0] + 8, outer // 2), F32)],
-        flops=stack.size * outer,
-        aliases={3: 1},
+        (((64, 48, 128), BF16),),
+        (core, first),
+        scratch=[pltpu.VMEM((rows, 2 * core.shape[1]), BF16), pltpu.VMEM((rows + 8, half), F32)],
+        flops=4 * rows * core.shape[1] * half,
     )
     return part
 
@@ -518,17 +532,16 @@
     second4 = swapped(lax.dynamic_index_in_dim(volumes, odd, 0, keepdims=False), 1)
     arranged4 = conv4_weight.transpose(1, 0, 2).reshape(conv4_weight.shape[1], -1)
     part4, stack4 = own4(volumes, arranged4)
-    pooled, slope, stack4 = layer4(first4, second4, arranged4, part4, stack4)
-    part5, back5 = own5(pooled, conv5_weight)
+    pooled, preact4, stack4 = layer4(first4, second4, arranged4, part4, stack4)
+    part5, back5, slope = own5(pooled, conv5_weight, preact4)
     output5, to_first, to_second, mine5, share5 = layer5(
         pooled, swapped(pooled, 0), swapped(pooled, 1), conv5_weight, cotangent[0], part5, back5
     )
     first, second = swapped(to_first, 0), swapped(to_second, 1)
-    inward = own_inward(mine5, back5)
-    outer = conv5_weight.shape[1]
     chip5 = other_chip(share5)
-    send5, chips5, output5 = regrouped(mine5, chip5, output5, outer)
-    part = weight5_part(mine5, chip5, other_core(send5), chips5, outer)
+    send5, output5 = regrouped(mine5, chip5, output5, conv5_weight.shape[1])
+    inward, chips5 = own_parts(mine5, chip5, back5)
+    part = weight5_part(other_core(send5), chips5)
     keep, send = weight4_parts(inward, first, second, stack4, slope)
     axes = ("dp", "space")
     spaces, groups = lax.axis_size("space"), lax.axis_size("dp")

time: 84.3 us -> 84.1 us (level)
  transfers between devices with their start and end apart: 10 -> 10, of which waited for: 3 -> 3; matrix products, arithmetic and copies ran while one was open for 1% -> 1% of each run, Pallas kernels for 8% -> 9%
where the time goes in v8:
time: 84.1 us; the launch traced here: 83.8 us
  blocking collectives  47.6 us (57%)
  starting transfers between devices  18.6 us (22%)
  Pallas kernels  11.8 us (14%)
  local copies, waits for them, and re-layouts  3.26 us (4%)
  waiting for transfers between devices  1.61 us (2%)
    all_to_all x2, blocking collectives, exchange(): lax.all_to_all(parts, axes, split_axis=0, concat_axis=0, tiled=True, axis...  47.6 us
    ppermute x6, starting transfers between devices, swapped(): return lax.ppermute(values, ('dp', 'space'), pairs)  11.5 us
    pallas_call x9, Pallas kernels, call(): pl.pallas_call(kernel, out_shape=tuple((pltpu.VMEM(shape, dtype) for shap...  9.15 us
    ppermute x3, starting transfers between devices, other_core(): return lax.ppermute(values, 'dp', [(i, i ^ 1) for i in range(count)])  6.57 us
    pallas_call x2, Pallas kernels, placed_half(): pl.pallas_call(kernel, out_shape=(jax.ShapeDtypeStruct((27, 64, 128), F32...  1.94 us
  transfers between devices with their start and end apart: 10, of which 3 were waited for; matrix products, arithmetic and copies ran while one was open for 1% of the time, Pallas kernels for 9%

profile of v8, /device:TPU:1, one launch (start us, length us, event | category | flops | bytes accessed | tf_op | source)
XLA Modules:
  0.0 83.8 jit_solution(1140018280202983996)
XLA Ops:
  0.6 1.0 %dynamic-slice_bitcast_fusion = (bf16[2,64,512]{2,1,0:T(8,128)(2,1)S(1)}, bf16[2,64,512]{2,1,0:T(8,128)(2,1)S(1)}) fusion(bf16[2,2,64,512]{3,2,1,0:T(8,128)(2,1)} %vol_ref.1, s32[]{:T(128)S(6)} %select_n.16, s32[]{:T(128)S(6)} %select_n.15), kind=kLoop, calls=%fused_computation.3 | loop fusion | bytes 524296 | tf_op jit(solution)/shard_map/jit(dynamic_index_in_dim)/squeeze | solution.py:532
  1.6 1.5 %collective-permute-start.1 = (bf16[2,64,512]{2,1,0:T(8,128)(2,1)S(1)}, bf16[2,64,512]{2,1,0:T(8,128)(2,1)S(1)}, u32[]{:S(2)}, u32[]{:S(2)}) collective-permute-start(bf16[2,64,512]{2,1,0:T(8,128)(2,1)S(1)} %get-tuple-element.53), channel_id=1, source_target_pairs={{0,32},{1,2},{2,1},{3,4},{4,3},{5,6},{6,5},{7,8},{8,7},{9,10},{10,... | collective-permute-start | bytes 393224 | tf_op jit(solution)/shard_map/ppermute | solution.py:45
  3.1 2.0 %collective-permute-start = (bf16[2,64,512]{2,1,0:T(8,128)(2,1)S(1)}, bf16[2,64,512]{2,1,0:T(8,128)(2,1)S(1)}, u32[]{:S(2)}, u32[]{:S(2)}) collective-permute-start(bf16[2,64,512]{2,1,0:T(8,128)(2,1)S(1)} %get-tuple-element.54), channel_id=1, source_target_pairs={{0,1},{1,0},{2,3},{3,2},{4,5},{5,4},{6,7},{7,6},{8,9},{9,8},{10,11... | collective-permute-start | bytes 393224 | tf_op jit(solution)/shard_map/ppermute | solution.py:45
  5.1 1.2 %copy.15.weight_ref = bf16[128,1728]{1,0:T(8,128)(2,1)S(1)} copy(bf16[128,1728]{0,1:T(8,128)(2,1)} %bitcast.17) | data formatting | bytes 884736 | tf_op jit(solution)/shard_map/reshape | solution.py:533
  6.4 0.9 %copy-done.1 = bf16[2,2,64,512]{3,2,1,0:T(8,128)(2,1)S(1)} copy-done((bf16[2,2,64,512]{3,2,1,0:T(8,128)(2,1)S(1)}, bf16[2,2,64,512]{3,2,1,0:T(8,128)(2,1)}, u32[]{:S(2)}) %copy-start.1) | copy-done | bytes 262168
  7.3 1.3 %own4.1 = (f32[2,128,1024]{2,1,0:T(8,128)S(1)}, bf16[2304,1024]{1,0:T(8,128)(2,1)S(1)}) custom-call(bf16[2,2,64,512]{3,2,1,0:T(8,128)(2,1)S(1)} %copy-done.1, bf16[128,1728]{1,0:T(8,128)(2,1)S(1)} %copy.15.weight_ref), custom_call_target="tpu_custom_call" | custom-call | flops 905969664 | bytes 704512 | tf_op jit(solution)/shard_map/own4/pallas_call | solution.py:18
  8.6 1.5 %layer4.1 = (bf16[128,256]{1,0:T(8,128)(2,1)S(1)}, f32[2,128,1024]{2,1,0:T(8,128)S(1)}, bf16[2304,1024]{1,0:T(8,128)(2,1)S(1)}) custom-call(bf16[2,64,512]{2,1,0:T(8,128)(2,1)S(1)} %collective-permute-done.first_ref, bf16[2,64,512]{2,1,0:T(8,128)(2,1)S(1)} %collective-permute-done.1.second_ref, ...), custom_call_target="tpu_custom_call", output_to_operand_aliasing={{1}: (3, {}), {2}: (4, {})} | custom-call | flops 452984832 | bytes 6471680 | tf_op jit(solution)/shard_map/layer4/pallas_call | solution.py:18
  10.1 1.3 %collective-permute-start.3 = (bf16[128,256]{1,0:T(8,128)(2,1)S(1)}, bf16[128,256]{1,0:T(8,128)(2,1)S(1)}, u32[]{:S(2)}, u32[]{:S(2)}) collective-permute-start(bf16[128,256]{1,0:T(8,128)(2,1)S(1)} %get-tuple-element.30.pooled_ref), channel_id=1, source_target_pairs={{0,32},{1,2},{2,1},{3,4},{4,3},{5,6},{6,5},{7,8},{8,7},{9,10},{10,... | collective-permute-start | bytes 196616 | tf_op jit(solution)/shard_map/ppermute | solution.py:45
  11.4 2.2 %collective-permute-start.2 = (bf16[128,256]{1,0:T(8,128)(2,1)S(1)}, bf16[128,256]{1,0:T(8,128)(2,1)S(1)}, u32[]{:S(2)}, u32[]{:S(2)}) collective-permute-start(bf16[128,256]{1,0:T(8,128)(2,1)S(1)} %get-tuple-element.30.pooled_ref), channel_id=1, source_target_pairs={{0,1},{1,0},{2,3},{3,2},{4,5},{5,4},{6,7},{7,6},{8,9},{9,8},{10,11... | collective-permute-start | bytes 196616 | tf_op jit(solution)/shard_map/ppermute | solution.py:45
  13.6 1.0 %own5.1 = (f32[256,256]{1,0:T(8,128)S(1)}, bf16[9,384,256]{2,1,0:T(8,128)(2,1)S(1)}, f32[2,128,1024]{2,1,0:T(8,128)S(1)}) custom-call(bf16[128,256]{1,0:T(8,128)(2,1)S(1)} %get-tuple-element.30.pooled_ref, bf16[27,256,128]{2,1,0:T(8,128)(2,1)S(1)} %copy-done, f32[2,128,1024]{2,1,0:T(8,128)S(1)} %get-tuple-element.31.preact4_ref), custom_call_target="tpu_custom_call", output_to_operand_aliasing={{2}: (2, {})} | custom-call | flops 150994944 | bytes 2883584 | tf_op jit(solution)/shard_map/own5/pallas_call | solution.py:18
  14.6 0.7 collective-permute-done.2.first_ref
  15.3 1.7 %layer5.1 = (bf16[2,256,128]{2,1,0:T(8,128)(2,1)S(1)}, bf16[128,256]{1,0:T(8,128)(2,1)S(1)}, bf16[128,256]{1,0:T(8,128)(2,1)S(1)}, bf16[448,256]{1,0:T(8,128)(2,1)S(1)}, bf16[448,256]{1,0:T(8,128)(2,1)S(1)}) custom-call(bf16[128,256]{1,0:T(8,128)(2,1)S(1)} %get-tuple-element.30.pooled_ref, bf16[128,256]{1,0:T(8,128)(2,1)S(1)} %collective-permute-done.2.first_ref, ...), custom_call_target="tpu_custom_call" | custom-call | flops 679477248 | bytes 4128768 | tf_op jit(solution)/shard_map/layer5/pallas_call | solution.py:18
  17.6 1.6 %collective-permute-start.5 = (bf16[128,256]{1,0:T(8,128)(2,1)S(1)}, bf16[128,256]{1,0:T(8,128)(2,1)S(1)}, u32[]{:S(2)}, u32[]{:S(2)}) collective-permute-start(bf16[128,256]{1,0:T(8,128)(2,1)S(1)} %get-tuple-element.39), channel_id=1, source_target_pairs={{0,1},{1,0},{2,3},{3,2},{4,5},{5,4},{6,7},{7,6},{8,9},{9,8},{10,11... | collective-permute-start | bytes 196616 | tf_op jit(solution)/shard_map/ppermute | solution.py:45
  19.2 2.9 %collective-permute-start.6 = (bf16[128,256]{1,0:T(8,128)(2,1)S(1)}, bf16[128,256]{1,0:T(8,128)(2,1)S(1)}, u32[]{:S(2)}, u32[]{:S(2)}) collective-permute-start(bf16[128,256]{1,0:T(8,128)(2,1)S(1)} %get-tuple-element.40), channel_id=1, source_target_pairs={{0,32},{1,2},{2,1},{3,4},{4,3},{5,6},{6,5},{7,8},{8,7},{9,10},{10,... | collective-permute-start | bytes 196616 | tf_op jit(solution)/shard_map/ppermute | solution.py:45
  22.1 0.7 regroup.1
  22.8 3.5 %collective-permute-start.8 = (bf16[640,256]{1,0:T(8,128)(2,1)S(1)}, bf16[640,256]{1,0:T(8,128)(2,1)S(1)}, u32[]{:S(2)}, u32[]{:S(2)}) collective-permute-start(bf16[640,256]{1,0:T(8,128)(2,1)S(1)} %get-tuple-element.45), channel_id=1, source_target_pairs={{0,32},{32,0},{64,96},{96,64},{1,33},{33,1},{65,97},{97,65},{2,34}... | collective-permute-start | bytes 983048 | tf_op jit(solution)/shard_map/ppermute | solution.py:50
  26.2 1.0 %own_parts.1 = (f32[128,256]{1,0:T(8,128)S(1)}, f32[1728,128]{1,0:T(8,128)S(1)}) custom-call(bf16[448,256]{1,0:T(8,128)(2,1)S(1)} %get-tuple-element.34.mine_ref, bf16[448,256]{1,0:T(8,128)(2,1)S(1)} %collective-permute-done.4.got_ref.chip_ref, bf16[9,384,256]{2,1,0:T(8,128)(2,1)S(1)} %get-tuple-element.33.back_ref), custom_call_target="tpu_custom_call" | custom-call | flops 377487360 | bytes 2228224 | tf_op jit(solution)/shard_map/own_parts/pallas_call | solution.py:18
  27.3 1.7 %weight4_parts.1 = (f32[54,16,128]{2,1,0:T(8,128)S(1)}, bf16[54,16,128]{2,1,0:T(8,128)(2,1)S(1)}) custom-call(f32[128,256]{1,0:T(8,128)S(1)} %get-tuple-element.38.inward_ref, bf16[128,256]{1,0:T(8,128)(2,1)S(1)} %collective-permute-done.5.first_ref, bf16[128,256]{1,0:T(8,128)(2,1)S(1)} %collective-permute-done.6.second_ref, ...), custom_call_target="tpu_custom_call" | custom-call | flops 905969664 | bytes 6029312 | tf_op jit(solution)/shard_map/weight4_parts/pallas_call | solution.py:18
  29.1 0.9 %weight5.1._ = bf16[64,48,128]{2,1,0:T(8,128)(2,1)S(1)} custom-call(bf16[640,256]{1,0:T(8,128)(2,1)S(1)} %collective-permute-done.8.core_ref, f32[1728,128]{1,0:T(8,128)S(1)} %get-tuple-element.46.first_ref), custom_call_target="tpu_custom_call" | custom-call | flops 226492416 | bytes 1212416 | tf_op jit(solution)/shard_map/weight5/pallas_call | solution.py:18
  30.6 31.7 %all_to_all.10.parts_ref = bf16[64,48,128]{2,1,0:T(8,128)(2,1)S(1)} all-to-all(bf16[64,48,128]{2,1,0:T(8,128)(2,1)S(1)} %pairs.1), channel_id=1, replica_groups={{0,1,2,3,4,5,6,7,8,9,10,11,12,13,14,15,16,17,18,19,20,21,22,23,24,25,26..., dimensions={0} | all-to-all | bytes 1572864 | tf_op jit(solution)/shard_map/all_to_all | solution.py:554
  62.5 15.9 %all_to_all.11 = bf16[64,24,128]{2,1,0:T(8,128)(2,1)S(1)} all-to-all(bf16[64,24,128]{2,1,0:T(8,128)(2,1)S(1)} %pad_maximum_fusion), channel_id=1, replica_groups={{0,1,2,3,4,5,6,7,8,9,10,11,12,13,14,15,16,17,18,19,20,21,22,23,24,25,26..., dimensions={0} | all-to-all | bytes 786432 | tf_op jit(solution)/shard_map/all_to_all | solution.py:554
  78.4 3.0 %collective-permute-start.9 = (bf16[64,24,128]{2,1,0:T(8,128)(2,1)S(1)}, bf16[64,24,128]{2,1,0:T(8,128)(2,1)S(1)}, u32[]{:S(2)}, u32[]{:S(2)}) collective-permute-start(bf16[64,24,128]{2,1,0:T(8,128)(2,1)S(1)} %all_to_all.11), channel_id=1, source_target_pairs={{0,32},{32,0},{64,96},{96,64},{1,33},{33,1},{65,97},{97,65},{2,34}... | collective-permute-start | bytes 1179656 | tf_op jit(solution)/shard_map/ppermute | solution.py:50
  81.5 1.0 %first_half.1 = (f32[27,64,128]{2,1,0:T(8,128)}, f32[27,4,256]{2,1,0:T(4,128)}) custom-call(bf16[64,16,128]{2,1,0:T(8,128)(2,1)S(1)} %slice.18.rows4_ref, f32[64,8,128]{2,1,0:T(8,128)S(1)} %slice_convert_fusion.rows5_ref), custom_call_target="tpu_custom_call" | custom-call | tf_op jit(solution)/shard_map/first_half/pallas_call | solution.py:511
  82.8 1.0 %second_half.1 = (f32[27,64,128]{2,1,0:T(8,128)}, f32[27,4,256]{2,1,0:T(4,128)}) custom-call(bf16[64,16,128]{2,1,0:T(8,128)(2,1)S(1)} %slice.16.rows4_ref, f32[64,8,128]{2,1,0:T(8,128)S(1)} %slice_convert_fusion.1.rows5_ref, f32[27,64,128]{2,1,0:T(8,128)} %get-tuple-element.49._, ...), custom_call_target="tpu_custom_call", output_to_operand_aliasing={{0}: (2, {}), {1}: (3, {})} | custom-call | tf_op jit(solution)/shard_map/second_half/pallas_call | solution.py:511
  (26 shorter events, 2.0 us)
Async XLA Ops:
  1.6 7.0 %collective-permute-start.1 = (bf16[2,64,512]{2,1,0:T(8,128)(2,1)S(1)}, bf16[2,64,512]{2,1,0:T(8,128)(2,1)S(1)}, u32[]{:S(2)}, u32[]{:S(2)}) collective-permute-start(bf16[2,64,512]{2,1,0:T(8,128)(2,1)S(1)} %get-tuple-element.53), channel_id=1, source_target_pairs={{0,32},{1,2},{2,1},{3,4},{4,3},{5,6},{6,5},{7,8},{8,7},{9,10},{10,... | collective-permute-start | bytes 393224 | tf_op jit(solution)/shard_map/ppermute | solution.py:45
  3.1 5.5 %collective-permute-start = (bf16[2,64,512]{2,1,0:T(8,128)(2,1)S(1)}, bf16[2,64,512]{2,1,0:T(8,128)(2,1)S(1)}, u32[]{:S(2)}, u32[]{:S(2)}) collective-permute-start(bf16[2,64,512]{2,1,0:T(8,128)(2,1)S(1)} %get-tuple-element.54), channel_id=1, source_target_pairs={{0,1},{1,0},{2,3},{3,2},{4,5},{5,4},{6,7},{7,6},{8,9},{9,8},{10,11... | collective-permute-start | bytes 393224 | tf_op jit(solution)/shard_map/ppermute | solution.py:45
  6.4 1.0 %copy-start.1 = (bf16[2,2,64,512]{3,2,1,0:T(8,128)(2,1)S(1)}, bf16[2,2,64,512]{3,2,1,0:T(8,128)(2,1)}, u32[]{:S(2)}) copy-start(bf16[2,2,64,512]{3,2,1,0:T(8,128)(2,1)} %vol_ref.1) | copy-start | bytes 786436
  7.3 6.3 %copy-start = (bf16[27,256,128]{2,1,0:T(8,128)(2,1)S(1)}, bf16[27,256,128]{2,1,0:T(8,128)(2,1)}, u32[]{:S(2)}) copy-start(bf16[27,256,128]{2,1,0:T(8,128)(2,1)} %weight_ref.3) | copy-start | bytes 5308420
  8.6 6.7 %copy-start.2 = (bf16[1,2,256,128]{3,2,1,0:T(8,128)(2,1)S(1)}, bf16[1,2,256,128]{3,2,1,0:T(8,128)(2,1)}, u32[]{:S(2)}) copy-start(bf16[1,2,256,128]{3,2,1,0:T(8,128)(2,1)} %param.5) | copy-start | bytes 393220
  10.1 4.5 %collective-permute-start.3 = (bf16[128,256]{1,0:T(8,128)(2,1)S(1)}, bf16[128,256]{1,0:T(8,128)(2,1)S(1)}, u32[]{:S(2)}, u32[]{:S(2)}) collective-permute-start(bf16[128,256]{1,0:T(8,128)(2,1)S(1)} %get-tuple-element.30.pooled_ref), channel_id=1, source_target_pairs={{0,32},{1,2},{2,1},{3,4},{4,3},{5,6},{6,5},{7,8},{8,7},{9,10},{10,... | collective-permute-start | bytes 196616 | tf_op jit(solution)/shard_map/ppermute | solution.py:45
  11.4 3.8 %collective-permute-start.2 = (bf16[128,256]{1,0:T(8,128)(2,1)S(1)}, bf16[128,256]{1,0:T(8,128)(2,1)S(1)}, u32[]{:S(2)}, u32[]{:S(2)}) collective-permute-start(bf16[128,256]{1,0:T(8,128)(2,1)S(1)} %get-tuple-element.30.pooled_ref), channel_id=1, source_target_pairs={{0,1},{1,0},{2,3},{3,2},{4,5},{5,4},{6,7},{7,6},{8,9},{9,8},{10,11... | collective-permute-start | bytes 196616 | tf_op jit(solution)/shard_map/ppermute | solution.py:45
  17.0 5.1 %collective-permute-start.4 = (bf16[448,256]{1,0:T(8,128)(2,1)S(1)}, bf16[448,256]{1,0:T(8,128)(2,1)S(1)}, u32[]{:S(2)}, u32[]{:S(2)}) collective-permute-start(bf16[448,256]{1,0:T(8,128)(2,1)S(1)} %get-tuple-element.35), channel_id=1, source_target_pairs={{0,64},{32,96},{64,0},{96,32},{1,65},{33,97},{65,1},{97,33},{2,66}... | collective-permute-start | bytes 688136 | tf_op jit(solution)/shard_map/ppermute | solution.py:55
  17.6 9.7 %collective-permute-start.5 = (bf16[128,256]{1,0:T(8,128)(2,1)S(1)}, bf16[128,256]{1,0:T(8,128)(2,1)S(1)}, u32[]{:S(2)}, u32[]{:S(2)}) collective-permute-start(bf16[128,256]{1,0:T(8,128)(2,1)S(1)} %get-tuple-element.39), channel_id=1, source_target_pairs={{0,1},{1,0},{2,3},{3,2},{4,5},{5,4},{6,7},{7,6},{8,9},{9,8},{10,11... | collective-permute-start | bytes 196616 | tf_op jit(solution)/shard_map/ppermute | solution.py:45
  19.2 8.1 %collective-permute-start.6 = (bf16[128,256]{1,0:T(8,128)(2,1)S(1)}, bf16[128,256]{1,0:T(8,128)(2,1)S(1)}, u32[]{:S(2)}, u32[]{:S(2)}) collective-permute-start(bf16[128,256]{1,0:T(8,128)(2,1)S(1)} %get-tuple-element.40), channel_id=1, source_target_pairs={{0,32},{1,2},{2,1},{3,4},{4,3},{5,6},{6,5},{7,8},{8,7},{9,10},{10,... | collective-permute-start | bytes 196616 | tf_op jit(solution)/shard_map/ppermute | solution.py:45
  22.8 6.3 %collective-permute-start.8 = (bf16[640,256]{1,0:T(8,128)(2,1)S(1)}, bf16[640,256]{1,0:T(8,128)(2,1)S(1)}, u32[]{:S(2)}, u32[]{:S(2)}) collective-permute-start(bf16[640,256]{1,0:T(8,128)(2,1)S(1)} %get-tuple-element.45), channel_id=1, source_target_pairs={{0,32},{32,0},{64,96},{96,64},{1,33},{33,1},{65,97},{97,65},{2,34}... | collective-permute-start | bytes 983048 | tf_op jit(solution)/shard_map/ppermute | solution.py:50
  29.0 1.6 %collective-permute-start.7 = (bf16[54,16,128]{2,1,0:T(8,128)(2,1)S(1)}, bf16[54,16,128]{2,1,0:T(8,128)(2,1)S(1)}, u32[]{:S(2)}, u32[]{:S(2)}) collective-permute-start(bf16[54,16,128]{2,1,0:T(8,128)(2,1)S(1)} %get-tuple-element.44), channel_id=1, source_target_pairs={{0,32},{32,0},{64,96},{96,64},{1,33},{33,1},{65,97},{97,65},{2,34}... | collective-permute-start | bytes 663560 | tf_op jit(solution)/shard_map/ppermute | solution.py:50
  78.4 4.3 %collective-permute-start.9 = (bf16[64,24,128]{2,1,0:T(8,128)(2,1)S(1)}, bf16[64,24,128]{2,1,0:T(8,128)(2,1)S(1)}, u32[]{:S(2)}, u32[]{:S(2)}) collective-permute-start(bf16[64,24,128]{2,1,0:T(8,128)(2,1)S(1)} %all_to_all.11), channel_id=1, source_target_pairs={{0,32},{32,0},{64,96},{96,64},{1,33},{33,1},{65,97},{97,65},{2,34}... | collective-permute-start | bytes 1179656 | tf_op jit(solution)/shard_map/ppermute | solution.py:50

commit v9 on v8

--- a/solution.py
+++ b/solution.py
@@ -294,9 +294,7 @@
     spread_taps(planes, out_ref.at[:, pl.ds(i * lanes, lanes)], WIDTH // 2, lanes // 2, 1)
 
 
-def regroup_kernel(mine_ref, got_ref, made_ref, send_ref, out_ref, sem):
-    copy = pltpu.make_async_copy(made_ref, out_ref, sem)
-    copy.start()
+def regroup_kernel(mine_ref, got_ref, send_ref):
     core = lax.axis_index("dp") % 2
     rows = send_ref.shape[0] // 2
     half = mine_ref.shape[0] - rows
@@ -304,24 +302,12 @@
         start = pl.multiple_of((1 - core) * half, half)
         send_ref[pl.ds(i * rows, half), :] = ref[pl.ds(start, half), :]
         send_ref[pl.ds(i * rows + half, rows - half), :] = ref[pl.ds(2 * half, rows - half), :]
-    copy.wait()
-
-
-def regrouped(mine, got, made, outer):
+
+
+def regrouped(mine, got, outer):
     rows = mine.shape[0] - outer // 2
-    lanes = mine.shape[1]
-    return pl.pallas_call(
-        regroup_kernel,
-        out_shape=(
-            pltpu.VMEM((2 * rows, lanes), BF16),
-            jax.ShapeDtypeStruct(made.shape, made.dtype),
-        ),
-        in_specs=[VMEM] * 3,
-        out_specs=(VMEM, pl.BlockSpec(memory_space=pl.ANY)),
-        scratch_shapes=[pltpu.SemaphoreType.DMA],
-        compiler_params=pltpu.CompilerParams(vmem_limit_bytes=12 * 2**20),
-        name="regroup",
-    )(*[pltpu.with_memory_space_constraint(x, pltpu.VMEM) for x in (mine, got, made)])
+    (send,) = call(regroup_kernel, "regroup", (((2 * rows, mine.shape[1]), BF16),), (mine, got))
+    return send
 
 
 def weight5_sums(sources, stack_ref, total_ref):
@@ -334,7 +320,9 @@
         total_ref[at, :] = dot_rows(stack_ref[at, :], grads)
 
 
-def own_kernel(mine_ref, chip_ref, back_ref, inward_ref, total_ref, stack_ref):
+def own_kernel(mine_ref, back_ref, made_ref, inward_ref, total_ref, out_ref, stack_ref, sem):
+    copy = pltpu.make_async_copy(made_ref, out_ref, sem)
+    copy.start()
     core = lax.axis_index("dp") % 2
     outer = back_ref.shape[2]
     chans, lanes = inward_ref.shape
@@ -342,26 +330,38 @@
     inward_ref[...] = inward_part(back_ref, grad, lanes // 2, 2 * chans, chans)
     own = pl.ds(pl.multiple_of(core * (outer // 2), outer // 2), outer // 2)
     rows = mine_ref.shape[0] - outer
-    weight5_sums([(ref[own, :], ref, outer, rows) for ref in (mine_ref, chip_ref)], stack_ref, total_ref)
-
-
-def own_parts(mine, chip, back):
+    weight5_sums([(mine_ref[own, :], mine_ref, outer, rows)], stack_ref, total_ref)
+    copy.wait()
+
+
+def own_parts(mine, back, made):
     lanes = mine.shape[1]
     chans, outer = back.shape[1] // 3, back.shape[2]
     rows = 9 * (mine.shape[0] - outer)
-    return call(
+    return pl.pallas_call(
         own_kernel,
-        "own_parts",
-        (((chans, lanes), F32), ((rows, outer // 2), F32)),
-        (mine, chip, back),
-        scratch=[pltpu.VMEM((rows, 2 * lanes), BF16)],
-        flops=2 * back.size * lanes // 3 + 2 * rows * lanes * outer,
-    )
-
-
-def weight5_kernel(core_ref, first_ref, part_ref, stack_ref, total_ref):
+        out_shape=(
+            pltpu.VMEM((chans, lanes), F32),
+            pltpu.VMEM((rows, outer // 2), F32),
+            jax.ShapeDtypeStruct(made.shape, made.dtype),
+        ),
+        in_specs=[VMEM] * 3,
+        out_specs=(VMEM, VMEM, pl.BlockSpec(memory_space=pl.ANY)),
+        scratch_shapes=[pltpu.VMEM((rows, lanes), BF16), pltpu.SemaphoreType.DMA],
+        compiler_params=pltpu.CompilerParams(vmem_limit_bytes=12 * 2**20),
+        cost_estimate=pl.CostEstimate(
+            flops=2 * back.size * lanes // 3 + 2 * rows * lanes * outer,
+            bytes_accessed=2 * back.size,
+            transcendentals=0,
+        ),
+        name="own_parts",
+    )(*[pltpu.with_memory_space_constraint(x, pltpu.VMEM) for x in (mine, back, made)])
+
+
+def weight5_kernel(chip_ref, core_ref, first_ref, part_ref, stack_ref, total_ref):
     rows, half = core_ref.shape[0] // 2, total_ref.shape[1]
-    sources = [
+    own = pl.multiple_of(lax.axis_index("dp") % 2 * half, half)
+    sources = [(chip_ref[pl.ds(own, half), :], chip_ref, 2 * half, rows - half)] + [
         (core_ref[pl.ds(i * rows, half), :], core_ref, i * rows + half, rows - half)
         for i in range(2)
     ]
@@ -376,25 +376,34 @@
         )
 
 
-def weight5_part(core, first):
+def weight5_part(chip, core, first):
     rows, half = first.shape
     (part,) = call(
         weight5_kernel,
         "weight5",
         (((64, 48, 128), BF16),),
-        (core, first),
-        scratch=[pltpu.VMEM((rows, 2 * core.shape[1]), BF16), pltpu.VMEM((rows + 8, half), F32)],
+        (chip, core, first),
+        scratch=[pltpu.VMEM((rows, 3 * core.shape[1]), BF16), pltpu.VMEM((rows + 8, half), F32)],
         flops=4 * rows * core.shape[1] * half,
     )
     return part
 
 
-def weight4_kernel(
-    inward_ref, first_ref, second_ref, stack_ref, slope_ref, keep_ref, send_ref, acc_ref
-):
+def halo_kernel(inward_ref, first_ref, second_ref, sum_ref):
+    below, above = neighbours(first_ref[...], second_ref[...])
+    sum_ref[...] = (inward_ref[...] + below.astype(F32) + above.astype(F32)).astype(BF16)
+
+
+def halo_sum(inward, first, second):
+    (total,) = call(
+        halo_kernel, "halo_sum", ((first.shape, BF16),), (inward, first, second), flops=8 * 10**9
+    )
+    return total
+
+
+def weight4_kernel(inward_ref, stack_ref, slope_ref, keep_ref, send_ref, acc_ref):
     core = lax.axis_index("dp") % 2
-    below, above = neighbours(first_ref[...], second_ref[...])
-    inward = (inward_ref[...] + below.astype(F32) + above.astype(F32)).astype(BF16)
+    inward = inward_ref[...]
     chans = inward.shape[0]
     cells = inward.shape[1] // 2
     unpool = pool_matrix(1, (cells, 4 * cells))
@@ -426,13 +435,13 @@
             send_ref[2 * o + k] = acc_ref[pl.ds(theirs, share), :].astype(BF16)
 
 
-def weight4_parts(inward, first, second, stack, slope):
+def weight4_parts(inward, stack, slope):
     chans = inward.shape[0]
     return call(
         weight4_kernel,
         "weight4_parts",
         (((54, 16, 128), F32), ((54, 16, 128), BF16)),
-        (inward, first, second, stack, slope),
+        (inward, stack, slope),
         scratch=[pltpu.VMEM((3 * stack.shape[0] // 4, chans), F32)],
         flops=3 * stack.size * chans,
     )
@@ -539,10 +548,11 @@
     )
     first, second = swapped(to_first, 0), swapped(to_second, 1)
     chip5 = other_chip(share5)
-    send5, output5 = regrouped(mine5, chip5, output5, conv5_weight.shape[1])
-    inward, chips5 = own_parts(mine5, chip5, back5)
-    part = weight5_part(other_core(send5), chips5)
-    keep, send = weight4_parts(inward, first, second, stack4, slope)
+    inward, chips5, output5 = own_parts(mine5, back5, output5)
+    inward, after = lax.optimization_barrier((halo_sum(inward, first, second), chip5))
+    send5 = regrouped(mine5, after, conv5_weight.shape[1])
+    part = weight5_part(chip5, other_core(send5), chips5)
+    keep, send = weight4_parts(inward, stack4, slope)
     axes = ("dp", "space")
     spaces, groups = lax.axis_size("space"), lax.axis_size("dp")
     per_core = [

time: 84.1 us -> 83.7 us (level)
  waiting for transfers between devices: 1.61 us -> 7.43 us
  starting transfers between devices: 18.6 us -> 15.7 us
  blocking collectives: 47.6 us -> 45 us
    ppermute x1, waiting for transfers between devices: 0.01 us -> 6.04 us  [other_chip(): return lax.ppermute(values, 'dp', [(i, i ^ 2) for i in range(count)])]
    ppermute x3, starting transfers between devices: 6.57 us -> 3.89 us  [other_core(): return lax.ppermute(values, 'dp', [(i, i ^ 1) for i in range(count)])]
    all_to_all x2, blocking collectives: 47.6 us -> 45 us  [exchange(): lax.all_to_all(parts, axes, split_axis=0, concat_axis=0, tiled=True, axis...]
    pallas_call x9 -> x10, Pallas kernels: 9.15 us -> 8.4 us  [call(): pl.pallas_call(kernel, out_shape=tuple((pltpu.VMEM(shape, dtype) for shap...]
  transfers between devices with their start and end apart: 10 -> 10, of which waited for: 3 -> 4; matrix products, arithmetic and copies ran while one was open for 1% -> 2% of each run, Pallas kernels for 9% -> 8%
where the time goes in v9:
time: 83.7 us; the launch traced here: 83.4 us
  blocking collectives  45 us (54%)
  starting transfers between devices  15.7 us (19%)
  Pallas kernels  11.2 us (13%)
  waiting for transfers between devices  7.43 us (9%)
  local copies, waits for them, and re-layouts  3.26 us (4%)
  between operations  0.84 us (1%)
    all_to_all x2, blocking collectives, exchange(): lax.all_to_all(parts, axes, split_axis=0, concat_axis=0, tiled=True, axis...  45 us
    ppermute x6, starting transfers between devices, swapped(): return lax.ppermute(values, ('dp', 'space'), pairs)  11.5 us
    pallas_call x10, Pallas kernels, call(): pl.pallas_call(kernel, out_shape=tuple((pltpu.VMEM(shape, dtype) for shap...  8.4 us
    ppermute x1, waiting for transfers between devices, other_chip(): return lax.ppermute(values, 'dp', [(i, i ^ 2) for i in range(count)])  6.04 us
    ppermute x3, starting transfers between devices, other_core(): return lax.ppermute(values, 'dp', [(i, i ^ 1) for i in range(count)])  3.89 us
    pallas_call x2, Pallas kernels, placed_half(): pl.pallas_call(kernel, out_shape=(jax.ShapeDtypeStruct((27, 64, 128), F32...  1.94 us
  transfers between devices with their start and end apart: 10, of which 4 were waited for; matrix products, arithmetic and copies ran while one was open for 2% of the time, Pallas kernels for 8%

profile of v9, /device:TPU:1, one launch (start us, length us, event | category | flops | bytes accessed | tf_op | source)
XLA Modules:
  0.0 83.4 jit_solution(4221671706759163903)
XLA Ops:
  0.6 1.0 %dynamic-slice_bitcast_fusion = (bf16[2,64,512]{2,1,0:T(8,128)(2,1)S(1)}, bf16[2,64,512]{2,1,0:T(8,128)(2,1)S(1)}) fusion(bf16[2,2,64,512]{3,2,1,0:T(8,128)(2,1)} %vol_ref.1, s32[]{:T(128)S(6)} %select_n.16, s32[]{:T(128)S(6)} %select_n.15), kind=kLoop, calls=%fused_computation.3 | loop fusion | bytes 524296 | tf_op jit(solution)/shard_map/jit(dynamic_index_in_dim)/squeeze | solution.py:541
  1.6 1.5 %collective-permute-start.1 = (bf16[2,64,512]{2,1,0:T(8,128)(2,1)S(1)}, bf16[2,64,512]{2,1,0:T(8,128)(2,1)S(1)}, u32[]{:S(2)}, u32[]{:S(2)}) collective-permute-start(bf16[2,64,512]{2,1,0:T(8,128)(2,1)S(1)} %get-tuple-element.55), channel_id=1, source_target_pairs={{0,32},{1,2},{2,1},{3,4},{4,3},{5,6},{6,5},{7,8},{8,7},{9,10},{10,... | collective-permute-start | bytes 393224 | tf_op jit(solution)/shard_map/ppermute | solution.py:45
  3.1 2.0 %collective-permute-start = (bf16[2,64,512]{2,1,0:T(8,128)(2,1)S(1)}, bf16[2,64,512]{2,1,0:T(8,128)(2,1)S(1)}, u32[]{:S(2)}, u32[]{:S(2)}) collective-permute-start(bf16[2,64,512]{2,1,0:T(8,128)(2,1)S(1)} %get-tuple-element.56), channel_id=1, source_target_pairs={{0,1},{1,0},{2,3},{3,2},{4,5},{5,4},{6,7},{7,6},{8,9},{9,8},{10,11... | collective-permute-start | bytes 393224 | tf_op jit(solution)/shard_map/ppermute | solution.py:45
  5.1 1.2 %copy.15.weight_ref = bf16[128,1728]{1,0:T(8,128)(2,1)S(1)} copy(bf16[128,1728]{0,1:T(8,128)(2,1)} %bitcast.17) | data formatting | bytes 884736 | tf_op jit(solution)/shard_map/reshape | solution.py:542
  6.4 0.9 %copy-done.1 = bf16[2,2,64,512]{3,2,1,0:T(8,128)(2,1)S(1)} copy-done((bf16[2,2,64,512]{3,2,1,0:T(8,128)(2,1)S(1)}, bf16[2,2,64,512]{3,2,1,0:T(8,128)(2,1)}, u32[]{:S(2)}) %copy-start.1) | copy-done | bytes 262168
  7.3 1.3 %own4.1 = (f32[2,128,1024]{2,1,0:T(8,128)S(1)}, bf16[2304,1024]{1,0:T(8,128)(2,1)S(1)}) custom-call(bf16[2,2,64,512]{3,2,1,0:T(8,128)(2,1)S(1)} %copy-done.1, bf16[128,1728]{1,0:T(8,128)(2,1)S(1)} %copy.15.weight_ref), custom_call_target="tpu_custom_call" | custom-call | flops 905969664 | bytes 704512 | tf_op jit(solution)/shard_map/own4/pallas_call | solution.py:18
  8.6 1.5 %layer4.1 = (bf16[128,256]{1,0:T(8,128)(2,1)S(1)}, f32[2,128,1024]{2,1,0:T(8,128)S(1)}, bf16[2304,1024]{1,0:T(8,128)(2,1)S(1)}) custom-call(bf16[2,64,512]{2,1,0:T(8,128)(2,1)S(1)} %collective-permute-done.first_ref, bf16[2,64,512]{2,1,0:T(8,128)(2,1)S(1)} %collective-permute-done.1.second_ref, ...), custom_call_target="tpu_custom_call", output_to_operand_aliasing={{1}: (3, {}), {2}: (4, {})} | custom-call | flops 452984832 | bytes 6471680 | tf_op jit(solution)/shard_map/layer4/pallas_call | solution.py:18
  10.1 1.3 %collective-permute-start.3 = (bf16[128,256]{1,0:T(8,128)(2,1)S(1)}, bf16[128,256]{1,0:T(8,128)(2,1)S(1)}, u32[]{:S(2)}, u32[]{:S(2)}) collective-permute-start(bf16[128,256]{1,0:T(8,128)(2,1)S(1)} %get-tuple-element.31.pooled_ref), channel_id=1, source_target_pairs={{0,32},{1,2},{2,1},{3,4},{4,3},{5,6},{6,5},{7,8},{8,7},{9,10},{10,... | collective-permute-start | bytes 196616 | tf_op jit(solution)/shard_map/ppermute | solution.py:45
  11.4 2.2 %collective-permute-start.2 = (bf16[128,256]{1,0:T(8,128)(2,1)S(1)}, bf16[128,256]{1,0:T(8,128)(2,1)S(1)}, u32[]{:S(2)}, u32[]{:S(2)}) collective-permute-start(bf16[128,256]{1,0:T(8,128)(2,1)S(1)} %get-tuple-element.31.pooled_ref), channel_id=1, source_target_pairs={{0,1},{1,0},{2,3},{3,2},{4,5},{5,4},{6,7},{7,6},{8,9},{9,8},{10,11... | collective-permute-start | bytes 196616 | tf_op jit(solution)/shard_map/ppermute | solution.py:45
  13.6 1.0 %own5.1 = (f32[256,256]{1,0:T(8,128)S(1)}, bf16[9,384,256]{2,1,0:T(8,128)(2,1)S(1)}, f32[2,128,1024]{2,1,0:T(8,128)S(1)}) custom-call(bf16[128,256]{1,0:T(8,128)(2,1)S(1)} %get-tuple-element.31.pooled_ref, bf16[27,256,128]{2,1,0:T(8,128)(2,1)S(1)} %copy-done, f32[2,128,1024]{2,1,0:T(8,128)S(1)} %get-tuple-element.32.preact4_ref), custom_call_target="tpu_custom_call", output_to_operand_aliasing={{2}: (2, {})} | custom-call | flops 150994944 | bytes 2883584 | tf_op jit(solution)/shard_map/own5/pallas_call | solution.py:18
  14.5 0.7 collective-permute-done.2.first_ref
  15.2 1.7 %layer5.1 = (bf16[2,256,128]{2,1,0:T(8,128)(2,1)S(1)}, bf16[128,256]{1,0:T(8,128)(2,1)S(1)}, bf16[128,256]{1,0:T(8,128)(2,1)S(1)}, bf16[448,256]{1,0:T(8,128)(2,1)S(1)}, bf16[448,256]{1,0:T(8,128)(2,1)S(1)}) custom-call(bf16[128,256]{1,0:T(8,128)(2,1)S(1)} %get-tuple-element.31.pooled_ref, bf16[128,256]{1,0:T(8,128)(2,1)S(1)} %collective-permute-done.2.first_ref, ...), custom_call_target="tpu_custom_call" | custom-call | flops 679477248 | bytes 4128768 | tf_op jit(solution)/shard_map/layer5/pallas_call | solution.py:18
  17.0 1.8 %collective-permute-start.4 = (bf16[128,256]{1,0:T(8,128)(2,1)S(1)}, bf16[128,256]{1,0:T(8,128)(2,1)S(1)}, u32[]{:S(2)}, u32[]{:S(2)}) collective-permute-start(bf16[128,256]{1,0:T(8,128)(2,1)S(1)} %get-tuple-element.39), channel_id=1, source_target_pairs={{0,1},{1,0},{2,3},{3,2},{4,5},{5,4},{6,7},{7,6},{8,9},{9,8},{10,11... | collective-permute-start | bytes 196616 | tf_op jit(solution)/shard_map/ppermute | solution.py:45
  18.8 2.7 %collective-permute-start.5 = (bf16[128,256]{1,0:T(8,128)(2,1)S(1)}, bf16[128,256]{1,0:T(8,128)(2,1)S(1)}, u32[]{:S(2)}, u32[]{:S(2)}) collective-permute-start(bf16[128,256]{1,0:T(8,128)(2,1)S(1)} %get-tuple-element.40), channel_id=1, source_target_pairs={{0,32},{1,2},{2,1},{3,4},{4,3},{5,6},{6,5},{7,8},{8,7},{9,10},{10,... | collective-permute-start | bytes 196616 | tf_op jit(solution)/shard_map/ppermute | solution.py:45
  21.8 0.8 own_parts.1
  22.7 6.0 %collective-permute-done.6.got_ref.chip_ref = bf16[448,256]{1,0:T(8,128)(2,1)S(1)} collective-permute-done((bf16[448,256]{1,0:T(8,128)(2,1)S(1)}, bf16[448,256]{1,0:T(8,128)(2,1)S(1)}, u32[]{:S(2)}, u32[]{:S(2)}) %collective-permute-start.6) | collective-permute-done | bytes 229408 | tf_op jit(solution)/shard_map/ppermute | solution.py:55
  28.7 0.9 %collective-permute-start.8 = (bf16[640,256]{1,0:T(8,128)(2,1)S(1)}, bf16[640,256]{1,0:T(8,128)(2,1)S(1)}, u32[]{:S(2)}, u32[]{:S(2)}) collective-permute-start(bf16[640,256]{1,0:T(8,128)(2,1)S(1)} %regroup.1), channel_id=1, source_target_pairs={{0,32},{32,0},{64,96},{96,64},{1,33},{33,1},{65,97},{97,65},{2,34}... | collective-permute-start | bytes 983048 | tf_op jit(solution)/shard_map/ppermute | solution.py:50
  29.6 1.7 %weight4_parts.1 = (f32[54,16,128]{2,1,0:T(8,128)S(1)}, bf16[54,16,128]{2,1,0:T(8,128)(2,1)S(1)}) custom-call(bf16[128,256]{1,0:T(8,128)(2,1)S(1)} %halo_sum.1.inward_ref, bf16[2304,1024]{1,0:T(8,128)(2,1)S(1)} %get-tuple-element.43.stack_ref, f32[2,128,1024]{2,1,0:T(8,128)S(1)} %get-tuple-element.44.slope_ref), custom_call_target="tpu_custom_call" | custom-call | flops 905969664 | bytes 5832704 | tf_op jit(solution)/shard_map/weight4_parts/pallas_call | solution.py:18
  31.4 1.1 %weight5.1._ = bf16[64,48,128]{2,1,0:T(8,128)(2,1)S(1)} custom-call(bf16[448,256]{1,0:T(8,128)(2,1)S(1)} %collective-permute-done.6.got_ref.chip_ref, bf16[640,256]{1,0:T(8,128)(2,1)S(1)} %collective-permute-done.8.core_ref, f32[1728,128]{1,0:T(8,128)S(1)} %get-tuple-element.48.first_ref), custom_call_target="tpu_custom_call" | custom-call | flops 226492416 | bytes 1441792 | tf_op jit(solution)/shard_map/weight5/pallas_call | solution.py:18
  32.9 29.3 %all_to_all.10.parts_ref = bf16[64,48,128]{2,1,0:T(8,128)(2,1)S(1)} all-to-all(bf16[64,48,128]{2,1,0:T(8,128)(2,1)S(1)} %pairs.1), channel_id=1, replica_groups={{0,1,2,3,4,5,6,7,8,9,10,11,12,13,14,15,16,17,18,19,20,21,22,23,24,25,26..., dimensions={0} | all-to-all | bytes 1572864 | tf_op jit(solution)/shard_map/all_to_all | solution.py:564
  62.5 15.6 %all_to_all.11 = bf16[64,24,128]{2,1,0:T(8,128)(2,1)S(1)} all-to-all(bf16[64,24,128]{2,1,0:T(8,128)(2,1)S(1)} %pad_maximum_fusion), channel_id=1, replica_groups={{0,1,2,3,4,5,6,7,8,9,10,11,12,13,14,15,16,17,18,19,20,21,22,23,24,25,26..., dimensions={0} | all-to-all | bytes 786432 | tf_op jit(solution)/shard_map/all_to_all | solution.py:564
  78.1 2.9 %collective-permute-start.9 = (bf16[64,24,128]{2,1,0:T(8,128)(2,1)S(1)}, bf16[64,24,128]{2,1,0:T(8,128)(2,1)S(1)}, u32[]{:S(2)}, u32[]{:S(2)}) collective-permute-start(bf16[64,24,128]{2,1,0:T(8,128)(2,1)S(1)} %all_to_all.11), channel_id=1, source_target_pairs={{0,32},{32,0},{64,96},{96,64},{1,33},{33,1},{65,97},{97,65},{2,34}... | collective-permute-start | bytes 1179656 | tf_op jit(solution)/shard_map/ppermute | solution.py:50
  81.1 1.0 %first_half.1 = (f32[27,64,128]{2,1,0:T(8,128)}, f32[27,4,256]{2,1,0:T(4,128)}) custom-call(bf16[64,16,128]{2,1,0:T(8,128)(2,1)S(1)} %slice.18.rows4_ref, f32[64,8,128]{2,1,0:T(8,128)S(1)} %slice_convert_fusion.rows5_ref), custom_call_target="tpu_custom_call" | custom-call | tf_op jit(solution)/shard_map/first_half/pallas_call | solution.py:520
  82.4 1.0 %second_half.1 = (f32[27,64,128]{2,1,0:T(8,128)}, f32[27,4,256]{2,1,0:T(4,128)}) custom-call(bf16[64,16,128]{2,1,0:T(8,128)(2,1)S(1)} %slice.16.rows4_ref, f32[64,8,128]{2,1,0:T(8,128)S(1)} %slice_convert_fusion.1.rows5_ref, f32[27,64,128]{2,1,0:T(8,128)} %get-tuple-element.51._, ...), custom_call_target="tpu_custom_call", output_to_operand_aliasing={{0}: (2, {}), {1}: (3, {})} | custom-call | tf_op jit(solution)/shard_map/second_half/pallas_call | solution.py:520
  (27 shorter events, 1.5 us)
Async XLA Ops:
  1.6 7.0 %collective-permute-start.1 = (bf16[2,64,512]{2,1,0:T(8,128)(2,1)S(1)}, bf16[2,64,512]{2,1,0:T(8,128)(2,1)S(1)}, u32[]{:S(2)}, u32[]{:S(2)}) collective-permute-start(bf16[2,64,512]{2,1,0:T(8,128)(2,1)S(1)} %get-tuple-element.55), channel_id=1, source_target_pairs={{0,32},{1,2},{2,1},{3,4},{4,3},{5,6},{6,5},{7,8},{8,7},{9,10},{10,... | collective-permute-start | bytes 393224 | tf_op jit(solution)/shard_map/ppermute | solution.py:45
  3.1 5.5 %collective-permute-start = (bf16[2,64,512]{2,1,0:T(8,128)(2,1)S(1)}, bf16[2,64,512]{2,1,0:T(8,128)(2,1)S(1)}, u32[]{:S(2)}, u32[]{:S(2)}) collective-permute-start(bf16[2,64,512]{2,1,0:T(8,128)(2,1)S(1)} %get-tuple-element.56), channel_id=1, source_target_pairs={{0,1},{1,0},{2,3},{3,2},{4,5},{5,4},{6,7},{7,6},{8,9},{9,8},{10,11... | collective-permute-start | bytes 393224 | tf_op jit(solution)/shard_map/ppermute | solution.py:45
  6.4 1.0 %copy-start.1 = (bf16[2,2,64,512]{3,2,1,0:T(8,128)(2,1)S(1)}, bf16[2,2,64,512]{3,2,1,0:T(8,128)(2,1)}, u32[]{:S(2)}) copy-start(bf16[2,2,64,512]{3,2,1,0:T(8,128)(2,1)} %vol_ref.1) | copy-start | bytes 786436
  7.3 6.3 %copy-start = (bf16[27,256,128]{2,1,0:T(8,128)(2,1)S(1)}, bf16[27,256,128]{2,1,0:T(8,128)(2,1)}, u32[]{:S(2)}) copy-start(bf16[27,256,128]{2,1,0:T(8,128)(2,1)} %weight_ref.3) | copy-start | bytes 5308420
  8.6 6.6 %copy-start.2 = (bf16[1,2,256,128]{3,2,1,0:T(8,128)(2,1)S(1)}, bf16[1,2,256,128]{3,2,1,0:T(8,128)(2,1)}, u32[]{:S(2)}) copy-start(bf16[1,2,256,128]{3,2,1,0:T(8,128)(2,1)} %param.5) | copy-start | bytes 393220
  10.1 4.4 %collective-permute-start.3 = (bf16[128,256]{1,0:T(8,128)(2,1)S(1)}, bf16[128,256]{1,0:T(8,128)(2,1)S(1)}, u32[]{:S(2)}, u32[]{:S(2)}) collective-permute-start(bf16[128,256]{1,0:T(8,128)(2,1)S(1)} %get-tuple-element.31.pooled_ref), channel_id=1, source_target_pairs={{0,32},{1,2},{2,1},{3,4},{4,3},{5,6},{6,5},{7,8},{8,7},{9,10},{10,... | collective-permute-start | bytes 196616 | tf_op jit(solution)/shard_map/ppermute | solution.py:45
  11.4 3.8 %collective-permute-start.2 = (bf16[128,256]{1,0:T(8,128)(2,1)S(1)}, bf16[128,256]{1,0:T(8,128)(2,1)S(1)}, u32[]{:S(2)}, u32[]{:S(2)}) collective-permute-start(bf16[128,256]{1,0:T(8,128)(2,1)S(1)} %get-tuple-element.31.pooled_ref), channel_id=1, source_target_pairs={{0,1},{1,0},{2,3},{3,2},{4,5},{5,4},{6,7},{7,6},{8,9},{9,8},{10,11... | collective-permute-start | bytes 196616 | tf_op jit(solution)/shard_map/ppermute | solution.py:45
  17.0 5.6 %collective-permute-start.4 = (bf16[128,256]{1,0:T(8,128)(2,1)S(1)}, bf16[128,256]{1,0:T(8,128)(2,1)S(1)}, u32[]{:S(2)}, u32[]{:S(2)}) collective-permute-start(bf16[128,256]{1,0:T(8,128)(2,1)S(1)} %get-tuple-element.39), channel_id=1, source_target_pairs={{0,1},{1,0},{2,3},{3,2},{4,5},{5,4},{6,7},{7,6},{8,9},{9,8},{10,11... | collective-permute-start | bytes 196616 | tf_op jit(solution)/shard_map/ppermute | solution.py:45
  18.8 3.8 %collective-permute-start.5 = (bf16[128,256]{1,0:T(8,128)(2,1)S(1)}, bf16[128,256]{1,0:T(8,128)(2,1)S(1)}, u32[]{:S(2)}, u32[]{:S(2)}) collective-permute-start(bf16[128,256]{1,0:T(8,128)(2,1)S(1)} %get-tuple-element.40), channel_id=1, source_target_pairs={{0,32},{1,2},{2,1},{3,4},{4,3},{5,6},{6,5},{7,8},{8,7},{9,10},{10,... | collective-permute-start | bytes 196616 | tf_op jit(solution)/shard_map/ppermute | solution.py:45
  21.5 7.2 %collective-permute-start.6 = (bf16[448,256]{1,0:T(8,128)(2,1)S(1)}, bf16[448,256]{1,0:T(8,128)(2,1)S(1)}, u32[]{:S(2)}, u32[]{:S(2)}) collective-permute-start(bf16[448,256]{1,0:T(8,128)(2,1)S(1)} %get-tuple-element.41), channel_id=1, source_target_pairs={{0,64},{32,96},{64,0},{96,32},{1,65},{33,97},{65,1},{97,33},{2,66}... | collective-permute-start | bytes 688136 | tf_op jit(solution)/shard_map/ppermute | solution.py:55
  28.7 2.6 %collective-permute-start.8 = (bf16[640,256]{1,0:T(8,128)(2,1)S(1)}, bf16[640,256]{1,0:T(8,128)(2,1)S(1)}, u32[]{:S(2)}, u32[]{:S(2)}) collective-permute-start(bf16[640,256]{1,0:T(8,128)(2,1)S(1)} %regroup.1), channel_id=1, source_target_pairs={{0,32},{32,0},{64,96},{96,64},{1,33},{33,1},{65,97},{97,65},{2,34}... | collective-permute-start | bytes 983048 | tf_op jit(solution)/shard_map/ppermute | solution.py:50
  31.3 1.6 %collective-permute-start.7 = (bf16[54,16,128]{2,1,0:T(8,128)(2,1)S(1)}, bf16[54,16,128]{2,1,0:T(8,128)(2,1)S(1)}, u32[]{:S(2)}, u32[]{:S(2)}) collective-permute-start(bf16[54,16,128]{2,1,0:T(8,128)(2,1)S(1)} %get-tuple-element.46), channel_id=1, source_target_pairs={{0,32},{32,0},{64,96},{96,64},{1,33},{33,1},{65,97},{97,65},{2,34}... | collective-permute-start | bytes 663560 | tf_op jit(solution)/shard_map/ppermute | solution.py:50
  78.1 4.3 %collective-permute-start.9 = (bf16[64,24,128]{2,1,0:T(8,128)(2,1)S(1)}, bf16[64,24,128]{2,1,0:T(8,128)(2,1)S(1)}, u32[]{:S(2)}, u32[]{:S(2)}) collective-permute-start(bf16[64,24,128]{2,1,0:T(8,128)(2,1)S(1)} %all_to_all.11), channel_id=1, source_target_pairs={{0,32},{32,0},{64,96},{96,64},{1,33},{33,1},{65,97},{97,65},{2,34}... | collective-permute-start | bytes 1179656 | tf_op jit(solution)/shard_map/ppermute | solution.py:50

commit v10 on v9

--- a/solution.py
+++ b/solution.py
@@ -314,10 +314,7 @@
     for i, (_, ref, first, rows) in enumerate(sources):
         stack_window(ref, first, rows, stack_ref, i)
     grads = jnp.concatenate([grad for grad, *_ in sources], axis=1)
-    block = stack_ref.shape[0] // 3
-    for j in range(3):
-        at = pl.ds(j * block, block)
-        total_ref[at, :] = dot_rows(stack_ref[at, :], grads)
+    total_ref[pl.ds(0, stack_ref.shape[0]), :] = dot_rows(stack_ref[...], grads)
 
 
 def own_kernel(mine_ref, back_ref, made_ref, inward_ref, total_ref, out_ref, stack_ref, sem):

time: 83.7 us -> 83.7 us (level)
  transfers between devices with their start and end apart: 10 -> 10, of which waited for: 4 -> 4; matrix products, arithmetic and copies ran while one was open for 2% -> 2% of each run, Pallas kernels for 8% -> 9%
where the time goes in v10:
time: 83.7 us; the launch traced here: 83.4 us
  blocking collectives  45 us (54%)
  starting transfers between devices  15.7 us (19%)
  Pallas kernels  11.5 us (14%)
  waiting for transfers between devices  7.03 us (8%)
  local copies, waits for them, and re-layouts  3.26 us (4%)
  between operations  0.85 us (1%)
    all_to_all x2, blocking collectives, exchange(): lax.all_to_all(parts, axes, split_axis=0, concat_axis=0, tiled=True, axis...  45 us
    ppermute x6, starting transfers between devices, swapped(): return lax.ppermute(values, ('dp', 'space'), pairs)  11.5 us
    pallas_call x10, Pallas kernels, call(): pl.pallas_call(kernel, out_shape=tuple((pltpu.VMEM(shape, dtype) for shap...  8.39 us
    ppermute x1, waiting for transfers between devices, other_chip(): return lax.ppermute(values, 'dp', [(i, i ^ 2) for i in range(count)])  5.64 us
    ppermute x3, starting transfers between devices, other_core(): return lax.ppermute(values, 'dp', [(i, i ^ 1) for i in range(count)])  3.88 us
    pallas_call x2, Pallas kernels, placed_half(): pl.pallas_call(kernel, out_shape=(jax.ShapeDtypeStruct((27, 64, 128), F32...  1.94 us
  transfers between devices with their start and end apart: 10, of which 4 were waited for; matrix products, arithmetic and copies ran while one was open for 2% of the time, Pallas kernels for 9%

profile of v10, /device:TPU:1, one launch (start us, length us, event | category | flops | bytes accessed | tf_op | source)
XLA Modules:
  0.0 83.4 jit_solution(9238333261193799470)
XLA Ops:
  0.6 1.0 %dynamic-slice_bitcast_fusion = (bf16[2,64,512]{2,1,0:T(8,128)(2,1)S(1)}, bf16[2,64,512]{2,1,0:T(8,128)(2,1)S(1)}) fusion(bf16[2,2,64,512]{3,2,1,0:T(8,128)(2,1)} %vol_ref.1, s32[]{:T(128)S(6)} %select_n.16, s32[]{:T(128)S(6)} %select_n.15), kind=kLoop, calls=%fused_computation.3 | loop fusion | bytes 524296 | tf_op jit(solution)/shard_map/jit(dynamic_index_in_dim)/squeeze | solution.py:538
  1.6 1.5 %collective-permute-start.1 = (bf16[2,64,512]{2,1,0:T(8,128)(2,1)S(1)}, bf16[2,64,512]{2,1,0:T(8,128)(2,1)S(1)}, u32[]{:S(2)}, u32[]{:S(2)}) collective-permute-start(bf16[2,64,512]{2,1,0:T(8,128)(2,1)S(1)} %get-tuple-element.55), channel_id=1, source_target_pairs={{0,32},{1,2},{2,1},{3,4},{4,3},{5,6},{6,5},{7,8},{8,7},{9,10},{10,... | collective-permute-start | bytes 393224 | tf_op jit(solution)/shard_map/ppermute | solution.py:45
  3.1 2.0 %collective-permute-start = (bf16[2,64,512]{2,1,0:T(8,128)(2,1)S(1)}, bf16[2,64,512]{2,1,0:T(8,128)(2,1)S(1)}, u32[]{:S(2)}, u32[]{:S(2)}) collective-permute-start(bf16[2,64,512]{2,1,0:T(8,128)(2,1)S(1)} %get-tuple-element.56), channel_id=1, source_target_pairs={{0,1},{1,0},{2,3},{3,2},{4,5},{5,4},{6,7},{7,6},{8,9},{9,8},{10,11... | collective-permute-start | bytes 393224 | tf_op jit(solution)/shard_map/ppermute | solution.py:45
  5.1 1.2 %copy.15.weight_ref = bf16[128,1728]{1,0:T(8,128)(2,1)S(1)} copy(bf16[128,1728]{0,1:T(8,128)(2,1)} %bitcast.17) | data formatting | bytes 884736 | tf_op jit(solution)/shard_map/reshape | solution.py:539
  6.4 0.9 %copy-done.1 = bf16[2,2,64,512]{3,2,1,0:T(8,128)(2,1)S(1)} copy-done((bf16[2,2,64,512]{3,2,1,0:T(8,128)(2,1)S(1)}, bf16[2,2,64,512]{3,2,1,0:T(8,128)(2,1)}, u32[]{:S(2)}) %copy-start.1) | copy-done | bytes 262168
  7.3 1.3 %own4.1 = (f32[2,128,1024]{2,1,0:T(8,128)S(1)}, bf16[2304,1024]{1,0:T(8,128)(2,1)S(1)}) custom-call(bf16[2,2,64,512]{3,2,1,0:T(8,128)(2,1)S(1)} %copy-done.1, bf16[128,1728]{1,0:T(8,128)(2,1)S(1)} %copy.15.weight_ref), custom_call_target="tpu_custom_call" | custom-call | flops 905969664 | bytes 704512 | tf_op jit(solution)/shard_map/own4/pallas_call | solution.py:18
  8.6 1.5 %layer4.1 = (bf16[128,256]{1,0:T(8,128)(2,1)S(1)}, f32[2,128,1024]{2,1,0:T(8,128)S(1)}, bf16[2304,1024]{1,0:T(8,128)(2,1)S(1)}) custom-call(bf16[2,64,512]{2,1,0:T(8,128)(2,1)S(1)} %collective-permute-done.first_ref, bf16[2,64,512]{2,1,0:T(8,128)(2,1)S(1)} %collective-permute-done.1.second_ref, ...), custom_call_target="tpu_custom_call", output_to_operand_aliasing={{1}: (3, {}), {2}: (4, {})} | custom-call | flops 452984832 | bytes 6471680 | tf_op jit(solution)/shard_map/layer4/pallas_call | solution.py:18
  10.1 1.3 %collective-permute-start.3 = (bf16[128,256]{1,0:T(8,128)(2,1)S(1)}, bf16[128,256]{1,0:T(8,128)(2,1)S(1)}, u32[]{:S(2)}, u32[]{:S(2)}) collective-permute-start(bf16[128,256]{1,0:T(8,128)(2,1)S(1)} %get-tuple-element.31.pooled_ref), channel_id=1, source_target_pairs={{0,32},{1,2},{2,1},{3,4},{4,3},{5,6},{6,5},{7,8},{8,7},{9,10},{10,... | collective-permute-start | bytes 196616 | tf_op jit(solution)/shard_map/ppermute | solution.py:45
  11.4 2.2 %collective-permute-start.2 = (bf16[128,256]{1,0:T(8,128)(2,1)S(1)}, bf16[128,256]{1,0:T(8,128)(2,1)S(1)}, u32[]{:S(2)}, u32[]{:S(2)}) collective-permute-start(bf16[128,256]{1,0:T(8,128)(2,1)S(1)} %get-tuple-element.31.pooled_ref), channel_id=1, source_target_pairs={{0,1},{1,0},{2,3},{3,2},{4,5},{5,4},{6,7},{7,6},{8,9},{9,8},{10,11... | collective-permute-start | bytes 196616 | tf_op jit(solution)/shard_map/ppermute | solution.py:45
  13.6 1.0 %own5.1 = (f32[256,256]{1,0:T(8,128)S(1)}, bf16[9,384,256]{2,1,0:T(8,128)(2,1)S(1)}, f32[2,128,1024]{2,1,0:T(8,128)S(1)}) custom-call(bf16[128,256]{1,0:T(8,128)(2,1)S(1)} %get-tuple-element.31.pooled_ref, bf16[27,256,128]{2,1,0:T(8,128)(2,1)S(1)} %copy-done, f32[2,128,1024]{2,1,0:T(8,128)S(1)} %get-tuple-element.32.preact4_ref), custom_call_target="tpu_custom_call", output_to_operand_aliasing={{2}: (2, {})} | custom-call | flops 150994944 | bytes 2883584 | tf_op jit(solution)/shard_map/own5/pallas_call | solution.py:18
  14.5 0.7 collective-permute-done.2.first_ref
  15.2 1.7 %layer5.1 = (bf16[2,256,128]{2,1,0:T(8,128)(2,1)S(1)}, bf16[128,256]{1,0:T(8,128)(2,1)S(1)}, bf16[128,256]{1,0:T(8,128)(2,1)S(1)}, bf16[448,256]{1,0:T(8,128)(2,1)S(1)}, bf16[448,256]{1,0:T(8,128)(2,1)S(1)}) custom-call(bf16[128,256]{1,0:T(8,128)(2,1)S(1)} %get-tuple-element.31.pooled_ref, bf16[128,256]{1,0:T(8,128)(2,1)S(1)} %collective-permute-done.2.first_ref, ...), custom_call_target="tpu_custom_call" | custom-call | flops 679477248 | bytes 4128768 | tf_op jit(solution)/shard_map/layer5/pallas_call | solution.py:18
  17.0 1.8 %collective-permute-start.4 = (bf16[128,256]{1,0:T(8,128)(2,1)S(1)}, bf16[128,256]{1,0:T(8,128)(2,1)S(1)}, u32[]{:S(2)}, u32[]{:S(2)}) collective-permute-start(bf16[128,256]{1,0:T(8,128)(2,1)S(1)} %get-tuple-element.39), channel_id=1, source_target_pairs={{0,1},{1,0},{2,3},{3,2},{4,5},{5,4},{6,7},{7,6},{8,9},{9,8},{10,11... | collective-permute-start | bytes 196616 | tf_op jit(solution)/shard_map/ppermute | solution.py:45
  18.8 2.7 %collective-permute-start.5 = (bf16[128,256]{1,0:T(8,128)(2,1)S(1)}, bf16[128,256]{1,0:T(8,128)(2,1)S(1)}, u32[]{:S(2)}, u32[]{:S(2)}) collective-permute-start(bf16[128,256]{1,0:T(8,128)(2,1)S(1)} %get-tuple-element.40), channel_id=1, source_target_pairs={{0,32},{1,2},{2,1},{3,4},{4,3},{5,6},{6,5},{7,8},{8,7},{9,10},{10,... | collective-permute-start | bytes 196616 | tf_op jit(solution)/shard_map/ppermute | solution.py:45
  21.8 1.2 %own_parts.1 = (f32[128,256]{1,0:T(8,128)S(1)}, f32[1728,128]{1,0:T(8,128)S(1)}, bf16[2,256,128]{2,1,0:T(8,128)(2,1)}) custom-call(bf16[448,256]{1,0:T(8,128)(2,1)S(1)} %get-tuple-element.35.mine_ref, bf16[9,384,256]{2,1,0:T(8,128)(2,1)S(1)} %get-tuple-element.34.back_ref, bf16[2,256,128]{2,1,0:T(8,128)(2,1)S(1)} %get-tuple-element.36.made_ref), custom_call_target="tpu_custom_call" | custom-call | flops 377487360 | bytes 1769472 | tf_op jit(solution)/shard_map/own_parts/pallas_call | solution.py:338
  23.1 5.6 %collective-permute-done.6.got_ref.chip_ref = bf16[448,256]{1,0:T(8,128)(2,1)S(1)} collective-permute-done((bf16[448,256]{1,0:T(8,128)(2,1)S(1)}, bf16[448,256]{1,0:T(8,128)(2,1)S(1)}, u32[]{:S(2)}, u32[]{:S(2)}) %collective-permute-start.6) | collective-permute-done | bytes 229408 | tf_op jit(solution)/shard_map/ppermute | solution.py:55
  28.7 0.9 %collective-permute-start.8 = (bf16[640,256]{1,0:T(8,128)(2,1)S(1)}, bf16[640,256]{1,0:T(8,128)(2,1)S(1)}, u32[]{:S(2)}, u32[]{:S(2)}) collective-permute-start(bf16[640,256]{1,0:T(8,128)(2,1)S(1)} %regroup.1), channel_id=1, source_target_pairs={{0,32},{32,0},{64,96},{96,64},{1,33},{33,1},{65,97},{97,65},{2,34}... | collective-permute-start | bytes 983048 | tf_op jit(solution)/shard_map/ppermute | solution.py:50
  29.6 1.7 %weight4_parts.1 = (f32[54,16,128]{2,1,0:T(8,128)S(1)}, bf16[54,16,128]{2,1,0:T(8,128)(2,1)S(1)}) custom-call(bf16[128,256]{1,0:T(8,128)(2,1)S(1)} %halo_sum.1.inward_ref, bf16[2304,1024]{1,0:T(8,128)(2,1)S(1)} %get-tuple-element.43.stack_ref, f32[2,128,1024]{2,1,0:T(8,128)S(1)} %get-tuple-element.44.slope_ref), custom_call_target="tpu_custom_call" | custom-call | flops 905969664 | bytes 5832704 | tf_op jit(solution)/shard_map/weight4_parts/pallas_call | solution.py:18
  31.4 1.1 %weight5.1._ = bf16[64,48,128]{2,1,0:T(8,128)(2,1)S(1)} custom-call(bf16[448,256]{1,0:T(8,128)(2,1)S(1)} %collective-permute-done.6.got_ref.chip_ref, bf16[640,256]{1,0:T(8,128)(2,1)S(1)} %collective-permute-done.8.core_ref, f32[1728,128]{1,0:T(8,128)S(1)} %get-tuple-element.48.first_ref), custom_call_target="tpu_custom_call" | custom-call | flops 226492416 | bytes 1441792 | tf_op jit(solution)/shard_map/weight5/pallas_call | solution.py:18
  32.9 29.3 %all_to_all.10.parts_ref = bf16[64,48,128]{2,1,0:T(8,128)(2,1)S(1)} all-to-all(bf16[64,48,128]{2,1,0:T(8,128)(2,1)S(1)} %pairs.1), channel_id=1, replica_groups={{0,1,2,3,4,5,6,7,8,9,10,11,12,13,14,15,16,17,18,19,20,21,22,23,24,25,26..., dimensions={0} | all-to-all | bytes 1572864 | tf_op jit(solution)/shard_map/all_to_all | solution.py:561
  62.5 15.6 %all_to_all.11 = bf16[64,24,128]{2,1,0:T(8,128)(2,1)S(1)} all-to-all(bf16[64,24,128]{2,1,0:T(8,128)(2,1)S(1)} %pad_maximum_fusion), channel_id=1, replica_groups={{0,1,2,3,4,5,6,7,8,9,10,11,12,13,14,15,16,17,18,19,20,21,22,23,24,25,26..., dimensions={0} | all-to-all | bytes 786432 | tf_op jit(solution)/shard_map/all_to_all | solution.py:561
  78.1 2.9 %collective-permute-start.9 = (bf16[64,24,128]{2,1,0:T(8,128)(2,1)S(1)}, bf16[64,24,128]{2,1,0:T(8,128)(2,1)S(1)}, u32[]{:S(2)}, u32[]{:S(2)}) collective-permute-start(bf16[64,24,128]{2,1,0:T(8,128)(2,1)S(1)} %all_to_all.11), channel_id=1, source_target_pairs={{0,32},{32,0},{64,96},{96,64},{1,33},{33,1},{65,97},{97,65},{2,34}... | collective-permute-start | bytes 1179656 | tf_op jit(solution)/shard_map/ppermute | solution.py:50
  81.1 1.0 %first_half.1 = (f32[27,64,128]{2,1,0:T(8,128)}, f32[27,4,256]{2,1,0:T(4,128)}) custom-call(bf16[64,16,128]{2,1,0:T(8,128)(2,1)S(1)} %slice.18.rows4_ref, f32[64,8,128]{2,1,0:T(8,128)S(1)} %slice_convert_fusion.rows5_ref), custom_call_target="tpu_custom_call" | custom-call | tf_op jit(solution)/shard_map/first_half/pallas_call | solution.py:517
  82.4 1.0 %second_half.1 = (f32[27,64,128]{2,1,0:T(8,128)}, f32[27,4,256]{2,1,0:T(4,128)}) custom-call(bf16[64,16,128]{2,1,0:T(8,128)(2,1)S(1)} %slice.16.rows4_ref, f32[64,8,128]{2,1,0:T(8,128)S(1)} %slice_convert_fusion.1.rows5_ref, f32[27,64,128]{2,1,0:T(8,128)} %get-tuple-element.51._, ...), custom_call_target="tpu_custom_call", output_to_operand_aliasing={{0}: (2, {}), {1}: (3, {})} | custom-call | tf_op jit(solution)/shard_map/second_half/pallas_call | solution.py:517
  (27 shorter events, 1.5 us)
Async XLA Ops:
  1.6 7.0 %collective-permute-start.1 = (bf16[2,64,512]{2,1,0:T(8,128)(2,1)S(1)}, bf16[2,64,512]{2,1,0:T(8,128)(2,1)S(1)}, u32[]{:S(2)}, u32[]{:S(2)}) collective-permute-start(bf16[2,64,512]{2,1,0:T(8,128)(2,1)S(1)} %get-tuple-element.55), channel_id=1, source_target_pairs={{0,32},{1,2},{2,1},{3,4},{4,3},{5,6},{6,5},{7,8},{8,7},{9,10},{10,... | collective-permute-start | bytes 393224 | tf_op jit(solution)/shard_map/ppermute | solution.py:45
  3.1 5.5 %collective-permute-start = (bf16[2,64,512]{2,1,0:T(8,128)(2,1)S(1)}, bf16[2,64,512]{2,1,0:T(8,128)(2,1)S(1)}, u32[]{:S(2)}, u32[]{:S(2)}) collective-permute-start(bf16[2,64,512]{2,1,0:T(8,128)(2,1)S(1)} %get-tuple-element.56), channel_id=1, source_target_pairs={{0,1},{1,0},{2,3},{3,2},{4,5},{5,4},{6,7},{7,6},{8,9},{9,8},{10,11... | collective-permute-start | bytes 393224 | tf_op jit(solution)/shard_map/ppermute | solution.py:45
  6.4 1.0 %copy-start.1 = (bf16[2,2,64,512]{3,2,1,0:T(8,128)(2,1)S(1)}, bf16[2,2,64,512]{3,2,1,0:T(8,128)(2,1)}, u32[]{:S(2)}) copy-start(bf16[2,2,64,512]{3,2,1,0:T(8,128)(2,1)} %vol_ref.1) | copy-start | bytes 786436
  7.3 6.3 %copy-start = (bf16[27,256,128]{2,1,0:T(8,128)(2,1)S(1)}, bf16[27,256,128]{2,1,0:T(8,128)(2,1)}, u32[]{:S(2)}) copy-start(bf16[27,256,128]{2,1,0:T(8,128)(2,1)} %weight_ref.3) | copy-start | bytes 5308420
  8.6 6.6 %copy-start.2 = (bf16[1,2,256,128]{3,2,1,0:T(8,128)(2,1)S(1)}, bf16[1,2,256,128]{3,2,1,0:T(8,128)(2,1)}, u32[]{:S(2)}) copy-start(bf16[1,2,256,128]{3,2,1,0:T(8,128)(2,1)} %param.5) | copy-start | bytes 393220
  10.1 4.4 %collective-permute-start.3 = (bf16[128,256]{1,0:T(8,128)(2,1)S(1)}, bf16[128,256]{1,0:T(8,128)(2,1)S(1)}, u32[]{:S(2)}, u32[]{:S(2)}) collective-permute-start(bf16[128,256]{1,0:T(8,128)(2,1)S(1)} %get-tuple-element.31.pooled_ref), channel_id=1, source_target_pairs={{0,32},{1,2},{2,1},{3,4},{4,3},{5,6},{6,5},{7,8},{8,7},{9,10},{10,... | collective-permute-start | bytes 196616 | tf_op jit(solution)/shard_map/ppermute | solution.py:45
  11.4 3.8 %collective-permute-start.2 = (bf16[128,256]{1,0:T(8,128)(2,1)S(1)}, bf16[128,256]{1,0:T(8,128)(2,1)S(1)}, u32[]{:S(2)}, u32[]{:S(2)}) collective-permute-start(bf16[128,256]{1,0:T(8,128)(2,1)S(1)} %get-tuple-element.31.pooled_ref), channel_id=1, source_target_pairs={{0,1},{1,0},{2,3},{3,2},{4,5},{5,4},{6,7},{7,6},{8,9},{9,8},{10,11... | collective-permute-start | bytes 196616 | tf_op jit(solution)/shard_map/ppermute | solution.py:45
  17.0 6.0 %collective-permute-start.4 = (bf16[128,256]{1,0:T(8,128)(2,1)S(1)}, bf16[128,256]{1,0:T(8,128)(2,1)S(1)}, u32[]{:S(2)}, u32[]{:S(2)}) collective-permute-start(bf16[128,256]{1,0:T(8,128)(2,1)S(1)} %get-tuple-element.39), channel_id=1, source_target_pairs={{0,1},{1,0},{2,3},{3,2},{4,5},{5,4},{6,7},{7,6},{8,9},{9,8},{10,11... | collective-permute-start | bytes 196616 | tf_op jit(solution)/shard_map/ppermute | solution.py:45
  18.8 4.2 %collective-permute-start.5 = (bf16[128,256]{1,0:T(8,128)(2,1)S(1)}, bf16[128,256]{1,0:T(8,128)(2,1)S(1)}, u32[]{:S(2)}, u32[]{:S(2)}) collective-permute-start(bf16[128,256]{1,0:T(8,128)(2,1)S(1)} %get-tuple-element.40), channel_id=1, source_target_pairs={{0,32},{1,2},{2,1},{3,4},{4,3},{5,6},{6,5},{7,8},{8,7},{9,10},{10,... | collective-permute-start | bytes 196616 | tf_op jit(solution)/shard_map/ppermute | solution.py:45
  21.5 7.2 %collective-permute-start.6 = (bf16[448,256]{1,0:T(8,128)(2,1)S(1)}, bf16[448,256]{1,0:T(8,128)(2,1)S(1)}, u32[]{:S(2)}, u32[]{:S(2)}) collective-permute-start(bf16[448,256]{1,0:T(8,128)(2,1)S(1)} %get-tuple-element.41), channel_id=1, source_target_pairs={{0,64},{32,96},{64,0},{96,32},{1,65},{33,97},{65,1},{97,33},{2,66}... | collective-permute-start | bytes 688136 | tf_op jit(solution)/shard_map/ppermute | solution.py:55
  28.7 2.6 %collective-permute-start.8 = (bf16[640,256]{1,0:T(8,128)(2,1)S(1)}, bf16[640,256]{1,0:T(8,128)(2,1)S(1)}, u32[]{:S(2)}, u32[]{:S(2)}) collective-permute-start(bf16[640,256]{1,0:T(8,128)(2,1)S(1)} %regroup.1), channel_id=1, source_target_pairs={{0,32},{32,0},{64,96},{96,64},{1,33},{33,1},{65,97},{97,65},{2,34}... | collective-permute-start | bytes 983048 | tf_op jit(solution)/shard_map/ppermute | solution.py:50
  31.3 1.6 %collective-permute-start.7 = (bf16[54,16,128]{2,1,0:T(8,128)(2,1)S(1)}, bf16[54,16,128]{2,1,0:T(8,128)(2,1)S(1)}, u32[]{:S(2)}, u32[]{:S(2)}) collective-permute-start(bf16[54,16,128]{2,1,0:T(8,128)(2,1)S(1)} %get-tuple-element.46), channel_id=1, source_target_pairs={{0,32},{32,0},{64,96},{96,64},{1,33},{33,1},{65,97},{97,65},{2,34}... | collective-permute-start | bytes 663560 | tf_op jit(solution)/shard_map/ppermute | solution.py:50
  78.1 4.3 %collective-permute-start.9 = (bf16[64,24,128]{2,1,0:T(8,128)(2,1)S(1)}, bf16[64,24,128]{2,1,0:T(8,128)(2,1)S(1)}, u32[]{:S(2)}, u32[]{:S(2)}) collective-permute-start(bf16[64,24,128]{2,1,0:T(8,128)(2,1)S(1)} %all_to_all.11), channel_id=1, source_target_pairs={{0,32},{32,0},{64,96},{96,64},{1,33},{33,1},{65,97},{97,65},{2,34}... | collective-permute-start | bytes 1179656 | tf_op jit(solution)/shard_map/ppermute | solution.py:50
